TPU v7x, 256 devices: a whole 4x4x8 slice. The times are simulated.
256 devices in a mesh: path: 32 (over z_hi, y, core), fsdp: 8 (over z_lo, x).
Axes of the slice: x: 4, y: 4, z: 8 (z_hi: 4, z_lo: 2; z = z_hi * 2 + z_lo), core: 2. Of those that a mesh axis runs over, the one named last changes fastest.
Arguments:
- inputs: bfloat16 [32, 6144, 2048], P('path', 'fsdp'), may hold values from -6 to 6
- targets: bfloat16 [32, 6144, 2048], P('path', 'fsdp'), may hold values from -6 to 6
- token_ids: int32 [32, 6144], P('path', 'fsdp'), may hold values from 0 to 31999, as said below
- path_weights: bfloat16 [32, 2048, 2048], P('path', 'fsdp'), may hold values from -6 to 6
- stale_deltas: bfloat16 [32, 2048, 2048], P('path', 'fsdp'), may hold values from -6 to 6
- module_params: float32 [4, 2048, 2048], P(None, 'fsdp', 'path'), may hold values from -6 to 6
- momentum: float32 [4, 2048, 2048], P(None, 'fsdp', 'path'), may hold values from -3 to 3
- module_of_path: int32 [32], replicated, may hold values from 0 to 3, as said below
- sharing_counts: int32 [4], replicated, may hold values from 1 to 16, as said below
Outputs:
- next_weights: bfloat16 [32, 2048, 2048], P('path', 'fsdp')
- new_params: float32 [4, 2048, 2048], P(None, 'fsdp', 'path')
- new_momentum: float32 [4, 2048, 2048], P(None, 'fsdp', 'path')
Inputs may be any that keep to these rules, and one draw needn't show every extreme that they name: `module_of_path`: every module is used by at least one path; one module is used by exactly 16 paths, every other by fewer. sharing_counts[m] is the number of paths p with module_of_path[p] = m. `token_ids`: each path's tokens with id 0 form a suffix that leaves at least a quarter of its 6144 tokens real.
All inputs are finite; a program needn't handle non-finite values.
Results may differ from a plain program's by a relative error of at most 0.015.
Values may be sent and summed in bfloat16 or wider, within the bound.
No kernel may reach another device: no remote copies, remote signals or barrier semaphores. Data moves between devices by JAX's collectives and lax.ppermute only.
A program may use at most 128 MiB of HBM per device.

v0:
```python
import math

import jax
import jax.numpy as jnp
from jax import lax
from jax.sharding import PartitionSpec as P


def per_device(
    inputs,
    targets,
    token_ids,
    path_weights,
    stale_deltas,
    module_params,
    momentum,
    module_of_path,
    sharing_counts,
):
    block_in = inputs[0]
    width_in = block_in.shape[-1]
    values = block_in.astype(jnp.float32)
    scale = lax.rsqrt(jnp.mean(values * values, axis=-1, keepdims=True) + 1e-06)
    normed = (values * scale).astype(jnp.bfloat16)
    mask = (token_ids[0] != 0).astype(jnp.float32)
    count = lax.psum(jnp.sum(mask), "fsdp")
    weights = path_weights[0]
    columns = normed
    projected = jnp.dot(
        columns,
        lax.all_gather(weights, "fsdp", axis=0, tiled=True),
        preferred_element_type=jnp.float32,
    ) / math.sqrt(width_in)
    residual_rows = ((projected - targets[0].astype(jnp.float32)) * mask[:, None]).astype(
        jnp.bfloat16
    )
    columns = normed
    grad = lax.psum_scatter(
        jnp.einsum("ti,tj->ij", columns, residual_rows, preferred_element_type=jnp.float32).astype(
            jnp.bfloat16
        ),
        "fsdp",
        scatter_dimension=0,
        tiled=True,
    ).astype(jnp.float32) / jnp.sqrt(count)
    inner = weights.astype(jnp.float32) - 0.25 * grad
    modules = sharing_counts.shape[0]
    labels = jnp.arange(modules, dtype=jnp.int32)
    mine = module_of_path[lax.axis_index("path")]
    mine_hot = (labels == mine).astype(jnp.float32)
    delta = stale_deltas[0]
    placed = mine_hot[:, None, None] * delta.astype(jnp.float32)[None]
    total = lax.psum_scatter(
        placed.astype(jnp.bfloat16), "path", scatter_dimension=2, tiled=True
    ).astype(jnp.float32)
    outer_grad = total / sharing_counts.astype(jnp.float32)[:, None, None]
    new_momentum = 0.9 * momentum + outer_grad
    outer_step = 0.7 * (outer_grad + 0.9 * new_momentum)
    new_params = module_params - outer_step
    outer_step_b = outer_step.astype(jnp.bfloat16)
    every_step = lax.all_gather(outer_step_b, "path", axis=2, tiled=True)
    correction = jnp.einsum(
        "m,mrc->rc", mine_hot.astype(jnp.bfloat16), every_step, preferred_element_type=jnp.float32
    )
    next_weights = (inner - correction).astype(jnp.bfloat16)[None]
    return (next_weights, new_params, new_momentum)


def solution(mesh):
    return jax.shard_map(
        per_device,
        mesh=mesh,
        in_specs=(
            P("path", "fsdp", None),
            P("path", "fsdp", None),
            P("path", "fsdp"),
            P("path", "fsdp", None),
            P("path", "fsdp", None),
            P(None, "fsdp", "path"),
            P(None, "fsdp", "path"),
            P(),
            P(),
        ),
        out_specs=(P("path", "fsdp", None), P(None, "fsdp", "path"), P(None, "fsdp", "path")),
        check_vma=False,
    )
```

profile of v0, /device:TPU:24, one launch (start us, length us, event | category | flops | bytes accessed | tf_op | source)
XLA Modules:
  0.0 319.8 jit_solution(2063434279221096219)
XLA Ops:
  8.0 0.0 reduce-scatter.5.cloned.1.call-start
  8.0 1.3 dynamic_slice.3
  9.4 0.6 compare_convert_fusion.1
  10.0 2.8 bitcast_convert_fusion
  12.8 1.9 copy.12
  14.7 3.1 multiply_convert_fusion
  17.9 0.0 copy-start.4
  17.9 0.0 copy-start.3
  17.9 0.0 copy-start.1
  17.9 0.0 reduce-scatter.5.cloned.1.call-update
  17.9 0.0 all-gather.6.cloned.1.call-start
  17.9 0.5 all-gather.6.cloned.1.call-update
  18.5 0.0 all-gather.4.cloned.1.call-start
  18.5 0.0 copy-done.4
  18.5 131.9 %reduce-scatter.5.cloned.1.call-done = bf16[4,256,64]{1,2,0:T(8,128)(2,1)} async-done(((bf16[4,256,2048]{1,2,0:T(8,128)(2,1)}), bf16[4,256,64]{1,2,0:T(8,128)(2,1)}) %reduce-scatter.5.cloned.1.call-update) | async-done | bytes 131088 | tf_op jit(solution)/shard_map/reduce_scatter | solution.py:53
  150.4 1.9 fusion.16
  152.3 0.0 copy-start.2
  152.3 1.8 fusion.17
  154.1 0.0 all-gather.4.cloned.1.call-update
  154.1 0.0 reduce-scatter.3.cloned.1.call-start
  154.2 0.0 copy-done.3
  154.2 0.7 fusion.14
  154.9 0.0 copy-done.1
  154.9 0.7 fusion.2
  155.6 0.0 all-gather.6.cloned.1.call-done
  155.6 9.7 %fusion.5 = bf16[768,2048]{1,0:T(8,128)(2,1)S(1)} fusion(bf16[1,2048,2048]{2,1,0:T(8,128)(2,1)} %all-gather.6.cloned.1.call-done, bf16[1,768,2048]{2,1,0:T(8,128)(2,1)} %param.10, f32[768]{0:T(1024)S(1)} %get-tuple-element.3, bf16[1,768,2048]{2,1,0:T(8,128)(2,1)S(1)} %copy-done.1, f32[768]{0:T(1024)S(1)} %add_rsqrt_fusion), kind=kOutput, calls=%fused_computation.10 | convolution fusion | flops 6455033856 | bytes 17831936 | tf_op jit(solution)/shard_map/dot_general | solution.py:29
  165.3 0.0 copy-done.2
  165.4 9.4 %convolution_convert_fusion = bf16[2048,2048]{1,0:T(8,128)(2,1)} fusion(bf16[768,2048]{1,0:T(8,128)(2,1)S(1)} %fusion.5, bf16[1,768,2048]{2,1,0:T(8,128)(2,1)S(1)} %copy-done.1, f32[768]{0:T(1024)S(1)} %add_rsqrt_fusion), kind=kOutput, calls=%fused_computation.5 | convolution fusion | flops 6451363840 | bytes 14683136 | tf_op jit(solution)/shard_map/ti,tj->ij/dot_general | solution.py:39
  174.7 0.0 reduce-scatter.3.cloned.1.call-update
  174.7 19.5 %psum.7 = f32[]{:T(128)} all-reduce(f32[]{:T(128)} %get-tuple-element.4), channel_id=1, replica_groups=mesh['path'=32,'fsdp'=8] {'fsdp'}, use_global_device_ids=true, to_apply=%region_3.0 | all-reduce | flops 1 | bytes 8 | tf_op jit(solution)/shard_map/psum | solution.py:26
  195.0 18.1 %all-gather.4.cloned.1.call-done = bf16[4,256,2048]{1,2,0:T(8,128)(2,1)} async-done(((bf16[4,256,64]{1,2,0:T(8,128)(2,1)}), bf16[4,256,2048]{1,2,0:T(8,128)(2,1)}) %all-gather.4.cloned.1.call-update) | async-done | bytes 4194320 | tf_op jit(solution)/shard_map/all_gather | solution.py:61
  213.1 7.9 %copy.13 = bf16[4,256,2048]{2,0,1:T(4,128)(2,1)} copy(bf16[4,256,2048]{1,2,0:T(8,128)(2,1)} %all-gather.4.cloned.1.call-done) | data formatting | bytes 8388608 | tf_op jit(solution)/shard_map/all_gather | solution.py:61
  221.0 0.0 copy-start
  221.0 5.2 %fusion.15 = f32[1,256,2048]{2,0,1:T(1,128)S(1)} fusion(bf16[4,256,2048]{2,0,1:T(4,128)(2,1)} %copy.13, s32[]{:T(128)} %bitcast.5), kind=kOutput, calls=%fused_computation.25 | convolution fusion | flops 4194316 | bytes 6291460 | tf_op jit(solution)/shard_map/m,mrc->rc/dot_general | solution.py:62
  226.3 82.6 %reduce-scatter.3.cloned.1.call-done = bf16[256,2048]{1,0:T(8,128)(2,1)} async-done(((bf16[2048,2048]{1,0:T(8,128)(2,1)}), bf16[256,2048]{1,0:T(8,128)(2,1)}) %reduce-scatter.3.cloned.1.call-update) | async-done | bytes 1048592 | tf_op jit(solution)/shard_map/reduce_scatter | solution.py:38
  308.9 0.0 copy-done
  308.9 3.3 %fusion.12 = bf16[1,256,2048]{2,1,0:T(8,128)(2,1)} fusion(f32[1,256,2048]{2,0,1:T(1,128)S(1)} %fusion.15, f32[]{:T(128)S(6)} %sqrt.3, bf16[256,2048]{1,0:T(8,128)(2,1)} %reduce-scatter.3.cloned.1.call-done, bf16[1,256,2048]{2,1,0:T(8,128)(2,1)S(1)} %copy-done), kind=kLoop, calls=%fused_computation.15 | loop fusion | flops 3670016 | bytes 5242884 | tf_op jit(solution)/shard_map/broadcast_in_dim | solution.py:65
  (2 shorter events, 0.0 us)
Async XLA Ops:
  8.0 142.4 %reduce-scatter.5.cloned.1.call-start = ((), (), s32[]{:S(2)}) async-start(), calls=%async_computation.3 | async-start | bytes 4325376 | tf_op jit(solution)/shard_map/reduce_scatter | solution.py:53
  17.9 0.7 copy-start.4
  17.9 136.3 %copy-start.3 = (s32[1,768]{1,0:T(1,128)S(1)}, s32[1,768]{1,0:T(1,128)}, u32[]{:S(2)}) copy-start(s32[1,768]{1,0:T(1,128)} %param.11) | copy-start | bytes 9220
  17.9 137.0 %copy-start.1 = (bf16[1,768,2048]{2,1,0:T(8,128)(2,1)S(1)}, bf16[1,768,2048]{2,1,0:T(8,128)(2,1)}, u32[]{:S(2)}) copy-start(bf16[1,768,2048]{2,1,0:T(8,128)(2,1)} %param.9) | copy-start | bytes 9437188
  17.9 137.7 %all-gather.6.cloned.1.call-start = ((), (), s32[]{:S(2)}) async-start(), calls=%async_computation.5 | async-start | bytes 9437184 | tf_op jit(solution)/shard_map/all_gather | solution.py:31
  18.5 194.6 %all-gather.4.cloned.1.call-start = ((), (), s32[]{:S(2)}) async-start(), calls=%async_computation.4 | async-start | bytes 4325376 | tf_op jit(solution)/shard_map/all_gather | solution.py:61
  152.3 13.0 %copy-start.2 = (f32[4,256,64]{1,2,0:T(8,128)}, f32[4,256,64]{1,2,0:T(8,128)S(1)}, u32[]{:S(2)}) copy-start(f32[4,256,64]{1,2,0:T(8,128)S(1)} %get-tuple-element.6) | copy-start | bytes 786436
  154.1 154.7 %reduce-scatter.3.cloned.1.call-start = ((), (), s32[]{:S(2)}) async-start(), calls=%async_computation.2 | async-start | bytes 9437184 | tf_op jit(solution)/shard_map/reduce_scatter | solution.py:38
  221.0 87.8 %copy-start = (bf16[1,256,2048]{2,1,0:T(8,128)(2,1)S(1)}, bf16[1,256,2048]{2,1,0:T(8,128)(2,1)}, u32[]{:S(2)}) copy-start(bf16[1,256,2048]{2,1,0:T(8,128)(2,1)} %param.12) | copy-start | bytes 3145732
Sparse Core Ops, SparseCore 0:
  18.0 132.3 reduce-scatter.4
Sparse Core Ops, SparseCore 1:
  20.1 114.0 all-gather.5
  154.2 58.8 all-gather.3
  215.7 93.1 reduce-scatter.2
where the time goes:
time: 321 us; the launch traced here: 320 us
  waiting for transfers between devices  233 us (73%)
  matrix products  24.3 us (8%)
  blocking collectives  19.5 us (6%)
  between operations  16.5 us (5%)
  other arithmetic  15 us (5%)
  local copies, waits for them, and re-layouts  11.2 us (3%)
    reduce_scatter x1, waiting for transfers between devices, per_device(): lax.psum_scatter(placed.astype(jnp.bfloat16), 'path', scatter_dimension=2...  132 us
    reduce_scatter x1, waiting for transfers between devices, per_device(): lax.psum_scatter(jnp.einsum('ti,tj->ij', columns, residual_rows, preferre...  82.6 us
    psum x1, blocking collectives, per_device(): count = lax.psum(jnp.sum(mask), 'fsdp')  19.5 us
    all_gather x1, waiting for transfers between devices, per_device(): every_step = lax.all_gather(outer_step_b, 'path', axis=2, tiled=True)  18.1 us
    dot_general x1, matrix products, per_device(): jnp.dot(columns, lax.all_gather(weights, 'fsdp', axis=0, tiled=True), pre...  9.73 us
    dot_general x1, matrix products, per_device(): jnp.einsum('ti,tj->ij', columns, residual_rows, preferred_element_type=jn...  9.35 us
    all_gather x1, local copies, waits for them, and re-layouts, per_device(): every_step = lax.all_gather(outer_step_b, 'path', axis=2, tiled=True)  7.94 us
  transfers between devices with their start and end apart: 4, of which 3 were waited for; matrix products, arithmetic and copies ran while one was open for 12% of the time, Pallas kernels for 0%

commit v1 on v0

v1 whole, which is shorter than its diff:
```python
import functools
import math

import jax
import jax.numpy as jnp
from jax import lax
from jax.experimental import pallas as pl
from jax.experimental.pallas import tpu as pltpu
from jax.sharding import PartitionSpec as P

Z_HI, Y, CORES, Z_LO, X = 4, 4, 2, 2, 4
HALF = 64
TILE = 512
BASE = 32.0
EXTRA = 16
VMEM_LIMIT = 48 * 1024 * 1024
SMALL_LIMIT = 16 * 1024 * 1024


def ring(step):
    return [(z * X + x, z * X + (x + step) % X) for z in range(Z_LO) for x in range(X)]


def pair():
    return [(z * X + x, (1 - z) * X + x) for z in range(Z_LO) for x in range(X)]


def along_y(step):
    return [
        ((z * Y + y) * CORES + c, (z * Y + (y + step) % Y) * CORES + c)
        for z in range(Z_HI)
        for y in range(Y)
        for c in range(CORES)
    ]


def cores():
    return [(p, p ^ 1) for p in range(Z_HI * Y * CORES)]


def owner(place, k):
    own_z, own_x = place // X, place % X
    return ((own_z + k // X) % Z_LO) * X + (own_x + k % X) % X


def norm_kernel(place_ref, x_ref, n_ref):
    values = x_ref[...].astype(jnp.float32)
    scale = lax.rsqrt(jnp.mean(values * values, axis=-1, keepdims=True) + 1e-06)
    width = x_ref.shape[1] // (Z_LO * X)
    for k in range(Z_LO * X):
        start = pl.multiple_of(owner(place_ref[1], k) * width, width)
        block = x_ref[:, pl.ds(start, width)].astype(jnp.float32) * scale
        n_ref[:, k * width : (k + 1) * width] = block.astype(jnp.bfloat16)


def norm(place, x):
    rows, width = x.shape
    step = 128
    block = pl.BlockSpec((step, width), lambda i, s: (i, 0))
    return pl.pallas_call(
        norm_kernel,
        grid_spec=pltpu.PrefetchScalarGridSpec(
            num_scalar_prefetch=1, grid=(rows // step,), in_specs=[block], out_specs=block
        ),
        out_shape=jax.ShapeDtypeStruct((rows, width), jnp.bfloat16),
        compiler_params=pltpu.CompilerParams(vmem_limit_bytes=SMALL_LIMIT),
        cost_estimate=pl.CostEstimate(flops=3 * rows * width, bytes_accessed=4 * rows * width, transcendentals=rows),
        name="norm",
    )(place, x)


def grad_kernel(n_ref, target_ref, mask_ref, *rest):
    pieces, outs, w_ref = rest[:8], rest[-9:-1], rest[-1]
    depth = pieces[0].shape[0]
    for k, piece in enumerate(pieces):
        w_ref[k * depth : (k + 1) * depth, :] = piece[...]
    projected = jnp.dot(n_ref[...], w_ref[...], preferred_element_type=jnp.float32)
    projected = projected * (1.0 / math.sqrt(n_ref.shape[1]))
    rows = ((projected - target_ref[...].astype(jnp.float32)) * mask_ref[...]).astype(jnp.bfloat16)
    for k, out in enumerate(outs):
        out[:depth, :] = lax.dot_general(
            n_ref[:, k * depth : (k + 1) * depth],
            rows,
            (((0,), (0,)), ((), ())),
            preferred_element_type=jnp.float32,
        ).astype(jnp.bfloat16)
    more = outs[0].shape[0] - depth
    if more:
        count = jnp.sum(mask_ref[...])
        high = jnp.floor(count * (1.0 / BASE))
        low = count - BASE * high
        upper = lax.broadcasted_iota(jnp.int32, (more, TILE), 0) < more // 2
        for out in outs:
            out[depth:, :] = jnp.where(upper, high, low).astype(jnp.bfloat16)


def grads(normed, targets, mask, weights, pieces, chunk, width, more, deps=()):
    rows, features = normed.shape
    depth = weights.shape[0]
    steps = width // TILE
    base = chunk * steps
    piece = pl.BlockSpec((depth, TILE), lambda j: (0, j))
    out = pl.BlockSpec((depth + more, TILE), lambda j: (0, j))
    return pl.pallas_call(
        grad_kernel,
        grid=(steps,),
        in_specs=[
            pl.BlockSpec((rows, features), lambda j: (0, 0), pipeline_mode=pl.Buffered(1)),
            pl.BlockSpec((rows, TILE), lambda j: (0, base + j)),
            pl.BlockSpec((rows, 1), lambda j: (0, 0), pipeline_mode=pl.Buffered(1)),
            pl.BlockSpec((depth, TILE), lambda j: (0, base + j)),
        ]
        + [piece] * 7
        + [pl.BlockSpec(memory_space=pl.ANY)] * len(deps),
        out_specs=[out] * 8,
        out_shape=[jax.ShapeDtypeStruct((depth + more, width), jnp.bfloat16)] * 8,
        scratch_shapes=[pltpu.VMEM((features, TILE), jnp.bfloat16)],
        compiler_params=pltpu.CompilerParams(vmem_limit_bytes=VMEM_LIMIT),
        cost_estimate=pl.CostEstimate(
            flops=4 * rows * features * width,
            bytes_accessed=2 * rows * features + 4 * features * width + 2 * rows * width,
            transcendentals=0,
        ),
        name="grads",
    )(normed, targets, mask, weights, *pieces, *deps)


def deal_kernel(place_ref, *refs):
    for source, out in zip(refs[:Y], refs[Y:]):
        out[0] = source[...]


def deal(place, delta):
    rows = delta.shape[0]
    lanes = CORES * HALF

    def at(step):
        return lambda z, s: (0, z * Y + (s[0] // CORES + step) % Y)

    return pl.pallas_call(
        deal_kernel,
        grid_spec=pltpu.PrefetchScalarGridSpec(
            num_scalar_prefetch=1,
            grid=(Z_HI,),
            in_specs=[pl.BlockSpec((rows, lanes), at(step)) for step in range(Y)],
            out_specs=[pl.BlockSpec((1, rows, lanes), lambda z, s: (z, 0, 0))] * Y,
        ),
        out_shape=[jax.ShapeDtypeStruct((Z_HI, rows, lanes), jnp.bfloat16)] * Y,
        compiler_params=pltpu.CompilerParams(vmem_limit_bytes=SMALL_LIMIT),
        cost_estimate=pl.CostEstimate(flops=0, bytes_accessed=4 * delta.size, transcendentals=0),
        name="deal",
    )(place, *[delta] * Y)


def halves(value):
    rows = value.shape[0] // 2
    top, bottom = value[:rows], value[rows:]
    left = lax.broadcasted_iota(jnp.int32, top.shape, 1) < HALF
    first = jnp.where(left, top, pltpu.roll(bottom, HALF, 1))
    second = jnp.where(left, pltpu.roll(top, HALF, 1), bottom)
    return first, second


def place_kernel(place_ref, module_ref, *refs):
    sources, mine, theirs = refs[:Y], refs[-2], refs[-1]
    path = place_ref[0]
    core, own_y, own_z = path % CORES, (path // CORES) % Y, path // (CORES * Y)
    values = [source[0].astype(jnp.float32) for source in sources]
    labels = [module_ref[(own_z * Y + (own_y + Y - step) % Y) * CORES + core] for step in range(Y)]
    for m in range(mine.shape[1]):
        total = jnp.zeros_like(values[0])
        for value, label in zip(values, labels):
            total = total + jnp.where(label == m, 1.0, 0.0) * value
        first, second = halves(total)
        mine[0, m] = jnp.where(core == 0, first, second).astype(jnp.bfloat16)
        theirs[0, m] = jnp.where(core == 0, second, first).astype(jnp.bfloat16)


def place_sums(place, module_of_path, sources, modules, deps):
    zs, rows, lanes = sources[0].shape

    return pl.pallas_call(
        place_kernel,
        grid_spec=pltpu.PrefetchScalarGridSpec(
            num_scalar_prefetch=2,
            grid=(zs,),
            in_specs=[pl.BlockSpec((1, rows, lanes), lambda z, s, t: (z, 0, 0))] * Y
            + [pl.BlockSpec(memory_space=pl.ANY)] * len(deps),
            out_specs=[pl.BlockSpec((1, modules, rows // 2, lanes), lambda z, s, t: (z, 0, 0, 0))] * 2,
        ),
        out_shape=[jax.ShapeDtypeStruct((zs, modules, rows // 2, lanes), jnp.bfloat16)] * 2,
        compiler_params=pltpu.CompilerParams(vmem_limit_bytes=SMALL_LIMIT),
        cost_estimate=pl.CostEstimate(
            flops=8 * modules * zs * rows * lanes, bytes_accessed=16 * zs * rows * lanes, transcendentals=0
        ),
        name="place_sums",
    )(place, module_of_path, *sources, *deps)


def outer_kernel(sources, count_ref, *refs):
    parts = refs[:sources]
    params_ref, momentum_ref = refs[sources : sources + 2]
    params_out, momentum_out, step_out = refs[-3:]
    count = count_ref[pl.program_id(0)].astype(jnp.float32)
    total = parts[0][0].astype(jnp.float32)
    for part in parts[1:]:
        total = total + part[0].astype(jnp.float32)
    turned = total.T
    total = jnp.concatenate([turned[:HALF], turned[HALF:]], axis=1)
    outer_grad = total / count
    new_momentum = 0.9 * momentum_ref[0] + outer_grad
    step = 0.7 * (outer_grad + 0.9 * new_momentum)
    momentum_out[0] = new_momentum
    params_out[0] = params_ref[0] - step
    rows = step.shape[1] // 2
    step_out[0] = jnp.concatenate([step[:, :rows], step[:, rows:]], axis=0).T.astype(jnp.bfloat16)


def outer(sharing_counts, parts, params, momentum, deps):
    modules, columns, rows = params.shape
    state = pl.BlockSpec((1, columns, rows), lambda m, s: (m, 0, 0))
    packed = pl.BlockSpec((1,) + parts[0].shape[1:], lambda m, s: (m, 0, 0))
    return pl.pallas_call(
        functools.partial(outer_kernel, len(parts)),
        grid_spec=pltpu.PrefetchScalarGridSpec(
            num_scalar_prefetch=1,
            grid=(modules,),
            in_specs=[packed] * len(parts) + [state, state] + [pl.BlockSpec(memory_space=pl.ANY)] * len(deps),
            out_specs=[state, state, packed],
        ),
        out_shape=[
            jax.ShapeDtypeStruct(params.shape, jnp.float32),
            jax.ShapeDtypeStruct(params.shape, jnp.float32),
            jax.ShapeDtypeStruct(parts[0].shape, jnp.bfloat16),
        ],
        compiler_params=pltpu.CompilerParams(vmem_limit_bytes=SMALL_LIMIT),
        cost_estimate=pl.CostEstimate(flops=8 * params.size, bytes_accessed=32 * params.size, transcendentals=0),
        name="outer",
    )(sharing_counts, *parts, params, momentum, *deps)


def final_kernel(terms, first_chunk, place_ref, module_ref, weight_ref, step_ref, *refs):
    depth = weight_ref.shape[0]
    grad = refs[0][...].astype(jnp.float32)
    for term in refs[1:terms]:
        grad = grad + term[...].astype(jnp.float32)
    if first_chunk:
        out, rate_out = refs[-2:]
        half = (grad.shape[0] - depth) // 2
        count = BASE * grad[depth : depth + half, :128] + grad[depth + half :, :128]
        rate_out[...] = 0.25 / jnp.sqrt(count)
        rate, grad = rate_out[0:1, 0:1], grad[:depth]
    else:
        rate, out = refs[terms][0:1, 0:1], refs[-1]
    inner = weight_ref[...].astype(jnp.float32) - rate * grad
    rows = step_ref.shape[2]
    left = lax.broadcasted_iota(jnp.int32, (rows, CORES * HALF), 1) < HALF
    for k in range(step_ref.shape[0] // CORES):
        first = step_ref[CORES * k, 0].astype(jnp.float32)
        second = step_ref[CORES * k + 1, 0].astype(jnp.float32)
        top = jnp.where(left, first, pltpu.roll(second, HALF, 1))
        bottom = jnp.where(left, pltpu.roll(first, HALF, 1), second)
        span = slice(k * CORES * HALF, (k + 1) * CORES * HALF)
        out[:rows, span] = (inner[:rows, span] - top).astype(jnp.bfloat16)
        out[rows:, span] = (inner[rows:, span] - bottom).astype(jnp.bfloat16)


def final(place, module_of_path, weights, steps, terms, earlier, chunk, width):
    depth, features = weights.shape
    grid = width // TILE
    base = chunk * grid
    rows, lanes = steps.shape[2:]
    tiles = TILE // HALF
    first = earlier is None
    rate = pl.BlockSpec((8, 128), lambda j, s, t: (0, 0))
    extra = [] if first else [rate, pl.BlockSpec(memory_space=pl.ANY)]
    out = pl.BlockSpec((depth, TILE), lambda j, s, t: (0, base + j))
    result = jax.ShapeDtypeStruct((depth, features), jnp.bfloat16)
    return pl.pallas_call(
        functools.partial(final_kernel, len(terms), first),
        grid_spec=pltpu.PrefetchScalarGridSpec(
            num_scalar_prefetch=2,
            grid=(grid,),
            in_specs=[
                pl.BlockSpec((depth, TILE), lambda j, s, t: (0, base + j)),
                pl.BlockSpec((tiles, 1, rows, lanes), lambda j, s, t: (base + j, t[s[0]], 0, 0)),
            ]
            + [pl.BlockSpec((terms[0].shape[0], TILE), lambda j, s, t: (0, j))] * len(terms)
            + extra,
            out_specs=[out, rate] if first else out,
        ),
        out_shape=[result, jax.ShapeDtypeStruct((8, 128), jnp.float32)] if first else result,
        input_output_aliases={} if first else {5 + len(terms): 0},
        compiler_params=pltpu.CompilerParams(vmem_limit_bytes=SMALL_LIMIT),
        cost_estimate=pl.CostEstimate(flops=8 * depth * width, bytes_accessed=14 * depth * width, transcendentals=0),
        name="final",
    )(place, module_of_path, weights, steps, *terms, *([] if first else [earlier[1], earlier[0]]))


def after(value, *deps):
    return lax.optimization_barrier((value,) + deps)[0]


def shift(value, way):
    return lax.ppermute(value, "fsdp", way)


def by_offset(s, left, right, far, other, other_left, other_right, other_far):
    pieces = [None] * 8
    pieces[-s % X], pieces[s % X], pieces[2] = left, right, far
    pieces[X], pieces[X + -s % X], pieces[X + s % X], pieces[X + 2] = other, other_left, other_right, other_far
    return pieces[1:]


def gather_first(own):
    up, down, across = ring(1), ring(-1), pair()
    with jax.named_scope("shards"):
        left, right, other = shift(own, up), shift(own, down), shift(own, across)
    begun = (left, right, other)
    with jax.named_scope("shards_on"):
        far = shift(after(left, right, other), up)
        other_right = shift(after(other, left, right), down)
        other_left = shift(after(left, right, other), across)
    with jax.named_scope("shards_last"):
        other_far = shift(after(other_left, far), up)
    return by_offset(1, left, right, far, other, other_left, other_right, other_far), begun, other_left, other_far


def gather_second(own, other_left_a, other_far_a):
    up, down, across = ring(1), ring(-1), pair()
    with jax.named_scope("late_shards"):
        left = shift(own, down)
        other = shift(after(own, other_left_a), across)
        right = shift(after(own, other_far_a), up)
    with jax.named_scope("late_shards_on"):
        far, other_left, other_right = shift(left, down), shift(left, across), shift(other, up)
    with jax.named_scope("late_shards_last"):
        other_far = shift(other_left, down)
    return by_offset(-1, left, right, far, other, other_left, other_right, other_far), (left, other)


def add(*values):
    total = values[0].astype(jnp.float32)
    for value in values[1:]:
        total = total + value.astype(jnp.float32)
    return total.astype(jnp.bfloat16)


def scatter(blocks, s):
    ahead, back, across = ring(s), ring(-s), pair()
    move = lambda value, way: lax.ppermute(value, "fsdp", way)
    behind, before = -s % X, s % X
    with jax.named_scope("sum_far_other"):
        far_other = move(blocks[X + 2], back)
    with jax.named_scope("sum_near_other"):
        near_other = move(blocks[X + before], ahead)
    with jax.named_scope("sum_far"):
        far = move(after(blocks[2], far_other), back)
    with jax.named_scope("sum_near"):
        near = move(after(blocks[before], near_other), ahead)
    with jax.named_scope("sum_cross_side"):
        cross_side = move(add(blocks[X + behind], far_other), across)
    with jax.named_scope("sum_cross"):
        cross = move(add(blocks[X], near_other), across)
    with jax.named_scope("sum_side"):
        side = move(add(blocks[behind], far, cross_side), back)
    return [blocks[0], near, cross, side]


def per_device(
    inputs,
    targets,
    token_ids,
    path_weights,
    stale_deltas,
    module_params,
    momentum,
    module_of_path,
    sharing_counts,
):
    weights, delta = path_weights[0], stale_deltas[0]
    features = weights.shape[1]
    modules = sharing_counts.shape[0]
    place = jnp.stack([lax.axis_index("path"), lax.axis_index("fsdp")]).astype(jnp.int32)
    width = features // 2

    pieces = [None, None]
    pieces[0], begun, other_left, other_far = gather_first(weights[:, :width])
    normed = norm(place, inputs[0])

    dealt = deal(place, delta)
    dealt = [dealt[0]] + [lax.ppermute(dealt[k], "path", along_y(k)) for k in range(1, Y)]
    late = after(weights, *begun, *dealt[1:])[:, width:]
    pieces[1], late_begun = gather_second(late, other_left, other_far)
    mine, theirs = place_sums(place, module_of_path, dealt, modules, [normed, *begun])
    sums = add(mine, lax.ppermute(theirs, "path", cores()))
    along_z = [[(z * Y + y) * CORES + c for z in range(Z_HI)] for y in range(Y) for c in range(CORES)]
    total = lax.psum_scatter(sums, "path", scatter_dimension=0, axis_index_groups=along_z, tiled=True)[0]

    mask = (token_ids[0] != 0).astype(jnp.float32)[:, None]
    blocks = grads(normed, targets[0], mask, weights, pieces[0], 0, width, EXTRA, late_begun)
    new_params, new_momentum, step = outer(
        sharing_counts,
        [total],
        jnp.swapaxes(module_params, 1, 2),
        jnp.swapaxes(momentum, 1, 2),
        [blocks[0], *pieces[1]],
    )
    steps = lax.all_gather(step, "path", axis=0)

    terms = scatter(blocks, 1)
    blocks = grads(normed, targets[0], mask, weights, pieces[1], 1, width, 0)
    late_terms = scatter(blocks, -1)
    out = final(place, module_of_path, weights, steps, terms, None, 0, width)
    out = final(place, module_of_path, weights, steps, late_terms, out, 1, width)
    return (out[None], jnp.swapaxes(new_params, 1, 2), jnp.swapaxes(new_momentum, 1, 2))


def solution(mesh):
    return jax.shard_map(
        per_device,
        mesh=mesh,
        in_specs=(
            P("path", "fsdp", None),
            P("path", "fsdp", None),
            P("path", "fsdp"),
            P("path", "fsdp", None),
            P("path", "fsdp", None),
            P(None, "fsdp", "path"),
            P(None, "fsdp", "path"),
            P(),
            P(),
        ),
        out_specs=(P("path", "fsdp", None), P(None, "fsdp", "path"), P(None, "fsdp", "path")),
        check_vma=False,
    )
```

time: 321 us -> 189 us (0.59)
  waiting for transfers between devices: 233 us -> 73.1 us
  starting transfers between devices: 0.17 us -> 43 us
  Pallas kernels: 0 us -> 33.8 us
  matrix products: 24.3 us -> 0 us
  blocking collectives: 19.5 us -> 0 us
  other arithmetic: 15 us -> 4 us
  local copies, waits for them, and re-layouts: 11.2 us -> 18.7 us
    reduce_scatter x2 -> x1, waiting for transfers between devices: 214 us -> 0.01 us  [per_device(): lax.psum_scatter(sums, 'path', scatter_dimension=0, axis_index_groups=alo...]
    ppermute x0 -> x32, waiting for transfers between devices: none -> 73.1 us  [the longest x14 46.9 us: scatter(): move = lambda value, way: lax.ppermute(value, 'fsdp', way)]
    ppermute x0 -> x32, starting transfers between devices: none -> 42.9 us  [the longest x14 20 us: shift(): return lax.ppermute(value, 'fsdp', way)]
    pallas_call x0 -> x8, Pallas kernels: none -> 33.8 us  [the longest x2 21.5 us: grads(): pl.pallas_call(grad_kernel, grid=(steps,), in_specs=[pl.BlockSpec((rows,...]
    dot_general x3 -> x0, matrix products: 24.3 us -> none  [the longest x1 9.73 us: per_device(): jnp.dot(columns, lax.all_gather(weights, 'fsdp', axis=0, tiled=True), pre...]
    psum x1 -> x0, blocking collectives: 19.5 us -> none  [per_device(): count = lax.psum(jnp.sum(mask), 'fsdp')]
    all_gather x2 -> x1, waiting for transfers between devices: 18.2 us -> 0.01 us  [per_device(): steps = lax.all_gather(step, 'path', axis=0)]
    unnamed x10 -> x70, local copies, waits for them, and re-layouts: 0.02 us -> 14.9 us
  transfers between devices with their start and end apart: 4 -> 34, of which waited for: 3 -> 16; matrix products, arithmetic and copies ran while one was open for 12% -> 3% of each run, Pallas kernels for 0% -> 15%
where the time goes in v1:
time: 189 us; the launch traced here: 187 us
  waiting for transfers between devices  73.1 us (39%)
  starting transfers between devices  43 us (23%)
  Pallas kernels  33.8 us (18%)
  local copies, waits for them, and re-layouts  18.7 us (10%)
  between operations  14.3 us (8%)
  other arithmetic  4 us (2%)
    ppermute x14, waiting for transfers between devices, scatter(): move = lambda value, way: lax.ppermute(value, 'fsdp', way)  46.9 us
    ppermute x14, waiting for transfers between devices, shift(): return lax.ppermute(value, 'fsdp', way)  23.7 us
    pallas_call x2, Pallas kernels, grads(): pl.pallas_call(grad_kernel, grid=(steps,), in_specs=[pl.BlockSpec((rows,...  21.5 us
    ppermute x14, starting transfers between devices, shift(): return lax.ppermute(value, 'fsdp', way)  20 us
    ppermute x14, starting transfers between devices, scatter(): move = lambda value, way: lax.ppermute(value, 'fsdp', way)  19.1 us
    unnamed x70, local copies, waits for them, and re-layouts  14.9 us
    pallas_call x2, Pallas kernels, final(): pl.pallas_call(functools.partial(final_kernel, len(terms), first), grid_s...  5.25 us
    convert_element_type x7, other arithmetic, add(): return total.astype(jnp.bfloat16)  3.92 us
  transfers between devices with their start and end apart: 34, of which 16 were waited for; matrix products, arithmetic and copies ran while one was open for 3% of the time, Pallas kernels for 15%

profile of v1, /device:TPU:24, one launch (start us, length us, event | category | flops | bytes accessed | tf_op | source)
XLA Modules:
  0.0 187.0 jit_solution(9370855629776786666)
XLA Ops:
  7.2 1.9 %slice.8 = bf16[256,1024]{1,0:T(8,128)(2,1)} slice(bf16[256,2048]{1,0:T(8,128)(2,1)} %bitcast.21), slice={[0:256], [0:1024]} | slice | bytes 1048576 | tf_op jit(solution)/shard_map/slice | solution.py:388
  9.2 1.9 %collective-permute-start.5 = (bf16[256,1024]{1,0:T(8,128)(2,1)}, bf16[256,1024]{1,0:T(8,128)(2,1)}, u32[]{:S(2)}, u32[]{:S(2)}) collective-permute-start(bf16[256,1024]{1,0:T(8,128)(2,1)} %slice.8), channel_id=1, source_target_pairs={{0,4},{1,5},{2,6},{3,7},{4,0},{5,1},{6,2},{7,3},{8,12},{9,13},{10,... | collective-permute-start | bytes 1572872 | tf_op jit(solution)/shard_map/shards/ppermute | solution.py:305
  11.1 2.8 %collective-permute-start.4 = (bf16[256,1024]{1,0:T(8,128)(2,1)}, bf16[256,1024]{1,0:T(8,128)(2,1)}, u32[]{:S(2)}, u32[]{:S(2)}) collective-permute-start(bf16[256,1024]{1,0:T(8,128)(2,1)} %slice.8), channel_id=1, source_target_pairs={{0,3},{1,0},{2,1},{3,2},{4,7},{5,4},{6,5},{7,6},{8,11},{9,8},{10,9... | collective-permute-start | bytes 1572872 | tf_op jit(solution)/shard_map/shards/ppermute | solution.py:305
  13.9 1.4 deal.1
  15.6 2.6 %collective-permute-start.1 = (bf16[4,256,128]{2,1,0:T(8,128)(2,1)S(1)}, bf16[4,256,128]{2,1,0:T(8,128)(2,1)S(1)}, u32[]{:S(2)}, u32[]{:S(2)}) collective-permute-start(bf16[4,256,128]{2,1,0:T(8,128)(2,1)S(1)} %get-tuple-element.42), channel_id=1, source_target_pairs={{0,32},{8,40},{16,48},{24,56},{32,0},{40,8},{48,16},{56,24},{64,96... | collective-permute-start | bytes 786440 | tf_op jit(solution)/shard_map/ppermute | solution.py:392
  18.2 5.1 %collective-permute-done.5.refs_7_.rest_4_ = bf16[256,1024]{1,0:T(8,128)(2,1)} collective-permute-done((bf16[256,1024]{1,0:T(8,128)(2,1)}, bf16[256,1024]{1,0:T(8,128)(2,1)}, u32[]{:S(2)}, u32[]{:S(2)}) %collective-permute-start.5) | collective-permute-done | bytes 524320 | tf_op jit(solution)/shard_map/shards/ppermute | solution.py:305
  23.3 0.7 collective-permute-start.2
  24.1 1.9 %norm.1.refs_4_.n_ref = bf16[768,2048]{1,0:T(8,128)(2,1)S(1)} custom-call(s32[2]{0:T(128)S(1)} %pad_add_fusion.place_ref, bf16[768,2048]{1,0:T(8,128)(2,1)S(1)} %bitcast.27), custom_call_target="tpu_custom_call" | custom-call | flops 4718592 | bytes 6291456 | tf_op jit(solution)/shard_map/norm/pallas_call | solution.py:60
  26.0 2.4 %collective-permute-done.3.refs_5_.rest_3_ = bf16[256,1024]{1,0:T(8,128)(2,1)} collective-permute-done((bf16[256,1024]{1,0:T(8,128)(2,1)}, bf16[256,1024]{1,0:T(8,128)(2,1)}, u32[]{:S(2)}, u32[]{:S(2)}) %collective-permute-start.3) | collective-permute-done | bytes 524320 | tf_op jit(solution)/shard_map/shards/ppermute | solution.py:305
  29.4 2.5 %collective-permute-done.2.refs_3_ = bf16[4,256,128]{2,1,0:T(8,128)(2,1)S(1)} collective-permute-done((bf16[4,256,128]{2,1,0:T(8,128)(2,1)S(1)}, bf16[4,256,128]{2,1,0:T(8,128)(2,1)S(1)}, u32[]{:S(2)}, u32[]{:S(2)}) %collective-permute-start.2) | collective-permute-done | bytes 262176 | tf_op jit(solution)/shard_map/ppermute | solution.py:392
  31.9 0.9 slice.7
  32.8 2.8 %collective-permute-start.11 = (bf16[256,1024]{1,0:T(8,128)(2,1)}, bf16[256,1024]{1,0:T(8,128)(2,1)}, u32[]{:S(2)}, u32[]{:S(2)}) collective-permute-start(bf16[256,1024]{1,0:T(8,128)(2,1)} %slice.7), channel_id=1, source_target_pairs={{0,3},{1,0},{2,1},{3,2},{4,7},{5,4},{6,5},{7,6},{8,11},{9,8},{10,9... | collective-permute-start | bytes 1572872 | tf_op jit(solution)/shard_map/late_shards/ppermute | solution.py:305
  35.5 1.5 place_sums.1
  37.2 0.9 collective-permute-start.8
  38.1 2.9 %collective-permute-done.9.rest_7_ = bf16[256,1024]{1,0:T(8,128)(2,1)} collective-permute-done((bf16[256,1024]{1,0:T(8,128)(2,1)}, bf16[256,1024]{1,0:T(8,128)(2,1)}, u32[]{:S(2)}, u32[]{:S(2)}) %collective-permute-start.9) | collective-permute-done | bytes 524320 | tf_op jit(solution)/shard_map/shards_on/ppermute | solution.py:305
  41.0 1.3 collective-permute-done.7.rest_2_
  42.3 0.8 copy-done.24
  43.1 1.6 collective-permute-start.12
  44.6 3.6 %collective-permute-done.11.rest_8_.refs_4_.rest_1_ = bf16[256,1024]{1,0:T(8,128)(2,1)} collective-permute-done((bf16[256,1024]{1,0:T(8,128)(2,1)}, bf16[256,1024]{1,0:T(8,128)(2,1)}, u32[]{:S(2)}, u32[]{:S(2)}) %collective-permute-start.11) | collective-permute-done | bytes 524320 | tf_op jit(solution)/shard_map/late_shards/ppermute | solution.py:305
  48.2 1.6 collective-permute-start.15
  49.8 1.0 add_convert_fusion.6
  50.8 0.9 copy.15.mask_ref
  51.8 3.7 %collective-permute-start.13 = (bf16[256,1024]{1,0:T(8,128)(2,1)}, bf16[256,1024]{1,0:T(8,128)(2,1)S(1)}, u32[]{:S(2)}, u32[]{:S(2)}) collective-permute-start(bf16[256,1024]{1,0:T(8,128)(2,1)} %collective-permute-done.11.rest_8_.refs_4_.rest_1_), channel_id=1, source_target_pairs={{0,3},{1,0},{2,1},{3,2},{4,7},{5,4},{6,5},{7,6},{8,11},{9,8},{10,9... | collective-permute-start | bytes 1572872 | tf_op jit(solution)/shard_map/late_shards_on/ppermute | solution.py:305
  55.6 0.8 copy-done.28
  56.4 1.7 collective-permute-done.12.rest_9_.refs_7_.rest_4_
  58.1 1.0 collective-permute-start.17
  59.2 6.5 %collective-permute-done.15.refs_8_.rest_5_ = bf16[256,1024]{1,0:T(8,128)(2,1)S(1)} collective-permute-done((bf16[256,1024]{1,0:T(8,128)(2,1)}, bf16[256,1024]{1,0:T(8,128)(2,1)S(1)}, u32[]{:S(2)}, u32[]{:S(2)}) %collective-permute-start.15) | collective-permute-done | bytes 524320 | tf_op jit(solution)/shard_map/late_shards_on/ppermute | solution.py:305
  65.7 3.0 %collective-permute-start.16 = (bf16[256,1024]{1,0:T(8,128)(2,1)S(1)}, bf16[256,1024]{1,0:T(8,128)(2,1)S(1)}, u32[]{:S(2)}, u32[]{:S(2)}) collective-permute-start(bf16[256,1024]{1,0:T(8,128)(2,1)S(1)} %collective-permute-done.15.refs_8_.rest_5_), channel_id=1, source_target_pairs={{0,3},{1,0},{2,1},{3,2},{4,7},{5,4},{6,5},{7,6},{8,11},{9,8},{10,9... | collective-permute-start | bytes 1572872 | tf_op jit(solution)/shard_map/late_shards_last/ppermute | solution.py:305
  68.6 0.8 copy-done.26
  69.4 1.0 copy-done.14
  70.4 1.0 copy-done.25
  71.4 1.0 copy-done.27
  72.5 1.0 copy-done.29
  73.5 10.8 %grads.2 = (bf16[272,1024]{1,0:T(8,128)(2,1)S(1)}, bf16[272,1024]{1,0:T(8,128)(2,1)S(1)}, bf16[272,1024]{1,0:T(8,128)(2,1)}, bf16[272,1024]{1,0:T(8,128)(2,1)}, ...) custom-call(bf16[768,2048]{1,0:T(8,128)(2,1)} %copy-done.3, ...), custom_call_target="tpu_custom_call" | custom-call | flops 6442450944 | bytes 13107200 | tf_op jit(solution)/shard_map/grads/pallas_call | solution.py:104
  84.4 0.8 copy-done.22
  85.2 0.8 copy-done.12
  86.1 1.0 copy-done.13
  87.1 0.9 copy-done.17
  88.1 0.9 copy-done.18
  89.0 2.3 %outer.1 = (f32[4,64,256]{2,1,0:T(8,128)}, f32[4,64,256]{2,1,0:T(8,128)}, bf16[4,128,128]{2,1,0:T(8,128)(2,1)S(1)}) custom-call(s32[4]{0:T(128)S(1)} %copy-done.21, bf16[4,128,128]{2,1,0:T(8,128)(2,1)S(1)} %bitcast.30, f32[4,64,256]{2,1,0:T(8,128)S(1)} %bitcast.28, f32[4,64,256]{2,1,0:T(8,128)S(1)} %bitcast.29, ...), custom_call_target="tpu_custom_call" | custom-call | flops 524288 | bytes 2097152 | tf_op jit(solution)/shard_map/outer/pallas_call | solution.py:223
  92.0 3.2 %collective-permute-start.28 = (bf16[272,1024]{1,0:T(8,128)(2,1)}, bf16[272,1024]{1,0:T(8,128)(2,1)S(1)}, u32[]{:S(2)}, u32[]{:S(2)}) collective-permute-start(bf16[272,1024]{1,0:T(8,128)(2,1)} %get-tuple-element.70), channel_id=1, source_target_pairs={{0,3},{1,0},{2,1},{3,2},{4,7},{5,4},{6,5},{7,6},{8,11},{9,8},{10,9... | collective-permute-start | bytes 1671176 | tf_op jit(solution)/shard_map/sum_far_other/ppermute | solution.py:351
  95.3 1.0 copy-done.15
  96.3 10.6 %grads.3 = (bf16[256,1024]{1,0:T(8,128)(2,1)S(1)}, bf16[256,1024]{1,0:T(8,128)(2,1)S(1)}, bf16[256,1024]{1,0:T(8,128)(2,1)S(1)}, bf16[256,1024]{1,0:T(8,128)(2,1...) custom-call(bf16[768,2048]{1,0:T(8,128)(2,1)} %copy-done.3, ...), custom_call_target="tpu_custom_call" | custom-call | flops 6442450944 | bytes 13107200 | tf_op jit(solution)/shard_map/grads/pallas_call | solution.py:104
  107.0 2.0 %collective-permute-start.21 = (bf16[256,1024]{1,0:T(8,128)(2,1)S(1)}, bf16[256,1024]{1,0:T(8,128)(2,1)S(1)}, u32[]{:S(2)}, u32[]{:S(2)}) collective-permute-start(bf16[256,1024]{1,0:T(8,128)(2,1)S(1)} %get-tuple-element.61), channel_id=1, source_target_pairs={{0,1},{1,2},{2,3},{3,0},{4,5},{5,6},{6,7},{7,4},{8,9},{9,10},{10,1... | collective-permute-start | bytes 1572872 | tf_op jit(solution)/shard_map/sum_far_other/ppermute | solution.py:351
  109.1 3.2 %collective-permute-start.29 = (bf16[272,1024]{1,0:T(8,128)(2,1)S(1)}, bf16[272,1024]{1,0:T(8,128)(2,1)S(1)}, u32[]{:S(2)}, u32[]{:S(2)}) collective-permute-start(bf16[272,1024]{1,0:T(8,128)(2,1)S(1)} %copy-done.34), channel_id=1, source_target_pairs={{0,3},{1,0},{2,1},{3,2},{4,7},{5,4},{6,5},{7,6},{8,11},{9,8},{10,9... | collective-permute-start | bytes 1671176 | tf_op jit(solution)/shard_map/sum_far/ppermute | solution.py:351
  112.5 2.7 %collective-permute-start.30 = (bf16[272,1024]{1,0:T(8,128)(2,1)S(1)}, bf16[272,1024]{1,0:T(8,128)(2,1)S(1)}, u32[]{:S(2)}, u32[]{:S(2)}) collective-permute-start(bf16[272,1024]{1,0:T(8,128)(2,1)S(1)} %add_convert_fusion.1), channel_id=1, source_target_pairs={{0,4},{1,5},{2,6},{3,7},{4,0},{5,1},{6,2},{7,3},{8,12},{9,13},{10,... | collective-permute-start | bytes 1671176 | tf_op jit(solution)/shard_map/sum_cross_side/ppermute | solution.py:351
  115.4 6.5 %collective-permute-done.18 = bf16[256,1024]{1,0:T(8,128)(2,1)S(1)} collective-permute-done((bf16[256,1024]{1,0:T(8,128)(2,1)S(1)}, bf16[256,1024]{1,0:T(8,128)(2,1)S(1)}, u32[]{:S(2)}, u32[]{:S(2)}) %collective-permute-start.18) | collective-permute-done | bytes 524320 | tf_op jit(solution)/shard_map/sum_near_other/ppermute | solution.py:351
  121.8 1.3 collective-permute-done.21
  123.1 0.7 collective-permute-start.22
  124.1 2.4 %collective-permute-start.23 = (bf16[256,1024]{1,0:T(8,128)(2,1)S(1)}, bf16[256,1024]{1,0:T(8,128)(2,1)S(1)}, u32[]{:S(2)}, u32[]{:S(2)}) collective-permute-start(bf16[256,1024]{1,0:T(8,128)(2,1)S(1)} %add_convert_fusion.4), channel_id=1, source_target_pairs={{0,4},{1,5},{2,6},{3,7},{4,0},{5,1},{6,2},{7,3},{8,12},{9,13},{10,... | collective-permute-start | bytes 1572872 | tf_op jit(solution)/shard_map/sum_cross_side/ppermute | solution.py:351
  126.5 1.0 add_convert_fusion.5
  127.5 3.2 %collective-permute-done.29 = bf16[272,1024]{1,0:T(8,128)(2,1)S(1)} collective-permute-done((bf16[272,1024]{1,0:T(8,128)(2,1)S(1)}, bf16[272,1024]{1,0:T(8,128)(2,1)S(1)}, u32[]{:S(2)}, u32[]{:S(2)}) %collective-permute-start.29) | collective-permute-done | bytes 557088 | tf_op jit(solution)/shard_map/sum_far/ppermute | solution.py:351
  130.7 0.7 collective-permute-start.27
  131.4 1.2 collective-permute-start.19
  132.9 8.2 %collective-permute-done.22 = bf16[256,1024]{1,0:T(8,128)(2,1)S(1)} collective-permute-done((bf16[256,1024]{1,0:T(8,128)(2,1)S(1)}, bf16[256,1024]{1,0:T(8,128)(2,1)S(1)}, u32[]{:S(2)}, u32[]{:S(2)}) %collective-permute-start.22) | collective-permute-done | bytes 524320 | tf_op jit(solution)/shard_map/sum_far/ppermute | solution.py:351
  141.0 0.8 collective-permute-start.20
  141.8 13.9 %collective-permute-done.23 = bf16[256,1024]{1,0:T(8,128)(2,1)S(1)} collective-permute-done((bf16[256,1024]{1,0:T(8,128)(2,1)S(1)}, bf16[256,1024]{1,0:T(8,128)(2,1)S(1)}, u32[]{:S(2)}, u32[]{:S(2)}) %collective-permute-start.23) | collective-permute-done | bytes 524320 | tf_op jit(solution)/shard_map/sum_cross_side/ppermute | solution.py:351
  155.7 1.1 add_convert_fusion.3
  156.8 2.0 %collective-permute-start.24 = (bf16[256,1024]{1,0:T(8,128)(2,1)}, bf16[256,1024]{1,0:T(8,128)(2,1)}, u32[]{:S(2)}, u32[]{:S(2)}) collective-permute-start(bf16[256,1024]{1,0:T(8,128)(2,1)} %add_convert_fusion.3), channel_id=1, source_target_pairs={{0,1},{1,2},{2,3},{3,0},{4,5},{5,6},{6,7},{7,4},{8,9},{9,10},{10,1... | collective-permute-start | bytes 1572872 | tf_op jit(solution)/shard_map/sum_side/ppermute | solution.py:351
  158.8 12.3 %collective-permute-done.27.refs_2_ = bf16[272,1024]{1,0:T(8,128)(2,1)S(1)} collective-permute-done((bf16[272,1024]{1,0:T(8,128)(2,1)S(1)}, bf16[272,1024]{1,0:T(8,128)(2,1)S(1)}, u32[]{:S(2)}, u32[]{:S(2)}) %collective-permute-start.27) | collective-permute-done | bytes 557088 | tf_op jit(solution)/shard_map/sum_cross/ppermute | solution.py:351
  171.1 2.2 %copy-done.1 = bf16[128,128,128]{2,1,0:T(8,128)(2,1)S(1)} copy-done((bf16[128,128,128]{2,1,0:T(8,128)(2,1)S(1)}, bf16[128,128,128]{2,1,0:T(8,128)(2,1)}, u32[]{:S(2)}) %copy-start.1) | copy-done | bytes 4194328
  173.2 2.2 %final.2 = (bf16[256,2048]{1,0:T(8,128)(2,1)}, f32[8,128]{1,0:T(8,128)S(1)}) custom-call(s32[2]{0:T(128)S(1)} %pad_add_fusion.place_ref, s32[32]{0:T(128)S(1)} %copy-done.20, bf16[256,2048]{1,0:T(8,128)(2,1)S(1)} %bitcast.25, bf16[32,4,128,128]{3,2,1,0:T(8,128)(2,1)S(1)} %bitcast.19, bf16[272,1024]{1,0:T(8,128)(2,1)S(1)} %get-tuple-element.51.refs_3_.refs_0_, ...), custom_call_target="tpu_custom_call" | custom-call | flops 2097152 | bytes 3670016 | tf_op jit(solution)/shard_map/final/pallas_call | solution.py:279
  175.4 1.6 collective-permute-done.20.refs_2_
  177.1 3.1 %final.3 = bf16[256,2048]{1,0:T(8,128)(2,1)} custom-call(s32[2]{0:T(128)S(1)} %pad_add_fusion.place_ref, s32[32]{0:T(128)S(1)} %copy-done.20, bf16[256,2048]{1,0:T(8,128)(2,1)S(1)} %bitcast.26, bf16[32,4,128,128]{3,2,1,0:T(8,128)(2,1)S(1)} %bitcast.20, bf16[256,1024]{1,0:T(8,128)(2,1)S(1)} %copy-done.8, ...), custom_call_target="tpu_custom_call", output_to_operand_aliasing={{}: (9, {})} | custom-call | flops 2097152 | bytes 3670016 | tf_op jit(solution)/shard_map/final/pallas_call | solution.py:279
  (96 shorter events, 3.6 us)
Async XLA Ops:
  7.2 6.8 %copy-start = (bf16[1,256,2048]{2,1,0:T(8,128)(2,1)S(1)}, bf16[1,256,2048]{2,1,0:T(8,128)(2,1)}, u32[]{:S(2)}) copy-start(bf16[1,256,2048]{2,1,0:T(8,128)(2,1)} %param.13) | copy-start | bytes 3145732
  7.2 78.9 %reduce-scatter.2.cloned.1.call-start = ((), (), s32[]{:S(2)}) async-start(), calls=%async_computation.1 | async-start | bytes 655360 | tf_op jit(solution)/shard_map/reduce_scatter | solution.py:398
  9.2 14.2 %collective-permute-start.5 = (bf16[256,1024]{1,0:T(8,128)(2,1)}, bf16[256,1024]{1,0:T(8,128)(2,1)}, u32[]{:S(2)}, u32[]{:S(2)}) collective-permute-start(bf16[256,1024]{1,0:T(8,128)(2,1)} %slice.8), channel_id=1, source_target_pairs={{0,4},{1,5},{2,6},{3,7},{4,0},{5,1},{6,2},{7,3},{8,12},{9,13},{10,... | collective-permute-start | bytes 1572872 | tf_op jit(solution)/shard_map/shards/ppermute | solution.py:305
  11.1 14.9 %collective-permute-start.4 = (bf16[256,1024]{1,0:T(8,128)(2,1)}, bf16[256,1024]{1,0:T(8,128)(2,1)}, u32[]{:S(2)}, u32[]{:S(2)}) collective-permute-start(bf16[256,1024]{1,0:T(8,128)(2,1)} %slice.8), channel_id=1, source_target_pairs={{0,3},{1,0},{2,1},{3,2},{4,7},{5,4},{6,5},{7,6},{8,11},{9,8},{10,9... | collective-permute-start | bytes 1572872 | tf_op jit(solution)/shard_map/shards/ppermute | solution.py:305
  13.8 14.6 %collective-permute-start.3 = (bf16[256,1024]{1,0:T(8,128)(2,1)}, bf16[256,1024]{1,0:T(8,128)(2,1)}, u32[]{:S(2)}, u32[]{:S(2)}) collective-permute-start(bf16[256,1024]{1,0:T(8,128)(2,1)} %slice.8), channel_id=1, source_target_pairs={{0,1},{1,2},{2,3},{3,0},{4,5},{5,6},{6,7},{7,4},{8,9},{9,10},{10,1... | collective-permute-start | bytes 1572872 | tf_op jit(solution)/shard_map/shards/ppermute | solution.py:305
  13.9 10.1 %copy-start.6 = (bf16[1,768,2048]{2,1,0:T(8,128)(2,1)S(1)}, bf16[1,768,2048]{2,1,0:T(8,128)(2,1)}, u32[]{:S(2)}) copy-start(bf16[1,768,2048]{2,1,0:T(8,128)(2,1)} %param.9) | copy-start | bytes 9437188
  15.3 14.0 %collective-permute-start = (bf16[4,256,128]{2,1,0:T(8,128)(2,1)S(1)}, bf16[4,256,128]{2,1,0:T(8,128)(2,1)S(1)}, u32[]{:S(2)}, u32[]{:S(2)}) collective-permute-start(bf16[4,256,128]{2,1,0:T(8,128)(2,1)S(1)} %get-tuple-element.41), channel_id=1, source_target_pairs={{0,16},{8,24},{16,32},{24,40},{32,48},{40,56},{48,0},{56,8},{64,80... | collective-permute-start | bytes 786440 | tf_op jit(solution)/shard_map/ppermute | solution.py:392
  15.6 13.7 %collective-permute-start.1 = (bf16[4,256,128]{2,1,0:T(8,128)(2,1)S(1)}, bf16[4,256,128]{2,1,0:T(8,128)(2,1)S(1)}, u32[]{:S(2)}, u32[]{:S(2)}) collective-permute-start(bf16[4,256,128]{2,1,0:T(8,128)(2,1)S(1)} %get-tuple-element.42), channel_id=1, source_target_pairs={{0,32},{8,40},{16,48},{24,56},{32,0},{40,8},{48,16},{56,24},{64,96... | collective-permute-start | bytes 786440 | tf_op jit(solution)/shard_map/ppermute | solution.py:392
  23.3 8.6 %collective-permute-start.2 = (bf16[4,256,128]{2,1,0:T(8,128)(2,1)S(1)}, bf16[4,256,128]{2,1,0:T(8,128)(2,1)S(1)}, u32[]{:S(2)}, u32[]{:S(2)}) collective-permute-start(bf16[4,256,128]{2,1,0:T(8,128)(2,1)S(1)} %get-tuple-element.43), channel_id=1, source_target_pairs={{0,48},{8,56},{16,0},{24,8},{32,16},{40,24},{48,32},{56,40},{64,11... | collective-permute-start | bytes 786440 | tf_op jit(solution)/shard_map/ppermute | solution.py:392
  24.1 7.8 %copy-start.4 = (bf16[1,256,2048]{2,1,0:T(8,128)(2,1)S(1)}, bf16[1,256,2048]{2,1,0:T(8,128)(2,1)}, u32[]{:S(2)}) copy-start(bf16[1,256,2048]{2,1,0:T(8,128)(2,1)} %param.12) | copy-start | bytes 3145732
  24.1 11.4 %copy-start.20 = (s32[32]{0:T(128)S(1)}, s32[32]{0:T(128)}, u32[]{:S(2)}) copy-start(s32[32]{0:T(128)} %module_ref.5) | copy-start | bytes 388
  26.0 11.1 %copy-start.3 = (bf16[768,2048]{1,0:T(8,128)(2,1)}, bf16[768,2048]{1,0:T(8,128)(2,1)S(1)}, u32[]{:S(2)}) copy-start(bf16[768,2048]{1,0:T(8,128)(2,1)S(1)} %norm.1.refs_4_.n_ref) | copy-start | bytes 9437188
  28.5 12.5 %collective-permute-start.9 = (bf16[256,1024]{1,0:T(8,128)(2,1)}, bf16[256,1024]{1,0:T(8,128)(2,1)}, u32[]{:S(2)}, u32[]{:S(2)}) collective-permute-start(bf16[256,1024]{1,0:T(8,128)(2,1)} %collective-permute-done.3.refs_5_.rest_3_), channel_id=1, source_target_pairs={{0,4},{1,5},{2,6},{3,7},{4,0},{5,1},{6,2},{7,3},{8,12},{9,13},{10,... | collective-permute-start | bytes 1572872 | tf_op jit(solution)/shard_map/shards_on/ppermute | solution.py:305
  28.8 13.5 %collective-permute-start.7 = (bf16[256,1024]{1,0:T(8,128)(2,1)}, bf16[256,1024]{1,0:T(8,128)(2,1)S(1)}, u32[]{:S(2)}, u32[]{:S(2)}) collective-permute-start(bf16[256,1024]{1,0:T(8,128)(2,1)} %collective-permute-done.3.refs_5_.rest_3_), channel_id=1, source_target_pairs={{0,1},{1,2},{2,3},{3,0},{4,5},{5,6},{6,7},{7,4},{8,9},{9,10},{10,1... | collective-permute-start | bytes 1572872 | tf_op jit(solution)/shard_map/shards_on/ppermute | solution.py:305
  32.8 15.5 %collective-permute-start.11 = (bf16[256,1024]{1,0:T(8,128)(2,1)}, bf16[256,1024]{1,0:T(8,128)(2,1)}, u32[]{:S(2)}, u32[]{:S(2)}) collective-permute-start(bf16[256,1024]{1,0:T(8,128)(2,1)} %slice.7), channel_id=1, source_target_pairs={{0,3},{1,0},{2,1},{3,2},{4,7},{5,4},{6,5},{7,6},{8,11},{9,8},{10,9... | collective-permute-start | bytes 1572872 | tf_op jit(solution)/shard_map/late_shards/ppermute | solution.py:305
  37.1 13.7 %copy-start.33 = (s32[1,768]{1,0:T(1,128)S(1)}, s32[1,768]{1,0:T(1,128)}, u32[]{:S(2)}) copy-start(s32[1,768]{1,0:T(1,128)} %param.11) | copy-start | bytes 9220
  37.1 12.7 %collective-permute-start.6 = (bf16[4,4,128,128]{3,2,1,0:T(8,128)(2,1)S(1)}, bf16[4,4,128,128]{3,2,1,0:T(8,128)(2,1)S(1)}, u32[]{:S(2)}, u32[]{:S(2)}) collective-permute-start(bf16[4,4,128,128]{3,2,1,0:T(8,128)(2,1)S(1)} %get-tuple-element.45), channel_id=1, source_target_pairs={{0,8},{8,0},{16,24},{24,16},{32,40},{40,32},{48,56},{56,48},{64,72... | collective-permute-start | bytes 1572872 | tf_op jit(solution)/shard_map/ppermute | solution.py:396
  37.2 31.4 %collective-permute-start.8 = (bf16[256,1024]{1,0:T(8,128)(2,1)}, bf16[256,1024]{1,0:T(8,128)(2,1)S(1)}, u32[]{:S(2)}, u32[]{:S(2)}) collective-permute-start(bf16[256,1024]{1,0:T(8,128)(2,1)} %collective-permute-done.5.refs_7_.rest_4_), channel_id=1, source_target_pairs={{0,3},{1,0},{2,1},{3,2},{4,7},{5,4},{6,5},{7,6},{8,11},{9,8},{10,9... | collective-permute-start | bytes 1572872 | tf_op jit(solution)/shard_map/shards_on/ppermute | solution.py:305
  43.0 12.6 %collective-permute-start.10 = (bf16[256,1024]{1,0:T(8,128)(2,1)}, bf16[256,1024]{1,0:T(8,128)(2,1)S(1)}, u32[]{:S(2)}, u32[]{:S(2)}) collective-permute-start(bf16[256,1024]{1,0:T(8,128)(2,1)} %collective-permute-done.9.rest_7_), channel_id=1, source_target_pairs={{0,1},{1,2},{2,3},{3,0},{4,5},{5,6},{6,7},{7,4},{8,9},{9,10},{10,1... | collective-permute-start | bytes 1572872 | tf_op jit(solution)/shard_map/shards_last/ppermute | solution.py:305
  43.1 15.1 %collective-permute-start.12 = (bf16[256,1024]{1,0:T(8,128)(2,1)}, bf16[256,1024]{1,0:T(8,128)(2,1)S(1)}, u32[]{:S(2)}, u32[]{:S(2)}) collective-permute-start(bf16[256,1024]{1,0:T(8,128)(2,1)} %slice.7), channel_id=1, source_target_pairs={{0,4},{1,5},{2,6},{3,7},{4,0},{5,1},{6,2},{7,3},{8,12},{9,13},{10,... | collective-permute-start | bytes 1572872 | tf_op jit(solution)/shard_map/late_shards/ppermute | solution.py:305
  48.2 17.4 %collective-permute-start.15 = (bf16[256,1024]{1,0:T(8,128)(2,1)}, bf16[256,1024]{1,0:T(8,128)(2,1)S(1)}, u32[]{:S(2)}, u32[]{:S(2)}) collective-permute-start(bf16[256,1024]{1,0:T(8,128)(2,1)} %collective-permute-done.11.rest_8_.refs_4_.rest_1_), channel_id=1, source_target_pairs={{0,4},{1,5},{2,6},{3,7},{4,0},{5,1},{6,2},{7,3},{8,12},{9,13},{10,... | collective-permute-start | bytes 1572872 | tf_op jit(solution)/shard_map/late_shards_on/ppermute | solution.py:305
  50.7 120.3 %all-gather.3.cloned.1.call-start = ((), (), s32[]{:S(2)}) async-start(), calls=%async_computation.2 | async-start | bytes 4325376 | tf_op jit(solution)/shard_map/all_gather | solution.py:409
  51.8 33.4 %collective-permute-start.13 = (bf16[256,1024]{1,0:T(8,128)(2,1)}, bf16[256,1024]{1,0:T(8,128)(2,1)S(1)}, u32[]{:S(2)}, u32[]{:S(2)}) collective-permute-start(bf16[256,1024]{1,0:T(8,128)(2,1)} %collective-permute-done.11.rest_8_.refs_4_.rest_1_), channel_id=1, source_target_pairs={{0,3},{1,0},{2,1},{3,2},{4,7},{5,4},{6,5},{7,6},{8,11},{9,8},{10,9... | collective-permute-start | bytes 1572872 | tf_op jit(solution)/shard_map/late_shards_on/ppermute | solution.py:305
  56.4 28.8 %collective-permute-start.14 = (bf16[256,1024]{1,0:T(8,128)(2,1)}, bf16[256,1024]{1,0:T(8,128)(2,1)S(1)}, u32[]{:S(2)}, u32[]{:S(2)}) collective-permute-start(bf16[256,1024]{1,0:T(8,128)(2,1)} %slice.7), channel_id=1, source_target_pairs={{0,1},{1,2},{2,3},{3,0},{4,5},{5,6},{6,7},{7,4},{8,9},{9,10},{10,1... | collective-permute-start | bytes 1572872 | tf_op jit(solution)/shard_map/late_shards/ppermute | solution.py:305
  58.1 28.0 %copy-start.9 = (bf16[256,1024]{1,0:T(8,128)(2,1)}, bf16[256,1024]{1,0:T(8,128)(2,1)S(1)}, u32[]{:S(2)}) copy-start(bf16[256,1024]{1,0:T(8,128)(2,1)S(1)} %collective-permute-done.12.rest_9_.refs_7_.rest_4_) | copy-start | bytes 1572868
  58.1 27.1 %collective-permute-start.17 = (bf16[256,1024]{1,0:T(8,128)(2,1)S(1)}, bf16[256,1024]{1,0:T(8,128)(2,1)S(1)}, u32[]{:S(2)}, u32[]{:S(2)}) collective-permute-start(bf16[256,1024]{1,0:T(8,128)(2,1)S(1)} %collective-permute-done.12.rest_9_.refs_7_.rest_4_), channel_id=1, source_target_pairs={{0,1},{1,2},{2,3},{3,0},{4,5},{5,6},{6,7},{7,4},{8,9},{9,10},{10,1... | collective-permute-start | bytes 1572872 | tf_op jit(solution)/shard_map/late_shards_on/ppermute | solution.py:305
  65.6 20.4 %copy-start.10 = (bf16[256,1024]{1,0:T(8,128)(2,1)}, bf16[256,1024]{1,0:T(8,128)(2,1)S(1)}, u32[]{:S(2)}) copy-start(bf16[256,1024]{1,0:T(8,128)(2,1)S(1)} %collective-permute-done.15.refs_8_.rest_5_) | copy-start | bytes 1572868
  65.7 19.6 %collective-permute-start.16 = (bf16[256,1024]{1,0:T(8,128)(2,1)S(1)}, bf16[256,1024]{1,0:T(8,128)(2,1)S(1)}, u32[]{:S(2)}, u32[]{:S(2)}) collective-permute-start(bf16[256,1024]{1,0:T(8,128)(2,1)S(1)} %collective-permute-done.15.refs_8_.rest_5_), channel_id=1, source_target_pairs={{0,3},{1,0},{2,1},{3,2},{4,7},{5,4},{6,5},{7,6},{8,11},{9,8},{10,9... | collective-permute-start | bytes 1572872 | tf_op jit(solution)/shard_map/late_shards_last/ppermute | solution.py:305
  69.4 1.0 copy-start.14
  70.4 1.0 copy-start.25
  71.4 1.0 copy-start.27
  72.5 1.0 copy-start.29
  73.5 12.6 %copy-start.16 = (f32[4,256,64]{1,2,0:T(8,128)S(1)}, f32[4,256,64]{1,2,0:T(8,128)}, u32[]{:S(2)}) copy-start(f32[4,256,64]{1,2,0:T(8,128)} %param.14) | copy-start | bytes 786436
  73.5 12.6 %copy-start.21 = (s32[4]{0:T(128)S(1)}, s32[4]{0:T(128)}, u32[]{:S(2)}) copy-start(s32[4]{0:T(128)} %count_ref.1) | copy-start | bytes 52
  85.2 6.1 %copy-start.11 = (bf16[256,1024]{1,0:T(8,128)(2,1)}, bf16[256,1024]{1,0:T(8,128)(2,1)S(1)}, u32[]{:S(2)}) copy-start(bf16[256,1024]{1,0:T(8,128)(2,1)S(1)} %collective-permute-done.17.refs_10_.rest_7_) | copy-start | bytes 1572868
  85.2 0.9 copy-start.12
  86.1 1.0 copy-start.13
  87.1 0.9 copy-start.17
  88.1 0.9 copy-start.18
  91.9 17.1 %collective-permute-start.25 = (bf16[272,1024]{1,0:T(8,128)(2,1)}, bf16[272,1024]{1,0:T(8,128)(2,1)S(1)}, u32[]{:S(2)}, u32[]{:S(2)}) collective-permute-start(bf16[272,1024]{1,0:T(8,128)(2,1)} %get-tuple-element.65), channel_id=1, source_target_pairs={{0,1},{1,2},{2,3},{3,0},{4,5},{5,6},{6,7},{7,4},{8,9},{9,10},{10,1... | collective-permute-start | bytes 1671176 | tf_op jit(solution)/shard_map/sum_near_other/ppermute | solution.py:351
  92.0 17.0 %collective-permute-start.28 = (bf16[272,1024]{1,0:T(8,128)(2,1)}, bf16[272,1024]{1,0:T(8,128)(2,1)S(1)}, u32[]{:S(2)}, u32[]{:S(2)}) collective-permute-start(bf16[272,1024]{1,0:T(8,128)(2,1)} %get-tuple-element.70), channel_id=1, source_target_pairs={{0,3},{1,0},{2,1},{3,2},{4,7},{5,4},{6,5},{7,6},{8,11},{9,8},{10,9... | collective-permute-start | bytes 1671176 | tf_op jit(solution)/shard_map/sum_far_other/ppermute | solution.py:351
  95.3 1.0 copy-start.15
  96.3 12.7 %copy-start.23 = (bf16[272,1024]{1,0:T(8,128)(2,1)S(1)}, bf16[272,1024]{1,0:T(8,128)(2,1)}, u32[]{:S(2)}) copy-start(bf16[272,1024]{1,0:T(8,128)(2,1)} %copy-done.22) | copy-start | bytes 1671172
  96.3 12.8 %copy-start.34 = (bf16[272,1024]{1,0:T(8,128)(2,1)S(1)}, bf16[272,1024]{1,0:T(8,128)(2,1)}, u32[]{:S(2)}) copy-start(bf16[272,1024]{1,0:T(8,128)(2,1)} %get-tuple-element.71) | copy-start | bytes 1671172
  96.3 16.0 %copy-start.32 = (bf16[272,1024]{1,0:T(8,128)(2,1)S(1)}, bf16[272,1024]{1,0:T(8,128)(2,1)}, u32[]{:S(2)}) copy-start(bf16[272,1024]{1,0:T(8,128)(2,1)} %get-tuple-element.72) | copy-start | bytes 1671172
  106.9 8.5 %copy-start.7 = (bf16[256,1024]{1,0:T(8,128)(2,1)}, bf16[256,1024]{1,0:T(8,128)(2,1)S(1)}, u32[]{:S(2)}) copy-start(bf16[256,1024]{1,0:T(8,128)(2,1)S(1)} %get-tuple-element.54.refs_0_) | copy-start | bytes 1572868
  106.9 8.2 %copy-start.31 = (bf16[272,1024]{1,0:T(8,128)(2,1)S(1)}, bf16[272,1024]{1,0:T(8,128)(2,1)}, u32[]{:S(2)}) copy-start(bf16[272,1024]{1,0:T(8,128)(2,1)} %get-tuple-element.67) | copy-start | bytes 1671172
  106.9 14.9 %collective-permute-start.18 = (bf16[256,1024]{1,0:T(8,128)(2,1)S(1)}, bf16[256,1024]{1,0:T(8,128)(2,1)S(1)}, u32[]{:S(2)}, u32[]{:S(2)}) collective-permute-start(bf16[256,1024]{1,0:T(8,128)(2,1)S(1)} %get-tuple-element.56), channel_id=1, source_target_pairs={{0,3},{1,0},{2,1},{3,2},{4,7},{5,4},{6,5},{7,6},{8,11},{9,8},{10,9... | collective-permute-start | bytes 1572872 | tf_op jit(solution)/shard_map/sum_near_other/ppermute | solution.py:351
  107.0 16.1 %collective-permute-start.21 = (bf16[256,1024]{1,0:T(8,128)(2,1)S(1)}, bf16[256,1024]{1,0:T(8,128)(2,1)S(1)}, u32[]{:S(2)}, u32[]{:S(2)}) collective-permute-start(bf16[256,1024]{1,0:T(8,128)(2,1)S(1)} %get-tuple-element.61), channel_id=1, source_target_pairs={{0,1},{1,2},{2,3},{3,0},{4,5},{5,6},{6,7},{7,4},{8,9},{9,10},{10,1... | collective-permute-start | bytes 1572872 | tf_op jit(solution)/shard_map/sum_far_other/ppermute | solution.py:351
  109.0 47.8 %collective-permute-start.26 = (bf16[272,1024]{1,0:T(8,128)(2,1)S(1)}, bf16[272,1024]{1,0:T(8,128)(2,1)S(1)}, u32[]{:S(2)}, u32[]{:S(2)}) collective-permute-start(bf16[272,1024]{1,0:T(8,128)(2,1)S(1)} %copy-done.23), channel_id=1, source_target_pairs={{0,1},{1,2},{2,3},{3,0},{4,5},{5,6},{6,7},{7,4},{8,9},{9,10},{10,1... | collective-permute-start | bytes 1671176 | tf_op jit(solution)/shard_map/sum_near/ppermute | solution.py:351
  109.1 21.6 %collective-permute-start.29 = (bf16[272,1024]{1,0:T(8,128)(2,1)S(1)}, bf16[272,1024]{1,0:T(8,128)(2,1)S(1)}, u32[]{:S(2)}, u32[]{:S(2)}) collective-permute-start(bf16[272,1024]{1,0:T(8,128)(2,1)S(1)} %copy-done.34), channel_id=1, source_target_pairs={{0,3},{1,0},{2,1},{3,2},{4,7},{5,4},{6,5},{7,6},{8,11},{9,8},{10,9... | collective-permute-start | bytes 1671176 | tf_op jit(solution)/shard_map/sum_far/ppermute | solution.py:351
  112.5 18.9 %collective-permute-start.30 = (bf16[272,1024]{1,0:T(8,128)(2,1)S(1)}, bf16[272,1024]{1,0:T(8,128)(2,1)S(1)}, u32[]{:S(2)}, u32[]{:S(2)}) collective-permute-start(bf16[272,1024]{1,0:T(8,128)(2,1)S(1)} %add_convert_fusion.1), channel_id=1, source_target_pairs={{0,4},{1,5},{2,6},{3,7},{4,0},{5,1},{6,2},{7,3},{8,12},{9,13},{10,... | collective-permute-start | bytes 1671176 | tf_op jit(solution)/shard_map/sum_cross_side/ppermute | solution.py:351
  123.1 17.9 %collective-permute-start.22 = (bf16[256,1024]{1,0:T(8,128)(2,1)S(1)}, bf16[256,1024]{1,0:T(8,128)(2,1)S(1)}, u32[]{:S(2)}, u32[]{:S(2)}) collective-permute-start(bf16[256,1024]{1,0:T(8,128)(2,1)S(1)} %get-tuple-element.62), channel_id=1, source_target_pairs={{0,1},{1,2},{2,3},{3,0},{4,5},{5,6},{6,7},{7,4},{8,9},{9,10},{10,1... | collective-permute-start | bytes 1572872 | tf_op jit(solution)/shard_map/sum_far/ppermute | solution.py:351
  124.1 8.5 %copy-start.30 = (bf16[272,1024]{1,0:T(8,128)(2,1)S(1)}, bf16[272,1024]{1,0:T(8,128)(2,1)}, u32[]{:S(2)}) copy-start(bf16[272,1024]{1,0:T(8,128)(2,1)} %get-tuple-element.68) | copy-start | bytes 1671172
  124.1 31.6 %collective-permute-start.23 = (bf16[256,1024]{1,0:T(8,128)(2,1)S(1)}, bf16[256,1024]{1,0:T(8,128)(2,1)S(1)}, u32[]{:S(2)}, u32[]{:S(2)}) collective-permute-start(bf16[256,1024]{1,0:T(8,128)(2,1)S(1)} %add_convert_fusion.4), channel_id=1, source_target_pairs={{0,4},{1,5},{2,6},{3,7},{4,0},{5,1},{6,2},{7,3},{8,12},{9,13},{10,... | collective-permute-start | bytes 1572872 | tf_op jit(solution)/shard_map/sum_cross_side/ppermute | solution.py:351
  130.7 40.4 %collective-permute-start.27 = (bf16[272,1024]{1,0:T(8,128)(2,1)S(1)}, bf16[272,1024]{1,0:T(8,128)(2,1)S(1)}, u32[]{:S(2)}, u32[]{:S(2)}) collective-permute-start(bf16[272,1024]{1,0:T(8,128)(2,1)S(1)} %add_convert_fusion.2), channel_id=1, source_target_pairs={{0,4},{1,5},{2,6},{3,7},{4,0},{5,1},{6,2},{7,3},{8,12},{9,13},{10,... | collective-permute-start | bytes 1671176 | tf_op jit(solution)/shard_map/sum_cross/ppermute | solution.py:351
  131.4 44.0 %collective-permute-start.19 = (bf16[256,1024]{1,0:T(8,128)(2,1)}, bf16[256,1024]{1,0:T(8,128)(2,1)}, u32[]{:S(2)}, u32[]{:S(2)}) collective-permute-start(bf16[256,1024]{1,0:T(8,128)(2,1)} %get-tuple-element.57), channel_id=1, source_target_pairs={{0,3},{1,0},{2,1},{3,2},{4,7},{5,4},{6,5},{7,6},{8,11},{9,8},{10,9... | collective-permute-start | bytes 1572872 | tf_op jit(solution)/shard_map/sum_near/ppermute | solution.py:351
  132.9 38.2 %copy-start.5 = (bf16[1,256,2048]{2,1,0:T(8,128)(2,1)S(1)}, bf16[1,256,2048]{2,1,0:T(8,128)(2,1)}, u32[]{:S(2)}) copy-start(bf16[1,256,2048]{2,1,0:T(8,128)(2,1)} %param.12) | copy-start | bytes 3145732
  141.0 36.0 %collective-permute-start.20 = (bf16[256,1024]{1,0:T(8,128)(2,1)}, bf16[256,1024]{1,0:T(8,128)(2,1)}, u32[]{:S(2)}, u32[]{:S(2)}) collective-permute-start(bf16[256,1024]{1,0:T(8,128)(2,1)} %add_convert_fusion.5), channel_id=1, source_target_pairs={{0,4},{1,5},{2,6},{3,7},{4,0},{5,1},{6,2},{7,3},{8,12},{9,13},{10,... | collective-permute-start | bytes 1572872 | tf_op jit(solution)/shard_map/sum_cross/ppermute | solution.py:351
  155.7 15.4 %collective-permute-start.31 = (bf16[272,1024]{1,0:T(8,128)(2,1)S(1)}, bf16[272,1024]{1,0:T(8,128)(2,1)S(1)}, u32[]{:S(2)}, u32[]{:S(2)}) collective-permute-start(bf16[272,1024]{1,0:T(8,128)(2,1)S(1)} %add_convert_fusion), channel_id=1, source_target_pairs={{0,3},{1,0},{2,1},{3,2},{4,7},{5,4},{6,5},{7,6},{8,11},{9,8},{10,9... | collective-permute-start | bytes 1671176 | tf_op jit(solution)/shard_map/sum_side/ppermute | solution.py:351
  156.8 20.3 %collective-permute-start.24 = (bf16[256,1024]{1,0:T(8,128)(2,1)}, bf16[256,1024]{1,0:T(8,128)(2,1)}, u32[]{:S(2)}, u32[]{:S(2)}) collective-permute-start(bf16[256,1024]{1,0:T(8,128)(2,1)} %add_convert_fusion.3), channel_id=1, source_target_pairs={{0,1},{1,2},{2,3},{3,0},{4,5},{5,6},{6,7},{7,4},{8,9},{9,10},{10,1... | collective-permute-start | bytes 1572872 | tf_op jit(solution)/shard_map/sum_side/ppermute | solution.py:351
  171.0 2.2 %copy-start.1 = (bf16[128,128,128]{2,1,0:T(8,128)(2,1)S(1)}, bf16[128,128,128]{2,1,0:T(8,128)(2,1)}, u32[]{:S(2)}) copy-start(bf16[128,128,128]{2,1,0:T(8,128)(2,1)} %all-gather.3.cloned.1.call-done) | copy-start | bytes 12582916
  173.2 3.8 %copy-start.2 = (bf16[128,128,128]{2,1,0:T(8,128)(2,1)S(1)}, bf16[128,128,128]{2,1,0:T(8,128)(2,1)}, u32[]{:S(2)}) copy-start(bf16[128,128,128]{2,1,0:T(8,128)(2,1)} %all-gather.3.cloned.1.call-done) | copy-start | bytes 12582916
  173.2 3.8 %copy-start.8 = (bf16[256,1024]{1,0:T(8,128)(2,1)S(1)}, bf16[256,1024]{1,0:T(8,128)(2,1)}, u32[]{:S(2)}) copy-start(bf16[256,1024]{1,0:T(8,128)(2,1)} %copy-done.7) | copy-start | bytes 1572868
  (5 other events, 3.8 us)
Sparse Core Ops, SparseCore 0:
  50.9 30.6 reduce-scatter.1
  92.1 73.6 all-gather.2

commit v2 on v1

--- a/solution.py
+++ b/solution.py
@@ -13,7 +13,7 @@
 TILE = 512
 BASE = 32.0
 EXTRA = 16
-VMEM_LIMIT = 48 * 1024 * 1024
+VMEM_LIMIT = 60 * 1024 * 1024
 SMALL_LIMIT = 16 * 1024 * 1024
 
 
@@ -28,6 +28,15 @@
 def along_y(step):
     return [
         ((z * Y + y) * CORES + c, (z * Y + (y + step) % Y) * CORES + c)
+        for z in range(Z_HI)
+        for y in range(Y)
+        for c in range(CORES)
+    ]
+
+
+def along_z(step):
+    return [
+        ((z * Y + y) * CORES + c, (((z + step) % Z_HI) * Y + y) * CORES + c)
         for z in range(Z_HI)
         for y in range(Y)
         for c in range(CORES)
@@ -216,7 +225,7 @@
     step_out[0] = jnp.concatenate([step[:, :rows], step[:, rows:]], axis=0).T.astype(jnp.bfloat16)
 
 
-def outer(sharing_counts, parts, params, momentum, deps):
+def outer(sharing_counts, parts, params, momentum):
     modules, columns, rows = params.shape
     state = pl.BlockSpec((1, columns, rows), lambda m, s: (m, 0, 0))
     packed = pl.BlockSpec((1,) + parts[0].shape[1:], lambda m, s: (m, 0, 0))
@@ -225,7 +234,7 @@
         grid_spec=pltpu.PrefetchScalarGridSpec(
             num_scalar_prefetch=1,
             grid=(modules,),
-            in_specs=[packed] * len(parts) + [state, state] + [pl.BlockSpec(memory_space=pl.ANY)] * len(deps),
+            in_specs=[packed] * len(parts) + [state, state],
             out_specs=[state, state, packed],
         ),
         out_shape=[
@@ -236,7 +245,7 @@
         compiler_params=pltpu.CompilerParams(vmem_limit_bytes=SMALL_LIMIT),
         cost_estimate=pl.CostEstimate(flops=8 * params.size, bytes_accessed=32 * params.size, transcendentals=0),
         name="outer",
-    )(sharing_counts, *parts, params, momentum, *deps)
+    )(sharing_counts, *parts, params, momentum)
 
 
 def final_kernel(terms, first_chunk, place_ref, module_ref, weight_ref, step_ref, *refs):
@@ -253,11 +262,11 @@
     else:
         rate, out = refs[terms][0:1, 0:1], refs[-1]
     inner = weight_ref[...].astype(jnp.float32) - rate * grad
-    rows = step_ref.shape[2]
+    rows = step_ref.shape[3]
     left = lax.broadcasted_iota(jnp.int32, (rows, CORES * HALF), 1) < HALF
     for k in range(step_ref.shape[0] // CORES):
-        first = step_ref[CORES * k, 0].astype(jnp.float32)
-        second = step_ref[CORES * k + 1, 0].astype(jnp.float32)
+        first = step_ref[CORES * k, 0, 0].astype(jnp.float32)
+        second = step_ref[CORES * k + 1, 0, 0].astype(jnp.float32)
         top = jnp.where(left, first, pltpu.roll(second, HALF, 1))
         bottom = jnp.where(left, pltpu.roll(first, HALF, 1), second)
         span = slice(k * CORES * HALF, (k + 1) * CORES * HALF)
@@ -269,8 +278,11 @@
     depth, features = weights.shape
     grid = width // TILE
     base = chunk * grid
-    rows, lanes = steps.shape[2:]
-    tiles = TILE // HALF
+    rows, lanes = steps.shape[3:]
+
+    def away(j, s, t):
+        return (0, (s[0] // (CORES * Y) + Z_HI - (base + j)) % Z_HI, t[s[0]], 0, 0)
+
     first = earlier is None
     rate = pl.BlockSpec((8, 128), lambda j, s, t: (0, 0))
     extra = [] if first else [rate, pl.BlockSpec(memory_space=pl.ANY)]
@@ -283,7 +295,7 @@
             grid=(grid,),
             in_specs=[
                 pl.BlockSpec((depth, TILE), lambda j, s, t: (0, base + j)),
-                pl.BlockSpec((tiles, 1, rows, lanes), lambda j, s, t: (base + j, t[s[0]], 0, 0)),
+                pl.BlockSpec((CORES * Y, 1, 1, rows, lanes), away),
             ]
             + [pl.BlockSpec((terms[0].shape[0], TILE), lambda j, s, t: (0, j))] * len(terms)
             + extra,
@@ -326,11 +338,11 @@
     return by_offset(1, left, right, far, other, other_left, other_right, other_far), begun, other_left, other_far
 
 
-def gather_second(own, other_left_a, other_far_a):
+def gather_second(own, other_left_a, other_far_a, sums):
     up, down, across = ring(1), ring(-1), pair()
     with jax.named_scope("late_shards"):
         left = shift(own, down)
-        other = shift(after(own, other_left_a), across)
+        other = shift(after(own, other_left_a, sums), across)
         right = shift(after(own, other_far_a), up)
     with jax.named_scope("late_shards_on"):
         far, other_left, other_right = shift(left, down), shift(left, across), shift(other, up)
@@ -364,7 +376,7 @@
         cross = move(add(blocks[X], near_other), across)
     with jax.named_scope("sum_side"):
         side = move(add(blocks[behind], far, cross_side), back)
-    return [blocks[0], near, cross, side]
+    return [blocks[0], near, cross, side], (far_other, near_other)
 
 
 def per_device(
@@ -391,26 +403,28 @@
     dealt = deal(place, delta)
     dealt = [dealt[0]] + [lax.ppermute(dealt[k], "path", along_y(k)) for k in range(1, Y)]
     late = after(weights, *begun, *dealt[1:])[:, width:]
-    pieces[1], late_begun = gather_second(late, other_left, other_far)
     mine, theirs = place_sums(place, module_of_path, dealt, modules, [normed, *begun])
     sums = add(mine, lax.ppermute(theirs, "path", cores()))
-    along_z = [[(z * Y + y) * CORES + c for z in range(Z_HI)] for y in range(Y) for c in range(CORES)]
-    total = lax.psum_scatter(sums, "path", scatter_dimension=0, axis_index_groups=along_z, tiled=True)[0]
+    pieces[1], late_begun = gather_second(late, other_left, other_far, sums)
+    columns = [[(z * Y + y) * CORES + c for z in range(Z_HI)] for y in range(Y) for c in range(CORES)]
+    total = lax.psum_scatter(sums, "path", scatter_dimension=0, axis_index_groups=columns, tiled=True)[0]
 
     mask = (token_ids[0] != 0).astype(jnp.float32)[:, None]
     blocks = grads(normed, targets[0], mask, weights, pieces[0], 0, width, EXTRA, late_begun)
     new_params, new_momentum, step = outer(
-        sharing_counts,
+        after(sharing_counts, blocks[0], *pieces[1]),
         [total],
         jnp.swapaxes(module_params, 1, 2),
         jnp.swapaxes(momentum, 1, 2),
-        [blocks[0], *pieces[1]],
     )
-    steps = lax.all_gather(step, "path", axis=0)
-
-    terms = scatter(blocks, 1)
+    with jax.named_scope("steps_along_z"):
+        steps = [step] + [lax.ppermute(step, "path", along_z(k)) for k in range(1, Z_HI)]
+    terms, begun = scatter(blocks, 1)
     blocks = grads(normed, targets[0], mask, weights, pieces[1], 1, width, 0)
-    late_terms = scatter(blocks, -1)
+    planes = [[(z * Y + y) * CORES + c for y in range(Y) for c in range(CORES)] for z in range(Z_HI)]
+    steps = after(jnp.stack(steps), blocks[0], *begun)
+    steps = lax.all_gather(steps, "path", axis=0, axis_index_groups=planes)
+    late_terms, _ = scatter(blocks, -1)
     out = final(place, module_of_path, weights, steps, terms, None, 0, width)
     out = final(place, module_of_path, weights, steps, late_terms, out, 1, width)
     return (out[None], jnp.swapaxes(new_params, 1, 2), jnp.swapaxes(new_momentum, 1, 2))

time: 189 us -> 185 us (0.979)
  starting transfers between devices: 43 us -> 53.8 us
  local copies, waits for them, and re-layouts: 18.7 us -> 9.47 us
  waiting for transfers between devices: 73.1 us -> 67.4 us
    ppermute x14, waiting for transfers between devices: 46.9 us -> 35.3 us  [scatter(): move = lambda value, way: lax.ppermute(value, 'fsdp', way)]
    ppermute x0 -> x3, starting transfers between devices: none -> 10.4 us  [per_device(): lax.ppermute(step, 'path', along_z(k))]
    unnamed x70 -> x62, local copies, waits for them, and re-layouts: 14.9 us -> 6.53 us
    ppermute x14, waiting for transfers between devices: 23.7 us -> 29.5 us  [shift(): return lax.ppermute(value, 'fsdp', way)]
  transfers between devices with their start and end apart: 34 -> 37, of which waited for: 16 -> 13; matrix products, arithmetic and copies ran while one was open for 3% -> 3% of each run, Pallas kernels for 15% -> 17%
where the time goes in v2:
time: 185 us
  waiting for transfers between devices  67.4 us (36%)
  starting transfers between devices  53.8 us (29%)
  Pallas kernels  34.8 us (19%)
  between operations  14.4 us (8%)
  local copies, waits for them, and re-layouts  9.47 us (5%)
  other arithmetic  4.92 us (3%)
    ppermute x14, waiting for transfers between devices, scatter(): move = lambda value, way: lax.ppermute(value, 'fsdp', way)  35.3 us
    ppermute x14, waiting for transfers between devices, shift(): return lax.ppermute(value, 'fsdp', way)  29.5 us
    pallas_call x2, Pallas kernels, grads(): pl.pallas_call(grad_kernel, grid=(steps,), in_specs=[pl.BlockSpec((rows,...  22.3 us
    ppermute x14, starting transfers between devices, shift(): return lax.ppermute(value, 'fsdp', way)  21.7 us
    ppermute x14, starting transfers between devices, scatter(): move = lambda value, way: lax.ppermute(value, 'fsdp', way)  17.9 us
    ppermute x3, starting transfers between devices, per_device(): lax.ppermute(step, 'path', along_z(k))  10.4 us
    unnamed x62, local copies, waits for them, and re-layouts  6.53 us
    pallas_call x2, Pallas kernels, final(): pl.pallas_call(functools.partial(final_kernel, len(terms), first), grid_s...  5.33 us
  transfers between devices with their start and end apart: 37, of which 13 were waited for; matrix products, arithmetic and copies ran while one was open for 3% of the time, Pallas kernels for 17%

profile of v2, /device:TPU:24, one launch (start us, length us, event | category | flops | bytes accessed | tf_op | source)
XLA Modules:
  0.0 184.8 jit_solution(7807608007425476935)
XLA Ops:
  7.2 1.9 %slice.8 = bf16[256,1024]{1,0:T(8,128)(2,1)} slice(bf16[256,2048]{1,0:T(8,128)(2,1)} %bitcast.25), slice={[0:256], [0:1024]} | slice | bytes 1048576 | tf_op jit(solution)/shard_map/slice | solution.py:400
  9.2 2.8 %collective-permute-start = (bf16[256,1024]{1,0:T(8,128)(2,1)}, bf16[256,1024]{1,0:T(8,128)(2,1)S(1)}, u32[]{:S(2)}, u32[]{:S(2)}) collective-permute-start(bf16[256,1024]{1,0:T(8,128)(2,1)} %slice.8), channel_id=1, source_target_pairs={{0,3},{1,0},{2,1},{3,2},{4,7},{5,4},{6,5},{7,6},{8,11},{9,8},{10,9... | collective-permute-start | bytes 1572872 | tf_op jit(solution)/shard_map/shards/ppermute | solution.py:317
  11.9 1.9 %collective-permute-start.2 = (bf16[256,1024]{1,0:T(8,128)(2,1)}, bf16[256,1024]{1,0:T(8,128)(2,1)}, u32[]{:S(2)}, u32[]{:S(2)}) collective-permute-start(bf16[256,1024]{1,0:T(8,128)(2,1)} %slice.8), channel_id=1, source_target_pairs={{0,4},{1,5},{2,6},{3,7},{4,0},{5,1},{6,2},{7,3},{8,12},{9,13},{10,... | collective-permute-start | bytes 1572872 | tf_op jit(solution)/shard_map/shards/ppermute | solution.py:317
  13.9 1.4 deal.1
  15.3 0.3 collective-permute-start.7
  15.6 2.6 %collective-permute-start.8 = (bf16[4,256,128]{2,1,0:T(8,128)(2,1)S(1)}, bf16[4,256,128]{2,1,0:T(8,128)(2,1)S(1)}, u32[]{:S(2)}, u32[]{:S(2)}) collective-permute-start(bf16[4,256,128]{2,1,0:T(8,128)(2,1)S(1)} %get-tuple-element.46), channel_id=1, source_target_pairs={{0,32},{8,40},{16,48},{24,56},{32,0},{40,8},{48,16},{56,24},{64,96... | collective-permute-start | bytes 786440 | tf_op jit(solution)/shard_map/ppermute | solution.py:404
  18.2 5.2 %collective-permute-done.refs_6_.rest_1_ = bf16[256,1024]{1,0:T(8,128)(2,1)S(1)} collective-permute-done((bf16[256,1024]{1,0:T(8,128)(2,1)}, bf16[256,1024]{1,0:T(8,128)(2,1)S(1)}, u32[]{:S(2)}, u32[]{:S(2)}) %collective-permute-start) | collective-permute-done | bytes 524320 | tf_op jit(solution)/shard_map/shards/ppermute | solution.py:317
  23.4 0.8 copy-done.8
  24.2 0.7 collective-permute-start.9
  25.0 1.9 %norm.1.refs_4_.n_ref = bf16[768,2048]{1,0:T(8,128)(2,1)S(1)} custom-call(s32[2]{0:T(128)S(1)} %pad_add_fusion.place_ref, bf16[768,2048]{1,0:T(8,128)(2,1)S(1)} %bitcast.31), custom_call_target="tpu_custom_call" | custom-call | flops 4718592 | bytes 6291456 | tf_op jit(solution)/shard_map/norm/pallas_call | solution.py:69
  27.0 2.0 %collective-permute-start.5 = (bf16[256,1024]{1,0:T(8,128)(2,1)}, bf16[256,1024]{1,0:T(8,128)(2,1)}, u32[]{:S(2)}, u32[]{:S(2)}) collective-permute-start(bf16[256,1024]{1,0:T(8,128)(2,1)} %collective-permute-done.1.refs_5_.rest_3_), channel_id=1, source_target_pairs={{0,4},{1,5},{2,6},{3,7},{4,0},{5,1},{6,2},{7,3},{8,12},{9,13},{10,... | collective-permute-start | bytes 1572872 | tf_op jit(solution)/shard_map/shards_on/ppermute | solution.py:317
  29.0 1.1 collective-permute-start.3
  30.1 2.5 %collective-permute-done.9.refs_3_ = bf16[4,256,128]{2,1,0:T(8,128)(2,1)S(1)} collective-permute-done((bf16[4,256,128]{2,1,0:T(8,128)(2,1)S(1)}, bf16[4,256,128]{2,1,0:T(8,128)(2,1)S(1)}, u32[]{:S(2)}, u32[]{:S(2)}) %collective-permute-start.9) | collective-permute-done | bytes 262176 | tf_op jit(solution)/shard_map/ppermute | solution.py:404
  32.6 1.5 place_sums.1
  34.4 3.7 %collective-permute-start.10 = (bf16[256,1024]{1,0:T(8,128)(2,1)S(1)}, bf16[256,1024]{1,0:T(8,128)(2,1)S(1)}, u32[]{:S(2)}, u32[]{:S(2)}) collective-permute-start(bf16[256,1024]{1,0:T(8,128)(2,1)S(1)} %slice.7), channel_id=1, source_target_pairs={{0,3},{1,0},{2,1},{3,2},{4,7},{5,4},{6,5},{7,6},{8,11},{9,8},{10,9... | collective-permute-start | bytes 1572872 | tf_op jit(solution)/shard_map/late_shards/ppermute | solution.py:317
  38.0 2.0 %collective-permute-done.5.rest_7_ = bf16[256,1024]{1,0:T(8,128)(2,1)} collective-permute-done((bf16[256,1024]{1,0:T(8,128)(2,1)}, bf16[256,1024]{1,0:T(8,128)(2,1)}, u32[]{:S(2)}, u32[]{:S(2)}) %collective-permute-start.5) | collective-permute-done | bytes 524320 | tf_op jit(solution)/shard_map/shards_on/ppermute | solution.py:317
  40.0 3.2 %collective-permute-done.3.rest_2_ = bf16[256,1024]{1,0:T(8,128)(2,1)S(1)} collective-permute-done((bf16[256,1024]{1,0:T(8,128)(2,1)}, bf16[256,1024]{1,0:T(8,128)(2,1)S(1)}, u32[]{:S(2)}, u32[]{:S(2)}) %collective-permute-start.3) | collective-permute-done | bytes 524320 | tf_op jit(solution)/shard_map/shards_on/ppermute | solution.py:317
  43.3 0.8 copy-done.26
  44.1 0.9 add_convert_fusion.6
  45.0 0.3 collective-permute-start.12
  45.3 4.5 %collective-permute-done.10.rest_8_.rest_1_ = bf16[256,1024]{1,0:T(8,128)(2,1)S(1)} collective-permute-done((bf16[256,1024]{1,0:T(8,128)(2,1)S(1)}, bf16[256,1024]{1,0:T(8,128)(2,1)S(1)}, u32[]{:S(2)}, u32[]{:S(2)}) %collective-permute-start.10) | collective-permute-done | bytes 524320 | tf_op jit(solution)/shard_map/late_shards/ppermute | solution.py:317
  49.9 1.9 %collective-permute-start.15 = (bf16[256,1024]{1,0:T(8,128)(2,1)S(1)}, bf16[256,1024]{1,0:T(8,128)(2,1)}, u32[]{:S(2)}, u32[]{:S(2)}) collective-permute-start(bf16[256,1024]{1,0:T(8,128)(2,1)S(1)} %collective-permute-done.10.rest_8_.rest_1_), channel_id=1, source_target_pairs={{0,4},{1,5},{2,6},{3,7},{4,0},{5,1},{6,2},{7,3},{8,12},{9,13},{10,... | collective-permute-start | bytes 1572872 | tf_op jit(solution)/shard_map/late_shards_on/ppermute | solution.py:317
  51.8 3.7 %collective-permute-start.4 = (bf16[256,1024]{1,0:T(8,128)(2,1)}, bf16[256,1024]{1,0:T(8,128)(2,1)}, u32[]{:S(2)}, u32[]{:S(2)}) collective-permute-start(bf16[256,1024]{1,0:T(8,128)(2,1)} %collective-permute-done.2.refs_7_.rest_4_), channel_id=1, source_target_pairs={{0,3},{1,0},{2,1},{3,2},{4,7},{5,4},{6,5},{7,6},{8,11},{9,8},{10,9... | collective-permute-start | bytes 1572872 | tf_op jit(solution)/shard_map/shards_on/ppermute | solution.py:317
  55.6 1.0 copy.15.mask_ref
  56.5 2.0 %collective-permute-start.14 = (bf16[256,1024]{1,0:T(8,128)(2,1)S(1)}, bf16[256,1024]{1,0:T(8,128)(2,1)S(1)}, u32[]{:S(2)}, u32[]{:S(2)}) collective-permute-start(bf16[256,1024]{1,0:T(8,128)(2,1)S(1)} %slice.7), channel_id=1, source_target_pairs={{0,1},{1,2},{2,3},{3,0},{4,5},{5,6},{6,7},{7,4},{8,9},{9,10},{10,1... | collective-permute-start | bytes 1572872 | tf_op jit(solution)/shard_map/late_shards/ppermute | solution.py:317
  58.6 1.3 collective-permute-done.12.rest_9_.rest_4_
  59.9 8.0 %collective-permute-done.15.rest_5_ = bf16[256,1024]{1,0:T(8,128)(2,1)} collective-permute-done((bf16[256,1024]{1,0:T(8,128)(2,1)S(1)}, bf16[256,1024]{1,0:T(8,128)(2,1)}, u32[]{:S(2)}, u32[]{:S(2)}) %collective-permute-start.15) | collective-permute-done | bytes 524320 | tf_op jit(solution)/shard_map/late_shards_on/ppermute | solution.py:317
  67.9 2.2 %collective-permute-start.16 = (bf16[256,1024]{1,0:T(8,128)(2,1)}, bf16[256,1024]{1,0:T(8,128)(2,1)}, u32[]{:S(2)}, u32[]{:S(2)}) collective-permute-start(bf16[256,1024]{1,0:T(8,128)(2,1)} %collective-permute-done.15.rest_5_), channel_id=1, source_target_pairs={{0,3},{1,0},{2,1},{3,2},{4,7},{5,4},{6,5},{7,6},{8,11},{9,8},{10,9... | collective-permute-start | bytes 1572872 | tf_op jit(solution)/shard_map/late_shards_last/ppermute | solution.py:317
  70.2 11.5 %grads.2 = (bf16[272,1024]{1,0:T(8,128)(2,1)}, bf16[272,1024]{1,0:T(8,128)(2,1)}, bf16[272,1024]{1,0:T(8,128)(2,1)}, bf16[272,1024]{1,0:T(8,128)(2,1)}, bf16[272...) custom-call(bf16[768,2048]{1,0:T(8,128)(2,1)} %copy-done.3, ...), custom_call_target="tpu_custom_call" | custom-call | flops 6442450944 | bytes 13107200 | tf_op jit(solution)/shard_map/grads/pallas_call | solution.py:113
  81.7 1.8 collective-permute-start.21
  83.5 0.8 copy-done.28
  84.3 0.3 collective-permute-start.22
  84.6 0.8 copy-done.29
  85.4 5.2 %collective-permute-done.16.rest_6_ = bf16[256,1024]{1,0:T(8,128)(2,1)} collective-permute-done((bf16[256,1024]{1,0:T(8,128)(2,1)}, bf16[256,1024]{1,0:T(8,128)(2,1)}, u32[]{:S(2)}, u32[]{:S(2)}) %collective-permute-start.16) | collective-permute-done | bytes 524320 | tf_op jit(solution)/shard_map/late_shards_last/ppermute | solution.py:317
  90.7 0.9 copy-done.13
  91.6 2.3 %outer.1 = (f32[4,64,256]{2,1,0:T(8,128)}, f32[4,64,256]{2,1,0:T(8,128)}, bf16[4,128,128]{2,1,0:T(8,128)(2,1)S(1)}) custom-call(s32[4]{0:T(128)S(1)} %copy-done.15, bf16[4,128,128]{2,1,0:T(8,128)(2,1)S(1)} %bitcast.34, f32[4,64,256]{2,1,0:T(8,128)S(1)} %bitcast.32, f32[4,64,256]{2,1,0:T(8,128)S(1)} %bitcast.33), custom_call_target="tpu_custom_call" | custom-call | flops 524288 | bytes 2097152 | tf_op jit(solution)/shard_map/outer/pallas_call | solution.py:232
  93.8 3.3 %collective-permute-start.18 = (bf16[4,128,128]{2,1,0:T(8,128)(2,1)S(1)}, bf16[4,128,128]{2,1,0:T(8,128)(2,1)S(1)}, u32[]{:S(2)}, u32[]{:S(2)}) collective-permute-start(bf16[4,128,128]{2,1,0:T(8,128)(2,1)S(1)} %get-tuple-element.56), channel_id=1, source_target_pairs={{0,64},{8,72},{16,80},{24,88},{32,96},{40,104},{48,112},{56,120},{... | collective-permute-start | bytes 393224 | tf_op jit(solution)/shard_map/steps_along_z/ppermute | solution.py:421
  97.1 4.5 %collective-permute-start.19 = (bf16[4,128,128]{2,1,0:T(8,128)(2,1)S(1)}, bf16[4,128,128]{2,1,0:T(8,128)(2,1)S(1)}, u32[]{:S(2)}, u32[]{:S(2)}) collective-permute-start(bf16[4,128,128]{2,1,0:T(8,128)(2,1)S(1)} %get-tuple-element.56), channel_id=1, source_target_pairs={{0,128},{8,136},{16,144},{24,152},{32,160},{40,168},{48,176},{56,1... | collective-permute-start | bytes 393224 | tf_op jit(solution)/shard_map/steps_along_z/ppermute | solution.py:421
  101.6 2.7 %collective-permute-start.20 = (bf16[4,128,128]{2,1,0:T(8,128)(2,1)S(1)}, bf16[4,128,128]{2,1,0:T(8,128)(2,1)S(1)}, u32[]{:S(2)}, u32[]{:S(2)}) collective-permute-start(bf16[4,128,128]{2,1,0:T(8,128)(2,1)S(1)} %get-tuple-element.56), channel_id=1, source_target_pairs={{0,192},{8,200},{16,208},{24,216},{32,224},{40,232},{48,240},{56,2... | collective-permute-start | bytes 393224 | tf_op jit(solution)/shard_map/steps_along_z/ppermute | solution.py:421
  104.3 10.9 %grads.3 = (bf16[256,1024]{1,0:T(8,128)(2,1)}, bf16[256,1024]{1,0:T(8,128)(2,1)}, bf16[256,1024]{1,0:T(8,128)(2,1)}, bf16[256,1024]{1,0:T(8,128)(2,1)}, bf16[256...) custom-call(bf16[768,2048]{1,0:T(8,128)(2,1)} %copy-done.3, ...), custom_call_target="tpu_custom_call" | custom-call | flops 6442450944 | bytes 13107200 | tf_op jit(solution)/shard_map/grads/pallas_call | solution.py:113
  115.1 0.9 pad_maximum_fusion
  116.2 3.8 %collective-permute-start.23 = (bf16[256,1024]{1,0:T(8,128)(2,1)}, bf16[256,1024]{1,0:T(8,128)(2,1)S(1)}, u32[]{:S(2)}, u32[]{:S(2)}) collective-permute-start(bf16[256,1024]{1,0:T(8,128)(2,1)} %get-tuple-element.62), channel_id=1, source_target_pairs={{0,3},{1,0},{2,1},{3,2},{4,7},{5,4},{6,5},{7,6},{8,11},{9,8},{10,9... | collective-permute-start | bytes 1572872 | tf_op jit(solution)/shard_map/sum_near_other/ppermute | solution.py:363
  120.0 1.9 %collective-permute-start.32 = (bf16[272,1024]{1,0:T(8,128)(2,1)}, bf16[272,1024]{1,0:T(8,128)(2,1)S(1)}, u32[]{:S(2)}, u32[]{:S(2)}) collective-permute-start(bf16[272,1024]{1,0:T(8,128)(2,1)} %get-tuple-element.75), channel_id=1, source_target_pairs={{0,3},{1,0},{2,1},{3,2},{4,7},{5,4},{6,5},{7,6},{8,11},{9,8},{10,9... | collective-permute-start | bytes 1671176 | tf_op jit(solution)/shard_map/sum_far/ppermute | solution.py:363
  121.9 0.2 add_convert_fusion.1
  122.1 1.1 collective-permute-start.33
  123.2 0.2 add_convert_fusion.2
  123.4 1.1 collective-permute-start.31
  124.6 4.4 %collective-permute-done.26 = bf16[256,1024]{1,0:T(8,128)(2,1)S(1)} collective-permute-done((bf16[256,1024]{1,0:T(8,128)(2,1)}, bf16[256,1024]{1,0:T(8,128)(2,1)S(1)}, u32[]{:S(2)}, u32[]{:S(2)}) %collective-permute-start.26) | collective-permute-done | bytes 524320 | tf_op jit(solution)/shard_map/sum_far_other/ppermute | solution.py:363
  129.2 3.5 %collective-permute-done.23 = bf16[256,1024]{1,0:T(8,128)(2,1)S(1)} collective-permute-done((bf16[256,1024]{1,0:T(8,128)(2,1)}, bf16[256,1024]{1,0:T(8,128)(2,1)S(1)}, u32[]{:S(2)}, u32[]{:S(2)}) %collective-permute-start.23) | collective-permute-done | bytes 524320 | tf_op jit(solution)/shard_map/sum_near_other/ppermute | solution.py:363
  132.7 1.0 collective-permute-start.28
  133.7 1.0 add_convert_fusion.5
  134.7 5.0 %collective-permute-done.32 = bf16[272,1024]{1,0:T(8,128)(2,1)S(1)} collective-permute-done((bf16[272,1024]{1,0:T(8,128)(2,1)}, bf16[272,1024]{1,0:T(8,128)(2,1)S(1)}, u32[]{:S(2)}, u32[]{:S(2)}) %collective-permute-start.32) | collective-permute-done | bytes 557088 | tf_op jit(solution)/shard_map/sum_far/ppermute | solution.py:363
  139.6 1.7 collective-permute-start.30
  141.3 1.0 collective-permute-start.25
  142.3 0.3 add_convert_fusion
  142.7 2.1 %collective-permute-start.24 = (bf16[256,1024]{1,0:T(8,128)(2,1)}, bf16[256,1024]{1,0:T(8,128)(2,1)}, u32[]{:S(2)}, u32[]{:S(2)}) collective-permute-start(bf16[256,1024]{1,0:T(8,128)(2,1)} %get-tuple-element.63), channel_id=1, source_target_pairs={{0,3},{1,0},{2,1},{3,2},{4,7},{5,4},{6,5},{7,6},{8,11},{9,8},{10,9... | collective-permute-start | bytes 1572872 | tf_op jit(solution)/shard_map/sum_near/ppermute | solution.py:363
  144.7 16.0 %collective-permute-done.28 = bf16[256,1024]{1,0:T(8,128)(2,1)S(1)} collective-permute-done((bf16[256,1024]{1,0:T(8,128)(2,1)S(1)}, bf16[256,1024]{1,0:T(8,128)(2,1)S(1)}, u32[]{:S(2)}, u32[]{:S(2)}) %collective-permute-start.28) | collective-permute-done | bytes 524320 | tf_op jit(solution)/shard_map/sum_cross_side/ppermute | solution.py:363
  160.8 0.2 collective-permute-start.34
  161.0 1.1 add_convert_fusion.3
  162.1 1.8 collective-permute-start.29
  163.9 6.4 %collective-permute-done.34.refs_3_ = bf16[272,1024]{1,0:T(8,128)(2,1)S(1)} collective-permute-done((bf16[272,1024]{1,0:T(8,128)(2,1)S(1)}, bf16[272,1024]{1,0:T(8,128)(2,1)S(1)}, u32[]{:S(2)}, u32[]{:S(2)}) %collective-permute-start.34) | collective-permute-done | bytes 557088 | tf_op jit(solution)/shard_map/sum_side/ppermute | solution.py:363
  170.3 2.2 %copy-done.1 = bf16[32,4,128,128]{3,2,1,0:T(8,128)(2,1)S(1)} copy-done((bf16[32,4,128,128]{3,2,1,0:T(8,128)(2,1)S(1)}, bf16[32,4,128,128]{3,2,1,0:T(8,128)(2,1)}, u32[]{:S(2)}) %copy-start.1) | copy-done | bytes 4194328
  172.5 2.2 %final.2 = (bf16[256,2048]{1,0:T(8,128)(2,1)}, f32[8,128]{1,0:T(8,128)S(1)}) custom-call(s32[2]{0:T(128)S(1)} %pad_add_fusion.place_ref, s32[32]{0:T(128)S(1)} %copy-done.14, bf16[256,2048]{1,0:T(8,128)(2,1)S(1)} %bitcast.29, bf16[8,4,4,128,128]{4,3,2,1,0:T(8,128)(2,1)S(1)} %bitcast.23, bf16[272,1024]{1,0:T(8,128)(2,1)S(1)} %copy-done.7, ...), custom_call_target="tpu_custom_call" | custom-call | flops 2097152 | bytes 3670016 | tf_op jit(solution)/shard_map/final/pallas_call | solution.py:291
  174.9 3.1 %final.3 = bf16[256,2048]{1,0:T(8,128)(2,1)} custom-call(s32[2]{0:T(128)S(1)} %pad_add_fusion.place_ref, s32[32]{0:T(128)S(1)} %copy-done.14, bf16[256,2048]{1,0:T(8,128)(2,1)S(1)} %bitcast.30, bf16[8,4,4,128,128]{4,3,2,1,0:T(8,128)(2,1)S(1)} %bitcast.24, bf16[256,1024]{1,0:T(8,128)(2,1)S(1)} %copy-done.10, ...), custom_call_target="tpu_custom_call", output_to_operand_aliasing={{}: (9, {})} | custom-call | flops 2097152 | bytes 3670016 | tf_op jit(solution)/shard_map/final/pallas_call | solution.py:291
  (95 shorter events, 1.0 us)
Async XLA Ops:
  7.2 6.8 %copy-start = (bf16[1,256,2048]{2,1,0:T(8,128)(2,1)S(1)}, bf16[1,256,2048]{2,1,0:T(8,128)(2,1)}, u32[]{:S(2)}) copy-start(bf16[1,256,2048]{2,1,0:T(8,128)(2,1)} %param.13) | copy-start | bytes 3145732
  7.2 83.5 %reduce-scatter.2.cloned.1.call-start = ((), (), s32[]{:S(2)}) async-start(), calls=%async_computation.1 | async-start | bytes 655360 | tf_op jit(solution)/shard_map/reduce_scatter | solution.py:410
  9.2 14.3 %collective-permute-start = (bf16[256,1024]{1,0:T(8,128)(2,1)}, bf16[256,1024]{1,0:T(8,128)(2,1)S(1)}, u32[]{:S(2)}, u32[]{:S(2)}) collective-permute-start(bf16[256,1024]{1,0:T(8,128)(2,1)} %slice.8), channel_id=1, source_target_pairs={{0,3},{1,0},{2,1},{3,2},{4,7},{5,4},{6,5},{7,6},{8,11},{9,8},{10,9... | collective-permute-start | bytes 1572872 | tf_op jit(solution)/shard_map/shards/ppermute | solution.py:317
  11.9 15.0 %collective-permute-start.1 = (bf16[256,1024]{1,0:T(8,128)(2,1)}, bf16[256,1024]{1,0:T(8,128)(2,1)}, u32[]{:S(2)}, u32[]{:S(2)}) collective-permute-start(bf16[256,1024]{1,0:T(8,128)(2,1)} %slice.8), channel_id=1, source_target_pairs={{0,1},{1,2},{2,3},{3,0},{4,5},{5,6},{6,7},{7,4},{8,9},{9,10},{10,1... | collective-permute-start | bytes 1572872 | tf_op jit(solution)/shard_map/shards/ppermute | solution.py:317
  11.9 15.0 %collective-permute-start.2 = (bf16[256,1024]{1,0:T(8,128)(2,1)}, bf16[256,1024]{1,0:T(8,128)(2,1)}, u32[]{:S(2)}, u32[]{:S(2)}) collective-permute-start(bf16[256,1024]{1,0:T(8,128)(2,1)} %slice.8), channel_id=1, source_target_pairs={{0,4},{1,5},{2,6},{3,7},{4,0},{5,1},{6,2},{7,3},{8,12},{9,13},{10,... | collective-permute-start | bytes 1572872 | tf_op jit(solution)/shard_map/shards/ppermute | solution.py:317
  13.9 11.1 %copy-start.6 = (bf16[1,768,2048]{2,1,0:T(8,128)(2,1)S(1)}, bf16[1,768,2048]{2,1,0:T(8,128)(2,1)}, u32[]{:S(2)}) copy-start(bf16[1,768,2048]{2,1,0:T(8,128)(2,1)} %param.9) | copy-start | bytes 9437188
  15.3 14.7 %collective-permute-start.7 = (bf16[4,256,128]{2,1,0:T(8,128)(2,1)S(1)}, bf16[4,256,128]{2,1,0:T(8,128)(2,1)S(1)}, u32[]{:S(2)}, u32[]{:S(2)}) collective-permute-start(bf16[4,256,128]{2,1,0:T(8,128)(2,1)S(1)} %get-tuple-element.45), channel_id=1, source_target_pairs={{0,16},{8,24},{16,32},{24,40},{32,48},{40,56},{48,0},{56,8},{64,80... | collective-permute-start | bytes 786440 | tf_op jit(solution)/shard_map/ppermute | solution.py:404
  15.6 14.4 %collective-permute-start.8 = (bf16[4,256,128]{2,1,0:T(8,128)(2,1)S(1)}, bf16[4,256,128]{2,1,0:T(8,128)(2,1)S(1)}, u32[]{:S(2)}, u32[]{:S(2)}) collective-permute-start(bf16[4,256,128]{2,1,0:T(8,128)(2,1)S(1)} %get-tuple-element.46), channel_id=1, source_target_pairs={{0,32},{8,40},{16,48},{24,56},{32,0},{40,8},{48,16},{56,24},{64,96... | collective-permute-start | bytes 786440 | tf_op jit(solution)/shard_map/ppermute | solution.py:404
  24.2 8.4 %collective-permute-start.9 = (bf16[4,256,128]{2,1,0:T(8,128)(2,1)S(1)}, bf16[4,256,128]{2,1,0:T(8,128)(2,1)S(1)}, u32[]{:S(2)}, u32[]{:S(2)}) collective-permute-start(bf16[4,256,128]{2,1,0:T(8,128)(2,1)S(1)} %get-tuple-element.47), channel_id=1, source_target_pairs={{0,48},{8,56},{16,0},{24,8},{32,16},{40,24},{48,32},{56,40},{64,11... | collective-permute-start | bytes 786440 | tf_op jit(solution)/shard_map/ppermute | solution.py:404
  25.0 7.6 %copy-start.9 = (bf16[256,1024]{1,0:T(8,128)(2,1)S(1)}, bf16[256,1024]{1,0:T(8,128)(2,1)}, u32[]{:S(2)}) copy-start(bf16[256,1024]{1,0:T(8,128)(2,1)} %copy-done.8) | copy-start | bytes 1572868
  25.0 7.6 %copy-start.14 = (s32[32]{0:T(128)S(1)}, s32[32]{0:T(128)}, u32[]{:S(2)}) copy-start(s32[32]{0:T(128)} %module_ref.5) | copy-start | bytes 388
  26.9 7.3 %copy-start.3 = (bf16[768,2048]{1,0:T(8,128)(2,1)}, bf16[768,2048]{1,0:T(8,128)(2,1)S(1)}, u32[]{:S(2)}) copy-start(bf16[768,2048]{1,0:T(8,128)(2,1)S(1)} %norm.1.refs_4_.n_ref) | copy-start | bytes 9437188
  27.0 13.1 %collective-permute-start.5 = (bf16[256,1024]{1,0:T(8,128)(2,1)}, bf16[256,1024]{1,0:T(8,128)(2,1)}, u32[]{:S(2)}, u32[]{:S(2)}) collective-permute-start(bf16[256,1024]{1,0:T(8,128)(2,1)} %collective-permute-done.1.refs_5_.rest_3_), channel_id=1, source_target_pairs={{0,4},{1,5},{2,6},{3,7},{4,0},{5,1},{6,2},{7,3},{8,12},{9,13},{10,... | collective-permute-start | bytes 1572872 | tf_op jit(solution)/shard_map/shards_on/ppermute | solution.py:317
  29.0 14.3 %collective-permute-start.3 = (bf16[256,1024]{1,0:T(8,128)(2,1)}, bf16[256,1024]{1,0:T(8,128)(2,1)S(1)}, u32[]{:S(2)}, u32[]{:S(2)}) collective-permute-start(bf16[256,1024]{1,0:T(8,128)(2,1)} %collective-permute-done.1.refs_5_.rest_3_), channel_id=1, source_target_pairs={{0,1},{1,2},{2,3},{3,0},{4,5},{5,6},{6,7},{7,4},{8,9},{9,10},{10,1... | collective-permute-start | bytes 1572872 | tf_op jit(solution)/shard_map/shards_on/ppermute | solution.py:317
  32.6 1.7 copy-start.4
  34.2 9.1 %collective-permute-start.11 = (bf16[4,4,128,128]{3,2,1,0:T(8,128)(2,1)S(1)}, bf16[4,4,128,128]{3,2,1,0:T(8,128)(2,1)S(1)}, u32[]{:S(2)}, u32[]{:S(2)}) collective-permute-start(bf16[4,4,128,128]{3,2,1,0:T(8,128)(2,1)S(1)} %get-tuple-element.51), channel_id=1, source_target_pairs={{0,8},{8,0},{16,24},{24,16},{32,40},{40,32},{48,56},{56,48},{64,72... | collective-permute-start | bytes 1572872 | tf_op jit(solution)/shard_map/ppermute | solution.py:407
  34.4 21.2 %copy-start.22 = (s32[1,768]{1,0:T(1,128)S(1)}, s32[1,768]{1,0:T(1,128)}, u32[]{:S(2)}) copy-start(s32[1,768]{1,0:T(1,128)} %param.11) | copy-start | bytes 9220
  34.4 15.5 %collective-permute-start.10 = (bf16[256,1024]{1,0:T(8,128)(2,1)S(1)}, bf16[256,1024]{1,0:T(8,128)(2,1)S(1)}, u32[]{:S(2)}, u32[]{:S(2)}) collective-permute-start(bf16[256,1024]{1,0:T(8,128)(2,1)S(1)} %slice.7), channel_id=1, source_target_pairs={{0,3},{1,0},{2,1},{3,2},{4,7},{5,4},{6,5},{7,6},{8,11},{9,8},{10,9... | collective-permute-start | bytes 1572872 | tf_op jit(solution)/shard_map/late_shards/ppermute | solution.py:317
  43.3 13.3 %collective-permute-start.6 = (bf16[256,1024]{1,0:T(8,128)(2,1)}, bf16[256,1024]{1,0:T(8,128)(2,1)S(1)}, u32[]{:S(2)}, u32[]{:S(2)}) collective-permute-start(bf16[256,1024]{1,0:T(8,128)(2,1)} %collective-permute-done.5.rest_7_), channel_id=1, source_target_pairs={{0,1},{1,2},{2,3},{3,0},{4,5},{5,6},{6,7},{7,4},{8,9},{9,10},{10,1... | collective-permute-start | bytes 1572872 | tf_op jit(solution)/shard_map/shards_last/ppermute | solution.py:317
  45.0 14.9 %collective-permute-start.12 = (bf16[256,1024]{1,0:T(8,128)(2,1)S(1)}, bf16[256,1024]{1,0:T(8,128)(2,1)S(1)}, u32[]{:S(2)}, u32[]{:S(2)}) collective-permute-start(bf16[256,1024]{1,0:T(8,128)(2,1)S(1)} %slice.7), channel_id=1, source_target_pairs={{0,4},{1,5},{2,6},{3,7},{4,0},{5,1},{6,2},{7,3},{8,12},{9,13},{10,... | collective-permute-start | bytes 1572872 | tf_op jit(solution)/shard_map/late_shards/ppermute | solution.py:317
  49.9 20.3 %copy-start.24 = (bf16[256,1024]{1,0:T(8,128)(2,1)}, bf16[256,1024]{1,0:T(8,128)(2,1)S(1)}, u32[]{:S(2)}) copy-start(bf16[256,1024]{1,0:T(8,128)(2,1)S(1)} %collective-permute-done.10.rest_8_.rest_1_) | copy-start | bytes 1572868
  49.9 18.1 %collective-permute-start.15 = (bf16[256,1024]{1,0:T(8,128)(2,1)S(1)}, bf16[256,1024]{1,0:T(8,128)(2,1)}, u32[]{:S(2)}, u32[]{:S(2)}) collective-permute-start(bf16[256,1024]{1,0:T(8,128)(2,1)S(1)} %collective-permute-done.10.rest_8_.rest_1_), channel_id=1, source_target_pairs={{0,4},{1,5},{2,6},{3,7},{4,0},{5,1},{6,2},{7,3},{8,12},{9,13},{10,... | collective-permute-start | bytes 1572872 | tf_op jit(solution)/shard_map/late_shards_on/ppermute | solution.py:317
  51.8 18.3 %collective-permute-start.4 = (bf16[256,1024]{1,0:T(8,128)(2,1)}, bf16[256,1024]{1,0:T(8,128)(2,1)}, u32[]{:S(2)}, u32[]{:S(2)}) collective-permute-start(bf16[256,1024]{1,0:T(8,128)(2,1)} %collective-permute-done.2.refs_7_.rest_4_), channel_id=1, source_target_pairs={{0,3},{1,0},{2,1},{3,2},{4,7},{5,4},{6,5},{7,6},{8,11},{9,8},{10,9... | collective-permute-start | bytes 1572872 | tf_op jit(solution)/shard_map/shards_on/ppermute | solution.py:317
  55.5 114.8 %all-gather.3.cloned.1.call-start = ((), (), s32[]{:S(2)}) async-start(), calls=%async_computation.2 | async-start | bytes 4718592 | tf_op jit(solution)/shard_map/all_gather | solution.py:426
  56.5 27.0 %collective-permute-start.13 = (bf16[256,1024]{1,0:T(8,128)(2,1)S(1)}, bf16[256,1024]{1,0:T(8,128)(2,1)S(1)}, u32[]{:S(2)}, u32[]{:S(2)}) collective-permute-start(bf16[256,1024]{1,0:T(8,128)(2,1)S(1)} %collective-permute-done.10.rest_8_.rest_1_), channel_id=1, source_target_pairs={{0,3},{1,0},{2,1},{3,2},{4,7},{5,4},{6,5},{7,6},{8,11},{9,8},{10,9... | collective-permute-start | bytes 1572872 | tf_op jit(solution)/shard_map/late_shards_on/ppermute | solution.py:317
  56.5 13.6 %copy-start.30 = (bf16[256,1024]{1,0:T(8,128)(2,1)}, bf16[256,1024]{1,0:T(8,128)(2,1)S(1)}, u32[]{:S(2)}) copy-start(bf16[256,1024]{1,0:T(8,128)(2,1)S(1)} %collective-permute-done.6.rest_6_) | copy-start | bytes 1572868
  56.5 28.1 %collective-permute-start.14 = (bf16[256,1024]{1,0:T(8,128)(2,1)S(1)}, bf16[256,1024]{1,0:T(8,128)(2,1)S(1)}, u32[]{:S(2)}, u32[]{:S(2)}) collective-permute-start(bf16[256,1024]{1,0:T(8,128)(2,1)S(1)} %slice.7), channel_id=1, source_target_pairs={{0,1},{1,2},{2,3},{3,0},{4,5},{5,6},{6,7},{7,4},{8,9},{9,10},{10,1... | collective-permute-start | bytes 1572872 | tf_op jit(solution)/shard_map/late_shards/ppermute | solution.py:317
  59.9 10.3 %copy-start.25 = (bf16[256,1024]{1,0:T(8,128)(2,1)}, bf16[256,1024]{1,0:T(8,128)(2,1)S(1)}, u32[]{:S(2)}) copy-start(bf16[256,1024]{1,0:T(8,128)(2,1)S(1)} %collective-permute-done.12.rest_9_.rest_4_) | copy-start | bytes 1572868
  59.9 24.7 %collective-permute-start.17 = (bf16[256,1024]{1,0:T(8,128)(2,1)S(1)}, bf16[256,1024]{1,0:T(8,128)(2,1)}, u32[]{:S(2)}, u32[]{:S(2)}) collective-permute-start(bf16[256,1024]{1,0:T(8,128)(2,1)S(1)} %collective-permute-done.12.rest_9_.rest_4_), channel_id=1, source_target_pairs={{0,1},{1,2},{2,3},{3,0},{4,5},{5,6},{6,7},{7,4},{8,9},{9,10},{10,1... | collective-permute-start | bytes 1572872 | tf_op jit(solution)/shard_map/late_shards_on/ppermute | solution.py:317
  67.9 22.7 %collective-permute-start.16 = (bf16[256,1024]{1,0:T(8,128)(2,1)}, bf16[256,1024]{1,0:T(8,128)(2,1)}, u32[]{:S(2)}, u32[]{:S(2)}) collective-permute-start(bf16[256,1024]{1,0:T(8,128)(2,1)} %collective-permute-done.15.rest_5_), channel_id=1, source_target_pairs={{0,3},{1,0},{2,1},{3,2},{4,7},{5,4},{6,5},{7,6},{8,11},{9,8},{10,9... | collective-permute-start | bytes 1572872 | tf_op jit(solution)/shard_map/late_shards_last/ppermute | solution.py:317
  70.1 20.5 %copy-start.11 = (f32[4,256,64]{1,2,0:T(8,128)S(1)}, f32[4,256,64]{1,2,0:T(8,128)}, u32[]{:S(2)}) copy-start(f32[4,256,64]{1,2,0:T(8,128)} %param.14) | copy-start | bytes 786436
  70.2 20.5 %copy-start.12 = (f32[4,256,64]{1,2,0:T(8,128)S(1)}, f32[4,256,64]{1,2,0:T(8,128)}, u32[]{:S(2)}) copy-start(f32[4,256,64]{1,2,0:T(8,128)} %param.15) | copy-start | bytes 786436
  70.2 20.5 %copy-start.15 = (s32[4]{0:T(128)S(1)}, s32[4]{0:T(128)}, u32[]{:S(2)}) copy-start(s32[4]{0:T(128)} %count_ref) | copy-start | bytes 52
  81.7 34.4 %collective-permute-start.21 = (bf16[272,1024]{1,0:T(8,128)(2,1)}, bf16[272,1024]{1,0:T(8,128)(2,1)S(1)}, u32[]{:S(2)}, u32[]{:S(2)}) collective-permute-start(bf16[272,1024]{1,0:T(8,128)(2,1)} %get-tuple-element.58), channel_id=1, source_target_pairs={{0,3},{1,0},{2,1},{3,2},{4,7},{5,4},{6,5},{7,6},{8,11},{9,8},{10,9... | collective-permute-start | bytes 1671176 | tf_op jit(solution)/shard_map/sum_far_other/ppermute | solution.py:363
  84.3 31.8 %collective-permute-start.22 = (bf16[272,1024]{1,0:T(8,128)(2,1)}, bf16[272,1024]{1,0:T(8,128)(2,1)S(1)}, u32[]{:S(2)}, u32[]{:S(2)}) collective-permute-start(bf16[272,1024]{1,0:T(8,128)(2,1)} %get-tuple-element.59), channel_id=1, source_target_pairs={{0,1},{1,2},{2,3},{3,0},{4,5},{5,6},{6,7},{7,4},{8,9},{9,10},{10,1... | collective-permute-start | bytes 1671176 | tf_op jit(solution)/shard_map/sum_near_other/ppermute | solution.py:363
  90.7 0.9 copy-start.13
  93.8 21.3 %collective-permute-start.18 = (bf16[4,128,128]{2,1,0:T(8,128)(2,1)S(1)}, bf16[4,128,128]{2,1,0:T(8,128)(2,1)S(1)}, u32[]{:S(2)}, u32[]{:S(2)}) collective-permute-start(bf16[4,128,128]{2,1,0:T(8,128)(2,1)S(1)} %get-tuple-element.56), channel_id=1, source_target_pairs={{0,64},{8,72},{16,80},{24,88},{32,96},{40,104},{48,112},{56,120},{... | collective-permute-start | bytes 393224 | tf_op jit(solution)/shard_map/steps_along_z/ppermute | solution.py:421
  97.1 18.0 %collective-permute-start.19 = (bf16[4,128,128]{2,1,0:T(8,128)(2,1)S(1)}, bf16[4,128,128]{2,1,0:T(8,128)(2,1)S(1)}, u32[]{:S(2)}, u32[]{:S(2)}) collective-permute-start(bf16[4,128,128]{2,1,0:T(8,128)(2,1)S(1)} %get-tuple-element.56), channel_id=1, source_target_pairs={{0,128},{8,136},{16,144},{24,152},{32,160},{40,168},{48,176},{56,1... | collective-permute-start | bytes 393224 | tf_op jit(solution)/shard_map/steps_along_z/ppermute | solution.py:421
  101.6 13.6 %collective-permute-start.20 = (bf16[4,128,128]{2,1,0:T(8,128)(2,1)S(1)}, bf16[4,128,128]{2,1,0:T(8,128)(2,1)S(1)}, u32[]{:S(2)}, u32[]{:S(2)}) collective-permute-start(bf16[4,128,128]{2,1,0:T(8,128)(2,1)S(1)} %get-tuple-element.56), channel_id=1, source_target_pairs={{0,192},{8,200},{16,208},{24,216},{32,224},{40,232},{48,240},{56,2... | collective-permute-start | bytes 393224 | tf_op jit(solution)/shard_map/steps_along_z/ppermute | solution.py:421
  115.1 6.8 %copy-start.18 = (bf16[272,1024]{1,0:T(8,128)(2,1)S(1)}, bf16[272,1024]{1,0:T(8,128)(2,1)}, u32[]{:S(2)}) copy-start(bf16[272,1024]{1,0:T(8,128)(2,1)} %get-tuple-element.76) | copy-start | bytes 1671172
  116.1 7.2 %copy-start.17 = (bf16[272,1024]{1,0:T(8,128)(2,1)S(1)}, bf16[272,1024]{1,0:T(8,128)(2,1)}, u32[]{:S(2)}) copy-start(bf16[272,1024]{1,0:T(8,128)(2,1)} %get-tuple-element.72) | copy-start | bytes 1671172
  116.1 12.8 %collective-permute-start.26 = (bf16[256,1024]{1,0:T(8,128)(2,1)}, bf16[256,1024]{1,0:T(8,128)(2,1)S(1)}, u32[]{:S(2)}, u32[]{:S(2)}) collective-permute-start(bf16[256,1024]{1,0:T(8,128)(2,1)} %get-tuple-element.67), channel_id=1, source_target_pairs={{0,1},{1,2},{2,3},{3,0},{4,5},{5,6},{6,7},{7,4},{8,9},{9,10},{10,1... | collective-permute-start | bytes 1572872 | tf_op jit(solution)/shard_map/sum_far_other/ppermute | solution.py:363
  116.2 16.5 %collective-permute-start.23 = (bf16[256,1024]{1,0:T(8,128)(2,1)}, bf16[256,1024]{1,0:T(8,128)(2,1)S(1)}, u32[]{:S(2)}, u32[]{:S(2)}) collective-permute-start(bf16[256,1024]{1,0:T(8,128)(2,1)} %get-tuple-element.62), channel_id=1, source_target_pairs={{0,3},{1,0},{2,1},{3,2},{4,7},{5,4},{6,5},{7,6},{8,11},{9,8},{10,9... | collective-permute-start | bytes 1572872 | tf_op jit(solution)/shard_map/sum_near_other/ppermute | solution.py:363
  120.0 19.7 %collective-permute-start.32 = (bf16[272,1024]{1,0:T(8,128)(2,1)}, bf16[272,1024]{1,0:T(8,128)(2,1)S(1)}, u32[]{:S(2)}, u32[]{:S(2)}) collective-permute-start(bf16[272,1024]{1,0:T(8,128)(2,1)} %get-tuple-element.75), channel_id=1, source_target_pairs={{0,3},{1,0},{2,1},{3,2},{4,7},{5,4},{6,5},{7,6},{8,11},{9,8},{10,9... | collective-permute-start | bytes 1671176 | tf_op jit(solution)/shard_map/sum_far/ppermute | solution.py:363
  122.1 6.8 %copy-start.27 = (bf16[256,1024]{1,0:T(8,128)(2,1)S(1)}, bf16[256,1024]{1,0:T(8,128)(2,1)}, u32[]{:S(2)}) copy-start(bf16[256,1024]{1,0:T(8,128)(2,1)} %get-tuple-element.68) | copy-start | bytes 1572868
  122.1 6.8 %copy-start.20 = (bf16[256,1024]{1,0:T(8,128)(2,1)S(1)}, bf16[256,1024]{1,0:T(8,128)(2,1)}, u32[]{:S(2)}) copy-start(bf16[256,1024]{1,0:T(8,128)(2,1)} %get-tuple-element.69) | copy-start | bytes 1572868
  122.1 19.2 %collective-permute-start.33 = (bf16[272,1024]{1,0:T(8,128)(2,1)S(1)}, bf16[272,1024]{1,0:T(8,128)(2,1)S(1)}, u32[]{:S(2)}, u32[]{:S(2)}) collective-permute-start(bf16[272,1024]{1,0:T(8,128)(2,1)S(1)} %add_convert_fusion.1), channel_id=1, source_target_pairs={{0,4},{1,5},{2,6},{3,7},{4,0},{5,1},{6,2},{7,3},{8,12},{9,13},{10,... | collective-permute-start | bytes 1671176 | tf_op jit(solution)/shard_map/sum_cross_side/ppermute | solution.py:363
  123.4 10.2 %copy-start.19 = (bf16[256,1024]{1,0:T(8,128)(2,1)S(1)}, bf16[256,1024]{1,0:T(8,128)(2,1)}, u32[]{:S(2)}) copy-start(bf16[256,1024]{1,0:T(8,128)(2,1)} %get-tuple-element.64) | copy-start | bytes 1572868
  123.4 38.7 %collective-permute-start.31 = (bf16[272,1024]{1,0:T(8,128)(2,1)S(1)}, bf16[272,1024]{1,0:T(8,128)(2,1)S(1)}, u32[]{:S(2)}, u32[]{:S(2)}) collective-permute-start(bf16[272,1024]{1,0:T(8,128)(2,1)S(1)} %add_convert_fusion.2), channel_id=1, source_target_pairs={{0,4},{1,5},{2,6},{3,7},{4,0},{5,1},{6,2},{7,3},{8,12},{9,13},{10,... | collective-permute-start | bytes 1671176 | tf_op jit(solution)/shard_map/sum_cross/ppermute | solution.py:363
  128.9 13.7 %collective-permute-start.27 = (bf16[256,1024]{1,0:T(8,128)(2,1)S(1)}, bf16[256,1024]{1,0:T(8,128)(2,1)S(1)}, u32[]{:S(2)}, u32[]{:S(2)}) collective-permute-start(bf16[256,1024]{1,0:T(8,128)(2,1)S(1)} %copy-done.27), channel_id=1, source_target_pairs={{0,1},{1,2},{2,3},{3,0},{4,5},{5,6},{6,7},{7,4},{8,9},{9,10},{10,1... | collective-permute-start | bytes 1572872 | tf_op jit(solution)/shard_map/sum_far/ppermute | solution.py:363
  129.2 10.5 %copy-start.23 = (bf16[272,1024]{1,0:T(8,128)(2,1)S(1)}, bf16[272,1024]{1,0:T(8,128)(2,1)}, u32[]{:S(2)}) copy-start(bf16[272,1024]{1,0:T(8,128)(2,1)} %get-tuple-element.71) | copy-start | bytes 1671172
  129.2 13.2 %copy-start.16 = (bf16[272,1024]{1,0:T(8,128)(2,1)S(1)}, bf16[272,1024]{1,0:T(8,128)(2,1)}, u32[]{:S(2)}) copy-start(bf16[272,1024]{1,0:T(8,128)(2,1)} %get-tuple-element.73) | copy-start | bytes 1671172
  132.7 28.1 %collective-permute-start.28 = (bf16[256,1024]{1,0:T(8,128)(2,1)S(1)}, bf16[256,1024]{1,0:T(8,128)(2,1)S(1)}, u32[]{:S(2)}, u32[]{:S(2)}) collective-permute-start(bf16[256,1024]{1,0:T(8,128)(2,1)S(1)} %add_convert_fusion.4), channel_id=1, source_target_pairs={{0,4},{1,5},{2,6},{3,7},{4,0},{5,1},{6,2},{7,3},{8,12},{9,13},{10,... | collective-permute-start | bytes 1572872 | tf_op jit(solution)/shard_map/sum_cross_side/ppermute | solution.py:363
  139.6 24.3 %collective-permute-start.30 = (bf16[272,1024]{1,0:T(8,128)(2,1)S(1)}, bf16[272,1024]{1,0:T(8,128)(2,1)S(1)}, u32[]{:S(2)}, u32[]{:S(2)}) collective-permute-start(bf16[272,1024]{1,0:T(8,128)(2,1)S(1)} %copy-done.23), channel_id=1, source_target_pairs={{0,1},{1,2},{2,3},{3,0},{4,5},{5,6},{6,7},{7,4},{8,9},{9,10},{10,1... | collective-permute-start | bytes 1671176 | tf_op jit(solution)/shard_map/sum_near/ppermute | solution.py:363
  141.3 33.4 %collective-permute-start.25 = (bf16[256,1024]{1,0:T(8,128)(2,1)}, bf16[256,1024]{1,0:T(8,128)(2,1)}, u32[]{:S(2)}, u32[]{:S(2)}) collective-permute-start(bf16[256,1024]{1,0:T(8,128)(2,1)} %add_convert_fusion.5), channel_id=1, source_target_pairs={{0,4},{1,5},{2,6},{3,7},{4,0},{5,1},{6,2},{7,3},{8,12},{9,13},{10,... | collective-permute-start | bytes 1572872 | tf_op jit(solution)/shard_map/sum_cross/ppermute | solution.py:363
  142.3 18.7 %copy-start.21 = (bf16[256,1024]{1,0:T(8,128)(2,1)S(1)}, bf16[256,1024]{1,0:T(8,128)(2,1)}, u32[]{:S(2)}) copy-start(bf16[256,1024]{1,0:T(8,128)(2,1)} %get-tuple-element.65) | copy-start | bytes 1572868
  142.6 27.7 %copy-start.5 = (bf16[1,256,2048]{2,1,0:T(8,128)(2,1)S(1)}, bf16[1,256,2048]{2,1,0:T(8,128)(2,1)}, u32[]{:S(2)}) copy-start(bf16[1,256,2048]{2,1,0:T(8,128)(2,1)} %param.12) | copy-start | bytes 3145732
  142.6 27.7 %copy-start.7 = (bf16[272,1024]{1,0:T(8,128)(2,1)S(1)}, bf16[272,1024]{1,0:T(8,128)(2,1)}, u32[]{:S(2)}) copy-start(bf16[272,1024]{1,0:T(8,128)(2,1)} %get-tuple-element.53.refs_0_) | copy-start | bytes 1671172
  142.7 32.1 %collective-permute-start.24 = (bf16[256,1024]{1,0:T(8,128)(2,1)}, bf16[256,1024]{1,0:T(8,128)(2,1)}, u32[]{:S(2)}, u32[]{:S(2)}) collective-permute-start(bf16[256,1024]{1,0:T(8,128)(2,1)} %get-tuple-element.63), channel_id=1, source_target_pairs={{0,3},{1,0},{2,1},{3,2},{4,7},{5,4},{6,5},{7,6},{8,11},{9,8},{10,9... | collective-permute-start | bytes 1572872 | tf_op jit(solution)/shard_map/sum_near/ppermute | solution.py:363
  160.8 9.5 %collective-permute-start.34 = (bf16[272,1024]{1,0:T(8,128)(2,1)S(1)}, bf16[272,1024]{1,0:T(8,128)(2,1)S(1)}, u32[]{:S(2)}, u32[]{:S(2)}) collective-permute-start(bf16[272,1024]{1,0:T(8,128)(2,1)S(1)} %add_convert_fusion), channel_id=1, source_target_pairs={{0,3},{1,0},{2,1},{3,2},{4,7},{5,4},{6,5},{7,6},{8,11},{9,8},{10,9... | collective-permute-start | bytes 1671176 | tf_op jit(solution)/shard_map/sum_side/ppermute | solution.py:363
  162.1 12.6 %collective-permute-start.29 = (bf16[256,1024]{1,0:T(8,128)(2,1)}, bf16[256,1024]{1,0:T(8,128)(2,1)}, u32[]{:S(2)}, u32[]{:S(2)}) collective-permute-start(bf16[256,1024]{1,0:T(8,128)(2,1)} %add_convert_fusion.3), channel_id=1, source_target_pairs={{0,1},{1,2},{2,3},{3,0},{4,5},{5,6},{6,7},{7,4},{8,9},{9,10},{10,1... | collective-permute-start | bytes 1572872 | tf_op jit(solution)/shard_map/sum_side/ppermute | solution.py:363
  170.3 2.2 %copy-start.1 = (bf16[32,4,128,128]{3,2,1,0:T(8,128)(2,1)S(1)}, bf16[32,4,128,128]{3,2,1,0:T(8,128)(2,1)}, u32[]{:S(2)}) copy-start(bf16[32,4,128,128]{3,2,1,0:T(8,128)(2,1)} %all-gather.3.cloned.1.call-done) | copy-start | bytes 12582916
  172.5 2.3 %copy-start.2 = (bf16[32,4,128,128]{3,2,1,0:T(8,128)(2,1)S(1)}, bf16[32,4,128,128]{3,2,1,0:T(8,128)(2,1)}, u32[]{:S(2)}) copy-start(bf16[32,4,128,128]{3,2,1,0:T(8,128)(2,1)} %all-gather.3.cloned.1.call-done) | copy-start | bytes 12582916
  172.5 2.4 %copy-start.10 = (bf16[256,1024]{1,0:T(8,128)(2,1)S(1)}, bf16[256,1024]{1,0:T(8,128)(2,1)}, u32[]{:S(2)}) copy-start(bf16[256,1024]{1,0:T(8,128)(2,1)} %get-tuple-element.57.refs_0_) | copy-start | bytes 1572868
  (4 other events, 3.2 us)
Sparse Core Ops, SparseCore 0:
  55.6 27.3 reduce-scatter.1
  116.2 29.8 all-gather.2

commit v3 on v2

--- a/solution.py
+++ b/solution.py
@@ -334,7 +334,7 @@
         other_right = shift(after(other, left, right), down)
         other_left = shift(after(left, right, other), across)
     with jax.named_scope("shards_last"):
-        other_far = shift(after(other_left, far), up)
+        other_far = shift(after(other_left, far, other_right), up)
     return by_offset(1, left, right, far, other, other_left, other_right, other_far), begun, other_left, other_far
 
 
@@ -401,6 +401,7 @@
     normed = norm(place, inputs[0])
 
     dealt = deal(place, delta)
+    dealt = [dealt[0], dealt[1], after(dealt[2], normed), dealt[3]]
     dealt = [dealt[0]] + [lax.ppermute(dealt[k], "path", along_y(k)) for k in range(1, Y)]
     late = after(weights, *begun, *dealt[1:])[:, width:]
     mine, theirs = place_sums(place, module_of_path, dealt, modules, [normed, *begun])

time: 185 us -> 179 us (0.968)
  waiting for transfers between devices: 67.4 us -> 60.2 us
    ppermute x14, waiting for transfers between devices: 29.5 us -> 24.7 us  [shift(): return lax.ppermute(value, 'fsdp', way)]
    unnamed x62 -> x60, local copies, waits for them, and re-layouts: 6.53 us -> 5.94 us
  transfers between devices with their start and end apart: 37 -> 37, of which waited for: 13 -> 14; matrix products, arithmetic and copies ran while one was open for 3% -> 3% of each run, Pallas kernels for 17% -> 18%
where the time goes in v3:
time: 179 us; the launch traced here: 178 us
  waiting for transfers between devices  60.2 us (34%)
  starting transfers between devices  54.4 us (30%)
  Pallas kernels  34.8 us (19%)
  between operations  14.4 us (8%)
  local copies, waits for them, and re-layouts  8.88 us (5%)
  other arithmetic  4.94 us (3%)
    ppermute x14, waiting for transfers between devices, scatter(): move = lambda value, way: lax.ppermute(value, 'fsdp', way)  34.4 us
    ppermute x14, waiting for transfers between devices, shift(): return lax.ppermute(value, 'fsdp', way)  24.7 us
    ppermute x14, starting transfers between devices, shift(): return lax.ppermute(value, 'fsdp', way)  23.2 us
    pallas_call x2, Pallas kernels, grads(): pl.pallas_call(grad_kernel, grid=(steps,), in_specs=[pl.BlockSpec((rows,...  22.4 us
    ppermute x14, starting transfers between devices, scatter(): move = lambda value, way: lax.ppermute(value, 'fsdp', way)  16.5 us
    ppermute x3, starting transfers between devices, per_device(): lax.ppermute(step, 'path', along_z(k))  10.3 us
    unnamed x60, local copies, waits for them, and re-layouts  5.94 us
    pallas_call x2, Pallas kernels, final(): pl.pallas_call(functools.partial(final_kernel, len(terms), first), grid_s...  5.33 us
  transfers between devices with their start and end apart: 37, of which 14 were waited for; matrix products, arithmetic and copies ran while one was open for 3% of the time, Pallas kernels for 18%

profile of v3, /device:TPU:24, one launch (start us, length us, event | category | flops | bytes accessed | tf_op | source)
XLA Modules:
  0.0 177.7 jit_solution(313785806877573139)
XLA Ops:
  7.2 1.9 %slice.8 = bf16[256,1024]{1,0:T(8,128)(2,1)} slice(bf16[256,2048]{1,0:T(8,128)(2,1)} %bitcast.25), slice={[0:256], [0:1024]} | slice | bytes 1048576 | tf_op jit(solution)/shard_map/slice | solution.py:400
  9.2 2.8 %collective-permute-start = (bf16[256,1024]{1,0:T(8,128)(2,1)}, bf16[256,1024]{1,0:T(8,128)(2,1)}, u32[]{:S(2)}, u32[]{:S(2)}) collective-permute-start(bf16[256,1024]{1,0:T(8,128)(2,1)} %slice.8), channel_id=1, source_target_pairs={{0,3},{1,0},{2,1},{3,2},{4,7},{5,4},{6,5},{7,6},{8,11},{9,8},{10,9... | collective-permute-start | bytes 1572872 | tf_op jit(solution)/shard_map/shards/ppermute | solution.py:317
  11.9 1.9 %collective-permute-start.2 = (bf16[256,1024]{1,0:T(8,128)(2,1)}, bf16[256,1024]{1,0:T(8,128)(2,1)}, u32[]{:S(2)}, u32[]{:S(2)}) collective-permute-start(bf16[256,1024]{1,0:T(8,128)(2,1)} %slice.8), channel_id=1, source_target_pairs={{0,4},{1,5},{2,6},{3,7},{4,0},{5,1},{6,2},{7,3},{8,12},{9,13},{10,... | collective-permute-start | bytes 1572872 | tf_op jit(solution)/shard_map/shards/ppermute | solution.py:317
  13.9 1.4 deal.1
  15.3 0.5 copy-done.6
  15.8 1.9 %norm.1.refs_4_.n_ref = bf16[768,2048]{1,0:T(8,128)(2,1)S(1)} custom-call(s32[2]{0:T(128)S(1)} %pad_add_fusion.place_ref, bf16[768,2048]{1,0:T(8,128)(2,1)S(1)} %bitcast.31), custom_call_target="tpu_custom_call" | custom-call | flops 4718592 | bytes 6291456 | tf_op jit(solution)/shard_map/norm/pallas_call | solution.py:69
  17.8 1.3 collective-permute-start.8
  19.1 2.2 %collective-permute-start.7 = (bf16[4,256,128]{2,1,0:T(8,128)(2,1)S(1)}, bf16[4,256,128]{2,1,0:T(8,128)(2,1)S(1)}, u32[]{:S(2)}, u32[]{:S(2)}) collective-permute-start(bf16[4,256,128]{2,1,0:T(8,128)(2,1)S(1)} %get-tuple-element.46), channel_id=1, source_target_pairs={{0,16},{8,24},{16,32},{24,40},{32,48},{40,56},{48,0},{56,8},{64,80... | collective-permute-start | bytes 786440 | tf_op jit(solution)/shard_map/ppermute | solution.py:405
  21.3 2.2 %collective-permute-done.refs_6_.rest_1_ = bf16[256,1024]{1,0:T(8,128)(2,1)} collective-permute-done((bf16[256,1024]{1,0:T(8,128)(2,1)}, bf16[256,1024]{1,0:T(8,128)(2,1)}, u32[]{:S(2)}, u32[]{:S(2)}) %collective-permute-start) | collective-permute-done | bytes 524320 | tf_op jit(solution)/shard_map/shards/ppermute | solution.py:317
  23.4 0.7 collective-permute-start.9
  24.2 2.7 %collective-permute-done.1.refs_5_.rest_3_ = bf16[256,1024]{1,0:T(8,128)(2,1)} collective-permute-done((bf16[256,1024]{1,0:T(8,128)(2,1)}, bf16[256,1024]{1,0:T(8,128)(2,1)}, u32[]{:S(2)}, u32[]{:S(2)}) %collective-permute-start.1) | collective-permute-done | bytes 524320 | tf_op jit(solution)/shard_map/shards/ppermute | solution.py:317
  26.8 1.9 %collective-permute-start.5 = (bf16[256,1024]{1,0:T(8,128)(2,1)}, bf16[256,1024]{1,0:T(8,128)(2,1)}, u32[]{:S(2)}, u32[]{:S(2)}) collective-permute-start(bf16[256,1024]{1,0:T(8,128)(2,1)} %collective-permute-done.1.refs_5_.rest_3_), channel_id=1, source_target_pairs={{0,4},{1,5},{2,6},{3,7},{4,0},{5,1},{6,2},{7,3},{8,12},{9,13},{10,... | collective-permute-start | bytes 1572872 | tf_op jit(solution)/shard_map/shards_on/ppermute | solution.py:317
  28.8 3.2 %collective-permute-start.4 = (bf16[256,1024]{1,0:T(8,128)(2,1)}, bf16[256,1024]{1,0:T(8,128)(2,1)S(1)}, u32[]{:S(2)}, u32[]{:S(2)}) collective-permute-start(bf16[256,1024]{1,0:T(8,128)(2,1)} %collective-permute-done.2.refs_7_.rest_4_), channel_id=1, source_target_pairs={{0,3},{1,0},{2,1},{3,2},{4,7},{5,4},{6,5},{7,6},{8,11},{9,8},{10,9... | collective-permute-start | bytes 1572872 | tf_op jit(solution)/shard_map/shards_on/ppermute | solution.py:317
  32.0 1.0 collective-permute-done.9.refs_3_
  33.0 1.5 place_sums.1
  34.8 3.2 %collective-permute-start.10 = (bf16[256,1024]{1,0:T(8,128)(2,1)S(1)}, bf16[256,1024]{1,0:T(8,128)(2,1)S(1)}, u32[]{:S(2)}, u32[]{:S(2)}) collective-permute-start(bf16[256,1024]{1,0:T(8,128)(2,1)S(1)} %slice.7), channel_id=1, source_target_pairs={{0,3},{1,0},{2,1},{3,2},{4,7},{5,4},{6,5},{7,6},{8,11},{9,8},{10,9... | collective-permute-start | bytes 1572872 | tf_op jit(solution)/shard_map/late_shards/ppermute | solution.py:317
  38.0 1.8 %collective-permute-done.5.rest_7_ = bf16[256,1024]{1,0:T(8,128)(2,1)} collective-permute-done((bf16[256,1024]{1,0:T(8,128)(2,1)}, bf16[256,1024]{1,0:T(8,128)(2,1)}, u32[]{:S(2)}, u32[]{:S(2)}) %collective-permute-start.5) | collective-permute-done | bytes 524320 | tf_op jit(solution)/shard_map/shards_on/ppermute | solution.py:317
  39.8 2.6 %collective-permute-done.3.rest_2_ = bf16[256,1024]{1,0:T(8,128)(2,1)S(1)} collective-permute-done((bf16[256,1024]{1,0:T(8,128)(2,1)}, bf16[256,1024]{1,0:T(8,128)(2,1)S(1)}, u32[]{:S(2)}, u32[]{:S(2)}) %collective-permute-start.3) | collective-permute-done | bytes 524320 | tf_op jit(solution)/shard_map/shards_on/ppermute | solution.py:317
  42.4 2.3 %collective-permute-done.4.rest_5_ = bf16[256,1024]{1,0:T(8,128)(2,1)S(1)} collective-permute-done((bf16[256,1024]{1,0:T(8,128)(2,1)}, bf16[256,1024]{1,0:T(8,128)(2,1)S(1)}, u32[]{:S(2)}, u32[]{:S(2)}) %collective-permute-start.4) | collective-permute-done | bytes 524320 | tf_op jit(solution)/shard_map/shards_on/ppermute | solution.py:317
  44.7 0.3 collective-permute-start.6
  45.0 0.5 copy-done.26
  45.5 0.9 add_convert_fusion.6
  46.4 6.4 %collective-permute-done.10.rest_8_.rest_1_ = bf16[256,1024]{1,0:T(8,128)(2,1)S(1)} collective-permute-done((bf16[256,1024]{1,0:T(8,128)(2,1)S(1)}, bf16[256,1024]{1,0:T(8,128)(2,1)S(1)}, u32[]{:S(2)}, u32[]{:S(2)}) %collective-permute-start.10) | collective-permute-done | bytes 524320 | tf_op jit(solution)/shard_map/late_shards/ppermute | solution.py:317
  52.9 0.3 collective-permute-start.15
  53.3 1.0 copy.15.mask_ref
  54.2 3.7 %collective-permute-start.13 = (bf16[256,1024]{1,0:T(8,128)(2,1)S(1)}, bf16[256,1024]{1,0:T(8,128)(2,1)S(1)}, u32[]{:S(2)}, u32[]{:S(2)}) collective-permute-start(bf16[256,1024]{1,0:T(8,128)(2,1)S(1)} %collective-permute-done.10.rest_8_.rest_1_), channel_id=1, source_target_pairs={{0,3},{1,0},{2,1},{3,2},{4,7},{5,4},{6,5},{7,6},{8,11},{9,8},{10,9... | collective-permute-start | bytes 1572872 | tf_op jit(solution)/shard_map/late_shards_on/ppermute | solution.py:317
  57.9 0.6 collective-permute-done.12.rest_9_.rest_4_
  58.5 2.3 %collective-permute-start.17 = (bf16[256,1024]{1,0:T(8,128)(2,1)S(1)}, bf16[256,1024]{1,0:T(8,128)(2,1)}, u32[]{:S(2)}, u32[]{:S(2)}) collective-permute-start(bf16[256,1024]{1,0:T(8,128)(2,1)S(1)} %collective-permute-done.12.rest_9_.rest_4_), channel_id=1, source_target_pairs={{0,1},{1,2},{2,3},{3,0},{4,5},{5,6},{6,7},{7,4},{8,9},{9,10},{10,1... | collective-permute-start | bytes 1572872 | tf_op jit(solution)/shard_map/late_shards_on/ppermute | solution.py:317
  60.8 6.1 %collective-permute-done.15.rest_5_ = bf16[256,1024]{1,0:T(8,128)(2,1)} collective-permute-done((bf16[256,1024]{1,0:T(8,128)(2,1)S(1)}, bf16[256,1024]{1,0:T(8,128)(2,1)}, u32[]{:S(2)}, u32[]{:S(2)}) %collective-permute-start.15) | collective-permute-done | bytes 524320 | tf_op jit(solution)/shard_map/late_shards_on/ppermute | solution.py:317
  67.0 3.6 %collective-permute-start.16 = (bf16[256,1024]{1,0:T(8,128)(2,1)}, bf16[256,1024]{1,0:T(8,128)(2,1)}, u32[]{:S(2)}, u32[]{:S(2)}) collective-permute-start(bf16[256,1024]{1,0:T(8,128)(2,1)} %collective-permute-done.15.rest_5_), channel_id=1, source_target_pairs={{0,3},{1,0},{2,1},{3,2},{4,7},{5,4},{6,5},{7,6},{8,11},{9,8},{10,9... | collective-permute-start | bytes 1572872 | tf_op jit(solution)/shard_map/late_shards_last/ppermute | solution.py:317
  70.6 11.5 %grads.2 = (bf16[272,1024]{1,0:T(8,128)(2,1)}, bf16[272,1024]{1,0:T(8,128)(2,1)}, bf16[272,1024]{1,0:T(8,128)(2,1)}, bf16[272,1024]{1,0:T(8,128)(2,1)}, bf16[272...) custom-call(bf16[768,2048]{1,0:T(8,128)(2,1)} %copy-done.3, ...), custom_call_target="tpu_custom_call" | custom-call | flops 6442450944 | bytes 13107200 | tf_op jit(solution)/shard_map/grads/pallas_call | solution.py:113
  82.1 1.3 collective-permute-start.21
  83.4 0.8 copy-done.27
  84.2 0.8 collective-permute-start.22
  85.0 0.8 copy-done.28
  85.8 0.9 copy-done.11
  86.7 2.3 %outer.1 = (f32[4,64,256]{2,1,0:T(8,128)}, f32[4,64,256]{2,1,0:T(8,128)}, bf16[4,128,128]{2,1,0:T(8,128)(2,1)S(1)}) custom-call(s32[4]{0:T(128)S(1)} %copy-done.13, bf16[4,128,128]{2,1,0:T(8,128)(2,1)S(1)} %bitcast.34, f32[4,64,256]{2,1,0:T(8,128)S(1)} %bitcast.32, f32[4,64,256]{2,1,0:T(8,128)S(1)} %bitcast.33), custom_call_target="tpu_custom_call" | custom-call | flops 524288 | bytes 2097152 | tf_op jit(solution)/shard_map/outer/pallas_call | solution.py:232
  89.0 3.3 %collective-permute-start.18 = (bf16[4,128,128]{2,1,0:T(8,128)(2,1)S(1)}, bf16[4,128,128]{2,1,0:T(8,128)(2,1)S(1)}, u32[]{:S(2)}, u32[]{:S(2)}) collective-permute-start(bf16[4,128,128]{2,1,0:T(8,128)(2,1)S(1)} %get-tuple-element.58), channel_id=1, source_target_pairs={{0,64},{8,72},{16,80},{24,88},{32,96},{40,104},{48,112},{56,120},{... | collective-permute-start | bytes 393224 | tf_op jit(solution)/shard_map/steps_along_z/ppermute | solution.py:422
  92.3 6.9 %collective-permute-start.19 = (bf16[4,128,128]{2,1,0:T(8,128)(2,1)S(1)}, bf16[4,128,128]{2,1,0:T(8,128)(2,1)S(1)}, u32[]{:S(2)}, u32[]{:S(2)}) collective-permute-start(bf16[4,128,128]{2,1,0:T(8,128)(2,1)S(1)} %get-tuple-element.58), channel_id=1, source_target_pairs={{0,128},{8,136},{16,144},{24,152},{32,160},{40,168},{48,176},{56,1... | collective-permute-start | bytes 393224 | tf_op jit(solution)/shard_map/steps_along_z/ppermute | solution.py:422
  99.3 10.9 %grads.3 = (bf16[256,1024]{1,0:T(8,128)(2,1)}, bf16[256,1024]{1,0:T(8,128)(2,1)}, bf16[256,1024]{1,0:T(8,128)(2,1)}, bf16[256,1024]{1,0:T(8,128)(2,1)}, bf16[256...) custom-call(bf16[768,2048]{1,0:T(8,128)(2,1)} %copy-done.3, ...), custom_call_target="tpu_custom_call" | custom-call | flops 6442450944 | bytes 13107200 | tf_op jit(solution)/shard_map/grads/pallas_call | solution.py:113
  110.2 0.9 pad_maximum_fusion
  111.2 3.2 %collective-permute-start.23 = (bf16[256,1024]{1,0:T(8,128)(2,1)}, bf16[256,1024]{1,0:T(8,128)(2,1)S(1)}, u32[]{:S(2)}, u32[]{:S(2)}) collective-permute-start(bf16[256,1024]{1,0:T(8,128)(2,1)} %get-tuple-element.64), channel_id=1, source_target_pairs={{0,3},{1,0},{2,1},{3,2},{4,7},{5,4},{6,5},{7,6},{8,11},{9,8},{10,9... | collective-permute-start | bytes 1572872 | tf_op jit(solution)/shard_map/sum_near_other/ppermute | solution.py:363
  114.5 1.4 collective-permute-start.32
  115.8 0.2 add_convert_fusion.1
  116.1 0.9 collective-permute-start.33
  117.0 0.2 add_convert_fusion.2
  117.2 1.3 collective-permute-start.31
  118.5 5.0 %collective-permute-done.26 = bf16[256,1024]{1,0:T(8,128)(2,1)S(1)} collective-permute-done((bf16[256,1024]{1,0:T(8,128)(2,1)}, bf16[256,1024]{1,0:T(8,128)(2,1)S(1)}, u32[]{:S(2)}, u32[]{:S(2)}) %collective-permute-start.26) | collective-permute-done | bytes 524320 | tf_op jit(solution)/shard_map/sum_far_other/ppermute | solution.py:363
  123.8 3.4 %collective-permute-done.23 = bf16[256,1024]{1,0:T(8,128)(2,1)S(1)} collective-permute-done((bf16[256,1024]{1,0:T(8,128)(2,1)}, bf16[256,1024]{1,0:T(8,128)(2,1)S(1)}, u32[]{:S(2)}, u32[]{:S(2)}) %collective-permute-start.23) | collective-permute-done | bytes 524320 | tf_op jit(solution)/shard_map/sum_near_other/ppermute | solution.py:363
  127.2 1.0 collective-permute-start.28
  128.2 1.0 add_convert_fusion.5
  129.2 4.8 %collective-permute-done.32 = bf16[272,1024]{1,0:T(8,128)(2,1)S(1)} collective-permute-done((bf16[272,1024]{1,0:T(8,128)(2,1)}, bf16[272,1024]{1,0:T(8,128)(2,1)S(1)}, u32[]{:S(2)}, u32[]{:S(2)}) %collective-permute-start.32) | collective-permute-done | bytes 557088 | tf_op jit(solution)/shard_map/sum_far/ppermute | solution.py:363
  134.0 0.2 collective-permute-start.30
  134.2 1.0 collective-permute-start.25
  135.2 0.3 add_convert_fusion
  135.5 3.3 %collective-permute-start.24 = (bf16[256,1024]{1,0:T(8,128)(2,1)}, bf16[256,1024]{1,0:T(8,128)(2,1)}, u32[]{:S(2)}, u32[]{:S(2)}) collective-permute-start(bf16[256,1024]{1,0:T(8,128)(2,1)} %get-tuple-element.65), channel_id=1, source_target_pairs={{0,3},{1,0},{2,1},{3,2},{4,7},{5,4},{6,5},{7,6},{8,11},{9,8},{10,9... | collective-permute-start | bytes 1572872 | tf_op jit(solution)/shard_map/sum_near/ppermute | solution.py:363
  138.8 14.8 %collective-permute-done.28 = bf16[256,1024]{1,0:T(8,128)(2,1)S(1)} collective-permute-done((bf16[256,1024]{1,0:T(8,128)(2,1)S(1)}, bf16[256,1024]{1,0:T(8,128)(2,1)S(1)}, u32[]{:S(2)}, u32[]{:S(2)}) %collective-permute-start.28) | collective-permute-done | bytes 524320 | tf_op jit(solution)/shard_map/sum_cross_side/ppermute | solution.py:363
  153.6 0.3 collective-permute-start.34
  153.9 1.1 add_convert_fusion.3
  155.0 1.7 collective-permute-start.29
  156.8 6.4 %collective-permute-done.34.refs_3_ = bf16[272,1024]{1,0:T(8,128)(2,1)S(1)} collective-permute-done((bf16[272,1024]{1,0:T(8,128)(2,1)S(1)}, bf16[272,1024]{1,0:T(8,128)(2,1)S(1)}, u32[]{:S(2)}, u32[]{:S(2)}) %collective-permute-start.34) | collective-permute-done | bytes 557088 | tf_op jit(solution)/shard_map/sum_side/ppermute | solution.py:363
  163.2 2.2 %copy-done.1 = bf16[32,4,128,128]{3,2,1,0:T(8,128)(2,1)S(1)} copy-done((bf16[32,4,128,128]{3,2,1,0:T(8,128)(2,1)S(1)}, bf16[32,4,128,128]{3,2,1,0:T(8,128)(2,1)}, u32[]{:S(2)}) %copy-start.1) | copy-done | bytes 4194328
  165.3 2.2 %final.2 = (bf16[256,2048]{1,0:T(8,128)(2,1)}, f32[8,128]{1,0:T(8,128)S(1)}) custom-call(s32[2]{0:T(128)S(1)} %pad_add_fusion.place_ref, s32[32]{0:T(128)S(1)} %copy-done.12, bf16[256,2048]{1,0:T(8,128)(2,1)S(1)} %bitcast.29, bf16[8,4,4,128,128]{4,3,2,1,0:T(8,128)(2,1)S(1)} %bitcast.23, bf16[272,1024]{1,0:T(8,128)(2,1)S(1)} %copy-done.7, ...), custom_call_target="tpu_custom_call" | custom-call | flops 2097152 | bytes 3670016 | tf_op jit(solution)/shard_map/final/pallas_call | solution.py:291
  167.7 3.1 %final.3 = bf16[256,2048]{1,0:T(8,128)(2,1)} custom-call(s32[2]{0:T(128)S(1)} %pad_add_fusion.place_ref, s32[32]{0:T(128)S(1)} %copy-done.12, bf16[256,2048]{1,0:T(8,128)(2,1)S(1)} %bitcast.30, bf16[8,4,4,128,128]{4,3,2,1,0:T(8,128)(2,1)S(1)} %bitcast.24, bf16[256,1024]{1,0:T(8,128)(2,1)S(1)} %copy-done.8, ...), custom_call_target="tpu_custom_call", output_to_operand_aliasing={{}: (9, {})} | custom-call | flops 2097152 | bytes 3670016 | tf_op jit(solution)/shard_map/final/pallas_call | solution.py:291
  (93 shorter events, 1.0 us)
Async XLA Ops:
  7.2 6.8 %copy-start = (bf16[1,256,2048]{2,1,0:T(8,128)(2,1)S(1)}, bf16[1,256,2048]{2,1,0:T(8,128)(2,1)}, u32[]{:S(2)}) copy-start(bf16[1,256,2048]{2,1,0:T(8,128)(2,1)} %param.13) | copy-start | bytes 3145732
  7.2 78.6 %reduce-scatter.2.cloned.1.call-start = ((), (), s32[]{:S(2)}) async-start(), calls=%async_computation.1 | async-start | bytes 655360 | tf_op jit(solution)/shard_map/reduce_scatter | solution.py:411
  9.2 14.3 %collective-permute-start = (bf16[256,1024]{1,0:T(8,128)(2,1)}, bf16[256,1024]{1,0:T(8,128)(2,1)}, u32[]{:S(2)}, u32[]{:S(2)}) collective-permute-start(bf16[256,1024]{1,0:T(8,128)(2,1)} %slice.8), channel_id=1, source_target_pairs={{0,3},{1,0},{2,1},{3,2},{4,7},{5,4},{6,5},{7,6},{8,11},{9,8},{10,9... | collective-permute-start | bytes 1572872 | tf_op jit(solution)/shard_map/shards/ppermute | solution.py:317
  11.9 14.9 %collective-permute-start.1 = (bf16[256,1024]{1,0:T(8,128)(2,1)}, bf16[256,1024]{1,0:T(8,128)(2,1)}, u32[]{:S(2)}, u32[]{:S(2)}) collective-permute-start(bf16[256,1024]{1,0:T(8,128)(2,1)} %slice.8), channel_id=1, source_target_pairs={{0,1},{1,2},{2,3},{3,0},{4,5},{5,6},{6,7},{7,4},{8,9},{9,10},{10,1... | collective-permute-start | bytes 1572872 | tf_op jit(solution)/shard_map/shards/ppermute | solution.py:317
  11.9 14.9 %collective-permute-start.2 = (bf16[256,1024]{1,0:T(8,128)(2,1)}, bf16[256,1024]{1,0:T(8,128)(2,1)}, u32[]{:S(2)}, u32[]{:S(2)}) collective-permute-start(bf16[256,1024]{1,0:T(8,128)(2,1)} %slice.8), channel_id=1, source_target_pairs={{0,4},{1,5},{2,6},{3,7},{4,0},{5,1},{6,2},{7,3},{8,12},{9,13},{10,... | collective-permute-start | bytes 1572872 | tf_op jit(solution)/shard_map/shards/ppermute | solution.py:317
  13.9 1.9 %copy-start.6 = (bf16[1,768,2048]{2,1,0:T(8,128)(2,1)S(1)}, bf16[1,768,2048]{2,1,0:T(8,128)(2,1)}, u32[]{:S(2)}) copy-start(bf16[1,768,2048]{2,1,0:T(8,128)(2,1)} %param.9) | copy-start | bytes 9437188
  15.8 17.2 %copy-start.12 = (s32[32]{0:T(128)S(1)}, s32[32]{0:T(128)}, u32[]{:S(2)}) copy-start(s32[32]{0:T(128)} %module_ref.5) | copy-start | bytes 388
  17.8 16.8 %copy-start.3 = (bf16[768,2048]{1,0:T(8,128)(2,1)}, bf16[768,2048]{1,0:T(8,128)(2,1)S(1)}, u32[]{:S(2)}) copy-start(bf16[768,2048]{1,0:T(8,128)(2,1)S(1)} %norm.1.refs_4_.n_ref) | copy-start | bytes 9437188
  17.8 11.0 %collective-permute-start.8 = (bf16[4,256,128]{2,1,0:T(8,128)(2,1)S(1)}, bf16[4,256,128]{2,1,0:T(8,128)(2,1)S(1)}, u32[]{:S(2)}, u32[]{:S(2)}) collective-permute-start(bf16[4,256,128]{2,1,0:T(8,128)(2,1)S(1)} %get-tuple-element.48), channel_id=1, source_target_pairs={{0,32},{8,40},{16,48},{24,56},{32,0},{40,8},{48,16},{56,24},{64,96... | collective-permute-start | bytes 786440 | tf_op jit(solution)/shard_map/ppermute | solution.py:405
  19.1 12.9 %collective-permute-start.7 = (bf16[4,256,128]{2,1,0:T(8,128)(2,1)S(1)}, bf16[4,256,128]{2,1,0:T(8,128)(2,1)S(1)}, u32[]{:S(2)}, u32[]{:S(2)}) collective-permute-start(bf16[4,256,128]{2,1,0:T(8,128)(2,1)S(1)} %get-tuple-element.46), channel_id=1, source_target_pairs={{0,16},{8,24},{16,32},{24,40},{32,48},{40,56},{48,0},{56,8},{64,80... | collective-permute-start | bytes 786440 | tf_op jit(solution)/shard_map/ppermute | solution.py:405
  23.4 9.6 %collective-permute-start.9 = (bf16[4,256,128]{2,1,0:T(8,128)(2,1)S(1)}, bf16[4,256,128]{2,1,0:T(8,128)(2,1)S(1)}, u32[]{:S(2)}, u32[]{:S(2)}) collective-permute-start(bf16[4,256,128]{2,1,0:T(8,128)(2,1)S(1)} %get-tuple-element.49), channel_id=1, source_target_pairs={{0,48},{8,56},{16,0},{24,8},{32,16},{40,24},{48,32},{56,40},{64,11... | collective-permute-start | bytes 786440 | tf_op jit(solution)/shard_map/ppermute | solution.py:405
  26.8 13.0 %collective-permute-start.5 = (bf16[256,1024]{1,0:T(8,128)(2,1)}, bf16[256,1024]{1,0:T(8,128)(2,1)}, u32[]{:S(2)}, u32[]{:S(2)}) collective-permute-start(bf16[256,1024]{1,0:T(8,128)(2,1)} %collective-permute-done.1.refs_5_.rest_3_), channel_id=1, source_target_pairs={{0,4},{1,5},{2,6},{3,7},{4,0},{5,1},{6,2},{7,3},{8,12},{9,13},{10,... | collective-permute-start | bytes 1572872 | tf_op jit(solution)/shard_map/shards_on/ppermute | solution.py:317
  28.8 13.6 %collective-permute-start.3 = (bf16[256,1024]{1,0:T(8,128)(2,1)}, bf16[256,1024]{1,0:T(8,128)(2,1)S(1)}, u32[]{:S(2)}, u32[]{:S(2)}) collective-permute-start(bf16[256,1024]{1,0:T(8,128)(2,1)} %collective-permute-done.1.refs_5_.rest_3_), channel_id=1, source_target_pairs={{0,1},{1,2},{2,3},{3,0},{4,5},{5,6},{6,7},{7,4},{8,9},{9,10},{10,1... | collective-permute-start | bytes 1572872 | tf_op jit(solution)/shard_map/shards_on/ppermute | solution.py:317
  28.8 15.9 %collective-permute-start.4 = (bf16[256,1024]{1,0:T(8,128)(2,1)}, bf16[256,1024]{1,0:T(8,128)(2,1)S(1)}, u32[]{:S(2)}, u32[]{:S(2)}) collective-permute-start(bf16[256,1024]{1,0:T(8,128)(2,1)} %collective-permute-done.2.refs_7_.rest_4_), channel_id=1, source_target_pairs={{0,3},{1,0},{2,1},{3,2},{4,7},{5,4},{6,5},{7,6},{8,11},{9,8},{10,9... | collective-permute-start | bytes 1572872 | tf_op jit(solution)/shard_map/shards_on/ppermute | solution.py:317
  33.0 1.7 copy-start.4
  34.6 10.4 %collective-permute-start.11 = (bf16[4,4,128,128]{3,2,1,0:T(8,128)(2,1)S(1)}, bf16[4,4,128,128]{3,2,1,0:T(8,128)(2,1)S(1)}, u32[]{:S(2)}, u32[]{:S(2)}) collective-permute-start(bf16[4,4,128,128]{3,2,1,0:T(8,128)(2,1)S(1)} %get-tuple-element.53), channel_id=1, source_target_pairs={{0,8},{8,0},{16,24},{24,16},{32,40},{40,32},{48,56},{56,48},{64,72... | collective-permute-start | bytes 1572872 | tf_op jit(solution)/shard_map/ppermute | solution.py:408
  34.7 18.5 %copy-start.20 = (s32[1,768]{1,0:T(1,128)S(1)}, s32[1,768]{1,0:T(1,128)}, u32[]{:S(2)}) copy-start(s32[1,768]{1,0:T(1,128)} %param.11) | copy-start | bytes 9220
  34.8 18.1 %collective-permute-start.10 = (bf16[256,1024]{1,0:T(8,128)(2,1)S(1)}, bf16[256,1024]{1,0:T(8,128)(2,1)S(1)}, u32[]{:S(2)}, u32[]{:S(2)}) collective-permute-start(bf16[256,1024]{1,0:T(8,128)(2,1)S(1)} %slice.7), channel_id=1, source_target_pairs={{0,3},{1,0},{2,1},{3,2},{4,7},{5,4},{6,5},{7,6},{8,11},{9,8},{10,9... | collective-permute-start | bytes 1572872 | tf_op jit(solution)/shard_map/late_shards/ppermute | solution.py:317
  42.4 2.6 %copy-start.23 = (bf16[256,1024]{1,0:T(8,128)(2,1)}, bf16[256,1024]{1,0:T(8,128)(2,1)S(1)}, u32[]{:S(2)}) copy-start(bf16[256,1024]{1,0:T(8,128)(2,1)S(1)} %collective-permute-done.3.rest_2_) | copy-start | bytes 1572868
  44.7 13.2 %collective-permute-start.6 = (bf16[256,1024]{1,0:T(8,128)(2,1)}, bf16[256,1024]{1,0:T(8,128)(2,1)S(1)}, u32[]{:S(2)}, u32[]{:S(2)}) collective-permute-start(bf16[256,1024]{1,0:T(8,128)(2,1)} %collective-permute-done.5.rest_7_), channel_id=1, source_target_pairs={{0,1},{1,2},{2,3},{3,0},{4,5},{5,6},{6,7},{7,4},{8,9},{9,10},{10,1... | collective-permute-start | bytes 1572872 | tf_op jit(solution)/shard_map/shards_last/ppermute | solution.py:317
  46.4 12.1 %collective-permute-start.12 = (bf16[256,1024]{1,0:T(8,128)(2,1)S(1)}, bf16[256,1024]{1,0:T(8,128)(2,1)S(1)}, u32[]{:S(2)}, u32[]{:S(2)}) collective-permute-start(bf16[256,1024]{1,0:T(8,128)(2,1)S(1)} %slice.7), channel_id=1, source_target_pairs={{0,4},{1,5},{2,6},{3,7},{4,0},{5,1},{6,2},{7,3},{8,12},{9,13},{10,... | collective-permute-start | bytes 1572872 | tf_op jit(solution)/shard_map/late_shards/ppermute | solution.py:317
  52.9 17.7 %copy-start.22 = (bf16[256,1024]{1,0:T(8,128)(2,1)}, bf16[256,1024]{1,0:T(8,128)(2,1)S(1)}, u32[]{:S(2)}) copy-start(bf16[256,1024]{1,0:T(8,128)(2,1)S(1)} %collective-permute-done.10.rest_8_.rest_1_) | copy-start | bytes 1572868
  52.9 14.1 %collective-permute-start.15 = (bf16[256,1024]{1,0:T(8,128)(2,1)S(1)}, bf16[256,1024]{1,0:T(8,128)(2,1)}, u32[]{:S(2)}, u32[]{:S(2)}) collective-permute-start(bf16[256,1024]{1,0:T(8,128)(2,1)S(1)} %collective-permute-done.10.rest_8_.rest_1_), channel_id=1, source_target_pairs={{0,4},{1,5},{2,6},{3,7},{4,0},{5,1},{6,2},{7,3},{8,12},{9,13},{10,... | collective-permute-start | bytes 1572872 | tf_op jit(solution)/shard_map/late_shards_on/ppermute | solution.py:317
  53.2 110.0 %all-gather.3.cloned.1.call-start = ((), (), s32[]{:S(2)}) async-start(), calls=%async_computation.2 | async-start | bytes 4718592 | tf_op jit(solution)/shard_map/all_gather | solution.py:427
  54.2 29.2 %collective-permute-start.13 = (bf16[256,1024]{1,0:T(8,128)(2,1)S(1)}, bf16[256,1024]{1,0:T(8,128)(2,1)S(1)}, u32[]{:S(2)}, u32[]{:S(2)}) collective-permute-start(bf16[256,1024]{1,0:T(8,128)(2,1)S(1)} %collective-permute-done.10.rest_8_.rest_1_), channel_id=1, source_target_pairs={{0,3},{1,0},{2,1},{3,2},{4,7},{5,4},{6,5},{7,6},{8,11},{9,8},{10,9... | collective-permute-start | bytes 1572872 | tf_op jit(solution)/shard_map/late_shards_on/ppermute | solution.py:317
  57.9 12.6 %copy-start.29 = (bf16[256,1024]{1,0:T(8,128)(2,1)}, bf16[256,1024]{1,0:T(8,128)(2,1)S(1)}, u32[]{:S(2)}) copy-start(bf16[256,1024]{1,0:T(8,128)(2,1)S(1)} %collective-permute-done.6.rest_6_) | copy-start | bytes 1572868
  57.9 27.1 %collective-permute-start.14 = (bf16[256,1024]{1,0:T(8,128)(2,1)S(1)}, bf16[256,1024]{1,0:T(8,128)(2,1)S(1)}, u32[]{:S(2)}, u32[]{:S(2)}) collective-permute-start(bf16[256,1024]{1,0:T(8,128)(2,1)S(1)} %slice.7), channel_id=1, source_target_pairs={{0,1},{1,2},{2,3},{3,0},{4,5},{5,6},{6,7},{7,4},{8,9},{9,10},{10,1... | collective-permute-start | bytes 1572872 | tf_op jit(solution)/shard_map/late_shards/ppermute | solution.py:317
  58.5 12.0 %copy-start.24 = (bf16[256,1024]{1,0:T(8,128)(2,1)}, bf16[256,1024]{1,0:T(8,128)(2,1)S(1)}, u32[]{:S(2)}) copy-start(bf16[256,1024]{1,0:T(8,128)(2,1)S(1)} %collective-permute-done.12.rest_9_.rest_4_) | copy-start | bytes 1572868
  58.5 26.5 %collective-permute-start.17 = (bf16[256,1024]{1,0:T(8,128)(2,1)S(1)}, bf16[256,1024]{1,0:T(8,128)(2,1)}, u32[]{:S(2)}, u32[]{:S(2)}) collective-permute-start(bf16[256,1024]{1,0:T(8,128)(2,1)S(1)} %collective-permute-done.12.rest_9_.rest_4_), channel_id=1, source_target_pairs={{0,1},{1,2},{2,3},{3,0},{4,5},{5,6},{6,7},{7,4},{8,9},{9,10},{10,1... | collective-permute-start | bytes 1572872 | tf_op jit(solution)/shard_map/late_shards_on/ppermute | solution.py:317
  67.0 18.8 %collective-permute-start.16 = (bf16[256,1024]{1,0:T(8,128)(2,1)}, bf16[256,1024]{1,0:T(8,128)(2,1)}, u32[]{:S(2)}, u32[]{:S(2)}) collective-permute-start(bf16[256,1024]{1,0:T(8,128)(2,1)} %collective-permute-done.15.rest_5_), channel_id=1, source_target_pairs={{0,3},{1,0},{2,1},{3,2},{4,7},{5,4},{6,5},{7,6},{8,11},{9,8},{10,9... | collective-permute-start | bytes 1572872 | tf_op jit(solution)/shard_map/late_shards_last/ppermute | solution.py:317
  70.6 15.3 %copy-start.9 = (f32[4,256,64]{1,2,0:T(8,128)S(1)}, f32[4,256,64]{1,2,0:T(8,128)}, u32[]{:S(2)}) copy-start(f32[4,256,64]{1,2,0:T(8,128)} %param.14) | copy-start | bytes 786436
  70.6 15.2 %copy-start.10 = (f32[4,256,64]{1,2,0:T(8,128)S(1)}, f32[4,256,64]{1,2,0:T(8,128)}, u32[]{:S(2)}) copy-start(f32[4,256,64]{1,2,0:T(8,128)} %param.15) | copy-start | bytes 786436
  70.6 15.2 %copy-start.13 = (s32[4]{0:T(128)S(1)}, s32[4]{0:T(128)}, u32[]{:S(2)}) copy-start(s32[4]{0:T(128)} %count_ref) | copy-start | bytes 52
  82.1 29.0 %collective-permute-start.21 = (bf16[272,1024]{1,0:T(8,128)(2,1)}, bf16[272,1024]{1,0:T(8,128)(2,1)S(1)}, u32[]{:S(2)}, u32[]{:S(2)}) collective-permute-start(bf16[272,1024]{1,0:T(8,128)(2,1)} %get-tuple-element.60), channel_id=1, source_target_pairs={{0,3},{1,0},{2,1},{3,2},{4,7},{5,4},{6,5},{7,6},{8,11},{9,8},{10,9... | collective-permute-start | bytes 1671176 | tf_op jit(solution)/shard_map/sum_far_other/ppermute | solution.py:363
  84.2 26.9 %collective-permute-start.22 = (bf16[272,1024]{1,0:T(8,128)(2,1)}, bf16[272,1024]{1,0:T(8,128)(2,1)S(1)}, u32[]{:S(2)}, u32[]{:S(2)}) collective-permute-start(bf16[272,1024]{1,0:T(8,128)(2,1)} %get-tuple-element.61), channel_id=1, source_target_pairs={{0,1},{1,2},{2,3},{3,0},{4,5},{5,6},{6,7},{7,4},{8,9},{9,10},{10,1... | collective-permute-start | bytes 1671176 | tf_op jit(solution)/shard_map/sum_near_other/ppermute | solution.py:363
  85.8 0.9 copy-start.11
  89.0 21.2 %collective-permute-start.18 = (bf16[4,128,128]{2,1,0:T(8,128)(2,1)S(1)}, bf16[4,128,128]{2,1,0:T(8,128)(2,1)S(1)}, u32[]{:S(2)}, u32[]{:S(2)}) collective-permute-start(bf16[4,128,128]{2,1,0:T(8,128)(2,1)S(1)} %get-tuple-element.58), channel_id=1, source_target_pairs={{0,64},{8,72},{16,80},{24,88},{32,96},{40,104},{48,112},{56,120},{... | collective-permute-start | bytes 393224 | tf_op jit(solution)/shard_map/steps_along_z/ppermute | solution.py:422
  92.3 17.9 %collective-permute-start.19 = (bf16[4,128,128]{2,1,0:T(8,128)(2,1)S(1)}, bf16[4,128,128]{2,1,0:T(8,128)(2,1)S(1)}, u32[]{:S(2)}, u32[]{:S(2)}) collective-permute-start(bf16[4,128,128]{2,1,0:T(8,128)(2,1)S(1)} %get-tuple-element.58), channel_id=1, source_target_pairs={{0,128},{8,136},{16,144},{24,152},{32,160},{40,168},{48,176},{56,1... | collective-permute-start | bytes 393224 | tf_op jit(solution)/shard_map/steps_along_z/ppermute | solution.py:422
  99.2 11.0 %collective-permute-start.20 = (bf16[4,128,128]{2,1,0:T(8,128)(2,1)S(1)}, bf16[4,128,128]{2,1,0:T(8,128)(2,1)S(1)}, u32[]{:S(2)}, u32[]{:S(2)}) collective-permute-start(bf16[4,128,128]{2,1,0:T(8,128)(2,1)S(1)} %get-tuple-element.58), channel_id=1, source_target_pairs={{0,192},{8,200},{16,208},{24,216},{32,224},{40,232},{48,240},{56,2... | collective-permute-start | bytes 393224 | tf_op jit(solution)/shard_map/steps_along_z/ppermute | solution.py:422
  110.1 5.7 %copy-start.16 = (bf16[272,1024]{1,0:T(8,128)(2,1)S(1)}, bf16[272,1024]{1,0:T(8,128)(2,1)}, u32[]{:S(2)}) copy-start(bf16[272,1024]{1,0:T(8,128)(2,1)} %get-tuple-element.78) | copy-start | bytes 1671172
  111.1 5.9 %copy-start.15 = (bf16[272,1024]{1,0:T(8,128)(2,1)S(1)}, bf16[272,1024]{1,0:T(8,128)(2,1)}, u32[]{:S(2)}) copy-start(bf16[272,1024]{1,0:T(8,128)(2,1)} %get-tuple-element.74) | copy-start | bytes 1671172
  111.2 12.4 %collective-permute-start.26 = (bf16[256,1024]{1,0:T(8,128)(2,1)}, bf16[256,1024]{1,0:T(8,128)(2,1)S(1)}, u32[]{:S(2)}, u32[]{:S(2)}) collective-permute-start(bf16[256,1024]{1,0:T(8,128)(2,1)} %get-tuple-element.69), channel_id=1, source_target_pairs={{0,1},{1,2},{2,3},{3,0},{4,5},{5,6},{6,7},{7,4},{8,9},{9,10},{10,1... | collective-permute-start | bytes 1572872 | tf_op jit(solution)/shard_map/sum_far_other/ppermute | solution.py:363
  111.2 15.9 %collective-permute-start.23 = (bf16[256,1024]{1,0:T(8,128)(2,1)}, bf16[256,1024]{1,0:T(8,128)(2,1)S(1)}, u32[]{:S(2)}, u32[]{:S(2)}) collective-permute-start(bf16[256,1024]{1,0:T(8,128)(2,1)} %get-tuple-element.64), channel_id=1, source_target_pairs={{0,3},{1,0},{2,1},{3,2},{4,7},{5,4},{6,5},{7,6},{8,11},{9,8},{10,9... | collective-permute-start | bytes 1572872 | tf_op jit(solution)/shard_map/sum_near_other/ppermute | solution.py:363
  114.5 19.5 %collective-permute-start.32 = (bf16[272,1024]{1,0:T(8,128)(2,1)}, bf16[272,1024]{1,0:T(8,128)(2,1)S(1)}, u32[]{:S(2)}, u32[]{:S(2)}) collective-permute-start(bf16[272,1024]{1,0:T(8,128)(2,1)} %get-tuple-element.77), channel_id=1, source_target_pairs={{0,3},{1,0},{2,1},{3,2},{4,7},{5,4},{6,5},{7,6},{8,11},{9,8},{10,9... | collective-permute-start | bytes 1671176 | tf_op jit(solution)/shard_map/sum_far/ppermute | solution.py:363
  116.0 7.5 %copy-start.25 = (bf16[256,1024]{1,0:T(8,128)(2,1)S(1)}, bf16[256,1024]{1,0:T(8,128)(2,1)}, u32[]{:S(2)}) copy-start(bf16[256,1024]{1,0:T(8,128)(2,1)} %get-tuple-element.70) | copy-start | bytes 1572868
  116.0 7.5 %copy-start.18 = (bf16[256,1024]{1,0:T(8,128)(2,1)S(1)}, bf16[256,1024]{1,0:T(8,128)(2,1)}, u32[]{:S(2)}) copy-start(bf16[256,1024]{1,0:T(8,128)(2,1)} %get-tuple-element.71) | copy-start | bytes 1572868
  116.1 18.1 %collective-permute-start.33 = (bf16[272,1024]{1,0:T(8,128)(2,1)S(1)}, bf16[272,1024]{1,0:T(8,128)(2,1)S(1)}, u32[]{:S(2)}, u32[]{:S(2)}) collective-permute-start(bf16[272,1024]{1,0:T(8,128)(2,1)S(1)} %add_convert_fusion.1), channel_id=1, source_target_pairs={{0,4},{1,5},{2,6},{3,7},{4,0},{5,1},{6,2},{7,3},{8,12},{9,13},{10,... | collective-permute-start | bytes 1671176 | tf_op jit(solution)/shard_map/sum_cross_side/ppermute | solution.py:363
  117.2 11.0 %copy-start.17 = (bf16[256,1024]{1,0:T(8,128)(2,1)S(1)}, bf16[256,1024]{1,0:T(8,128)(2,1)}, u32[]{:S(2)}) copy-start(bf16[256,1024]{1,0:T(8,128)(2,1)} %get-tuple-element.66) | copy-start | bytes 1572868
  117.2 37.8 %collective-permute-start.31 = (bf16[272,1024]{1,0:T(8,128)(2,1)S(1)}, bf16[272,1024]{1,0:T(8,128)(2,1)S(1)}, u32[]{:S(2)}, u32[]{:S(2)}) collective-permute-start(bf16[272,1024]{1,0:T(8,128)(2,1)S(1)} %add_convert_fusion.2), channel_id=1, source_target_pairs={{0,4},{1,5},{2,6},{3,7},{4,0},{5,1},{6,2},{7,3},{8,12},{9,13},{10,... | collective-permute-start | bytes 1671176 | tf_op jit(solution)/shard_map/sum_cross/ppermute | solution.py:363
  123.5 12.0 %collective-permute-start.27 = (bf16[256,1024]{1,0:T(8,128)(2,1)S(1)}, bf16[256,1024]{1,0:T(8,128)(2,1)S(1)}, u32[]{:S(2)}, u32[]{:S(2)}) collective-permute-start(bf16[256,1024]{1,0:T(8,128)(2,1)S(1)} %copy-done.25), channel_id=1, source_target_pairs={{0,1},{1,2},{2,3},{3,0},{4,5},{5,6},{6,7},{7,4},{8,9},{9,10},{10,1... | collective-permute-start | bytes 1572872 | tf_op jit(solution)/shard_map/sum_far/ppermute | solution.py:363
  123.7 10.2 %copy-start.21 = (bf16[272,1024]{1,0:T(8,128)(2,1)S(1)}, bf16[272,1024]{1,0:T(8,128)(2,1)}, u32[]{:S(2)}) copy-start(bf16[272,1024]{1,0:T(8,128)(2,1)} %get-tuple-element.73) | copy-start | bytes 1671172
  123.7 11.4 %copy-start.14 = (bf16[272,1024]{1,0:T(8,128)(2,1)S(1)}, bf16[272,1024]{1,0:T(8,128)(2,1)}, u32[]{:S(2)}) copy-start(bf16[272,1024]{1,0:T(8,128)(2,1)} %get-tuple-element.75) | copy-start | bytes 1671172
  127.2 26.4 %collective-permute-start.28 = (bf16[256,1024]{1,0:T(8,128)(2,1)S(1)}, bf16[256,1024]{1,0:T(8,128)(2,1)S(1)}, u32[]{:S(2)}, u32[]{:S(2)}) collective-permute-start(bf16[256,1024]{1,0:T(8,128)(2,1)S(1)} %add_convert_fusion.4), channel_id=1, source_target_pairs={{0,4},{1,5},{2,6},{3,7},{4,0},{5,1},{6,2},{7,3},{8,12},{9,13},{10,... | collective-permute-start | bytes 1572872 | tf_op jit(solution)/shard_map/sum_cross_side/ppermute | solution.py:363
  134.0 22.8 %collective-permute-start.30 = (bf16[272,1024]{1,0:T(8,128)(2,1)S(1)}, bf16[272,1024]{1,0:T(8,128)(2,1)S(1)}, u32[]{:S(2)}, u32[]{:S(2)}) collective-permute-start(bf16[272,1024]{1,0:T(8,128)(2,1)S(1)} %copy-done.21), channel_id=1, source_target_pairs={{0,1},{1,2},{2,3},{3,0},{4,5},{5,6},{6,7},{7,4},{8,9},{9,10},{10,1... | collective-permute-start | bytes 1671176 | tf_op jit(solution)/shard_map/sum_near/ppermute | solution.py:363
  134.2 33.4 %collective-permute-start.25 = (bf16[256,1024]{1,0:T(8,128)(2,1)}, bf16[256,1024]{1,0:T(8,128)(2,1)}, u32[]{:S(2)}, u32[]{:S(2)}) collective-permute-start(bf16[256,1024]{1,0:T(8,128)(2,1)} %add_convert_fusion.5), channel_id=1, source_target_pairs={{0,4},{1,5},{2,6},{3,7},{4,0},{5,1},{6,2},{7,3},{8,12},{9,13},{10,... | collective-permute-start | bytes 1572872 | tf_op jit(solution)/shard_map/sum_cross/ppermute | solution.py:363
  135.2 18.7 %copy-start.19 = (bf16[256,1024]{1,0:T(8,128)(2,1)S(1)}, bf16[256,1024]{1,0:T(8,128)(2,1)}, u32[]{:S(2)}) copy-start(bf16[256,1024]{1,0:T(8,128)(2,1)} %get-tuple-element.67) | copy-start | bytes 1572868
  135.5 27.7 %copy-start.5 = (bf16[1,256,2048]{2,1,0:T(8,128)(2,1)S(1)}, bf16[1,256,2048]{2,1,0:T(8,128)(2,1)}, u32[]{:S(2)}) copy-start(bf16[1,256,2048]{2,1,0:T(8,128)(2,1)} %param.12) | copy-start | bytes 3145732
  135.5 27.7 %copy-start.7 = (bf16[272,1024]{1,0:T(8,128)(2,1)S(1)}, bf16[272,1024]{1,0:T(8,128)(2,1)}, u32[]{:S(2)}) copy-start(bf16[272,1024]{1,0:T(8,128)(2,1)} %get-tuple-element.55.refs_0_) | copy-start | bytes 1671172
  135.5 32.1 %collective-permute-start.24 = (bf16[256,1024]{1,0:T(8,128)(2,1)}, bf16[256,1024]{1,0:T(8,128)(2,1)}, u32[]{:S(2)}, u32[]{:S(2)}) collective-permute-start(bf16[256,1024]{1,0:T(8,128)(2,1)} %get-tuple-element.65), channel_id=1, source_target_pairs={{0,3},{1,0},{2,1},{3,2},{4,7},{5,4},{6,5},{7,6},{8,11},{9,8},{10,9... | collective-permute-start | bytes 1572872 | tf_op jit(solution)/shard_map/sum_near/ppermute | solution.py:363
  153.6 9.5 %collective-permute-start.34 = (bf16[272,1024]{1,0:T(8,128)(2,1)S(1)}, bf16[272,1024]{1,0:T(8,128)(2,1)S(1)}, u32[]{:S(2)}, u32[]{:S(2)}) collective-permute-start(bf16[272,1024]{1,0:T(8,128)(2,1)S(1)} %add_convert_fusion), channel_id=1, source_target_pairs={{0,3},{1,0},{2,1},{3,2},{4,7},{5,4},{6,5},{7,6},{8,11},{9,8},{10,9... | collective-permute-start | bytes 1671176 | tf_op jit(solution)/shard_map/sum_side/ppermute | solution.py:363
  155.0 12.5 %collective-permute-start.29 = (bf16[256,1024]{1,0:T(8,128)(2,1)}, bf16[256,1024]{1,0:T(8,128)(2,1)}, u32[]{:S(2)}, u32[]{:S(2)}) collective-permute-start(bf16[256,1024]{1,0:T(8,128)(2,1)} %add_convert_fusion.3), channel_id=1, source_target_pairs={{0,1},{1,2},{2,3},{3,0},{4,5},{5,6},{6,7},{7,4},{8,9},{9,10},{10,1... | collective-permute-start | bytes 1572872 | tf_op jit(solution)/shard_map/sum_side/ppermute | solution.py:363
  163.1 2.2 %copy-start.1 = (bf16[32,4,128,128]{3,2,1,0:T(8,128)(2,1)S(1)}, bf16[32,4,128,128]{3,2,1,0:T(8,128)(2,1)}, u32[]{:S(2)}) copy-start(bf16[32,4,128,128]{3,2,1,0:T(8,128)(2,1)} %all-gather.3.cloned.1.call-done) | copy-start | bytes 12582916
  165.3 2.3 %copy-start.2 = (bf16[32,4,128,128]{3,2,1,0:T(8,128)(2,1)S(1)}, bf16[32,4,128,128]{3,2,1,0:T(8,128)(2,1)}, u32[]{:S(2)}) copy-start(bf16[32,4,128,128]{3,2,1,0:T(8,128)(2,1)} %all-gather.3.cloned.1.call-done) | copy-start | bytes 12582916
  165.3 2.4 %copy-start.8 = (bf16[256,1024]{1,0:T(8,128)(2,1)S(1)}, bf16[256,1024]{1,0:T(8,128)(2,1)}, u32[]{:S(2)}) copy-start(bf16[256,1024]{1,0:T(8,128)(2,1)} %get-tuple-element.59.refs_0_) | copy-start | bytes 1572868
  (3 other events, 2.4 us)
Sparse Core Ops, SparseCore 0:
  53.3 30.4 reduce-scatter.1
  111.3 31.5 all-gather.2

commit v4 on v3

--- a/solution.py
+++ b/solution.py
@@ -338,11 +338,11 @@
     return by_offset(1, left, right, far, other, other_left, other_right, other_far), begun, other_left, other_far
 
 
-def gather_second(own, other_left_a, other_far_a, sums):
+def gather_second(own, other_left_a, other_far_a):
     up, down, across = ring(1), ring(-1), pair()
     with jax.named_scope("late_shards"):
         left = shift(own, down)
-        other = shift(after(own, other_left_a, sums), across)
+        other = shift(after(own, other_left_a), across)
         right = shift(after(own, other_far_a), up)
     with jax.named_scope("late_shards_on"):
         far, other_left, other_right = shift(left, down), shift(left, across), shift(other, up)
@@ -406,7 +406,7 @@
     late = after(weights, *begun, *dealt[1:])[:, width:]
     mine, theirs = place_sums(place, module_of_path, dealt, modules, [normed, *begun])
     sums = add(mine, lax.ppermute(theirs, "path", cores()))
-    pieces[1], late_begun = gather_second(late, other_left, other_far, sums)
+    pieces[1], late_begun = gather_second(late, other_left, other_far)
     columns = [[(z * Y + y) * CORES + c for z in range(Z_HI)] for y in range(Y) for c in range(CORES)]
     total = lax.psum_scatter(sums, "path", scatter_dimension=0, axis_index_groups=columns, tiled=True)[0]
 

time: 179 us -> 175 us (0.978); the launches traced: 178 us -> 172 us
  starting transfers between devices: 54.4 us -> 49 us
    ppermute x3, starting transfers between devices: 10.3 us -> 7.05 us  [per_device(): lax.ppermute(step, 'path', along_z(k))]
    unnamed x60, local copies, waits for them, and re-layouts: 5.94 us -> 3.34 us
    reduce_scatter x1, waiting for transfers between devices: 0.01 us -> 2.49 us  [per_device(): lax.psum_scatter(sums, 'path', scatter_dimension=0, axis_index_groups=col...]
    ppermute x14, starting transfers between devices: 23.2 us -> 20.9 us  [shift(): return lax.ppermute(value, 'fsdp', way)]
  transfers between devices with their start and end apart: 37 -> 37, of which waited for: 14 -> 16; matrix products, arithmetic and copies ran while one was open for 3% -> 4% of each run, Pallas kernels for 18% -> 18%
where the time goes in v4:
time: 175 us; the launch traced here: 172 us
  waiting for transfers between devices  61.4 us (35%)
  starting transfers between devices  49 us (28%)
  Pallas kernels  34.8 us (20%)
  between operations  14.4 us (8%)
  local copies, waits for them, and re-layouts  7.1 us (4%)
  other arithmetic  4.91 us (3%)
    ppermute x14, waiting for transfers between devices, scatter(): move = lambda value, way: lax.ppermute(value, 'fsdp', way)  32.7 us
    ppermute x14, waiting for transfers between devices, shift(): return lax.ppermute(value, 'fsdp', way)  23.5 us
    pallas_call x2, Pallas kernels, grads(): pl.pallas_call(grad_kernel, grid=(steps,), in_specs=[pl.BlockSpec((rows,...  22.4 us
    ppermute x14, starting transfers between devices, shift(): return lax.ppermute(value, 'fsdp', way)  20.9 us
    ppermute x14, starting transfers between devices, scatter(): move = lambda value, way: lax.ppermute(value, 'fsdp', way)  17.6 us
    ppermute x3, starting transfers between devices, per_device(): lax.ppermute(step, 'path', along_z(k))  7.05 us
    pallas_call x2, Pallas kernels, final(): pl.pallas_call(functools.partial(final_kernel, len(terms), first), grid_s...  5.33 us
    convert_element_type x7, other arithmetic, add(): return total.astype(jnp.bfloat16)  3.91 us
  transfers between devices with their start and end apart: 37, of which 16 were waited for; matrix products, arithmetic and copies ran while one was open for 4% of the time, Pallas kernels for 18%

profile of v4, /device:TPU:24, one launch (start us, length us, event | category | flops | bytes accessed | tf_op | source)
XLA Modules:
  0.0 171.6 jit_solution(7363600998016811874)
XLA Ops:
  7.2 1.9 %slice.8 = bf16[256,1024]{1,0:T(8,128)(2,1)} slice(bf16[256,2048]{1,0:T(8,128)(2,1)} %bitcast.25), slice={[0:256], [0:1024]} | slice | bytes 1048576 | tf_op jit(solution)/shard_map/slice | solution.py:400
  9.2 1.9 %collective-permute-start.2 = (bf16[256,1024]{1,0:T(8,128)(2,1)}, bf16[256,1024]{1,0:T(8,128)(2,1)}, u32[]{:S(2)}, u32[]{:S(2)}) collective-permute-start(bf16[256,1024]{1,0:T(8,128)(2,1)} %slice.8), channel_id=1, source_target_pairs={{0,4},{1,5},{2,6},{3,7},{4,0},{5,1},{6,2},{7,3},{8,12},{9,13},{10,... | collective-permute-start | bytes 1572872 | tf_op jit(solution)/shard_map/shards/ppermute | solution.py:317
  11.1 1.5 collective-permute-start.1
  12.6 1.7 %collective-permute-start = (bf16[256,1024]{1,0:T(8,128)(2,1)}, bf16[256,1024]{1,0:T(8,128)(2,1)}, u32[]{:S(2)}, u32[]{:S(2)}) collective-permute-start(bf16[256,1024]{1,0:T(8,128)(2,1)} %slice.8), channel_id=1, source_target_pairs={{0,3},{1,0},{2,1},{3,2},{4,7},{5,4},{6,5},{7,6},{8,11},{9,8},{10,9... | collective-permute-start | bytes 1572872 | tf_op jit(solution)/shard_map/shards/ppermute | solution.py:317
  14.4 1.4 deal.1
  15.8 0.3 collective-permute-start.7
  16.1 1.8 %collective-permute-start.9 = (bf16[4,256,128]{2,1,0:T(8,128)(2,1)S(1)}, bf16[4,256,128]{2,1,0:T(8,128)(2,1)S(1)}, u32[]{:S(2)}, u32[]{:S(2)}) collective-permute-start(bf16[4,256,128]{2,1,0:T(8,128)(2,1)S(1)} %get-tuple-element.49), channel_id=1, source_target_pairs={{0,48},{8,56},{16,0},{24,8},{32,16},{40,24},{48,32},{56,40},{64,11... | collective-permute-start | bytes 786440 | tf_op jit(solution)/shard_map/ppermute | solution.py:405
  17.9 1.9 %norm.1.n_ref.refs_4_ = bf16[768,2048]{1,0:T(8,128)(2,1)S(1)} custom-call(s32[2]{0:T(128)S(1)} %pad_add_fusion.place_ref, bf16[768,2048]{1,0:T(8,128)(2,1)S(1)} %bitcast.31), custom_call_target="tpu_custom_call" | custom-call | flops 4718592 | bytes 6291456 | tf_op jit(solution)/shard_map/norm/pallas_call | solution.py:69
  19.9 3.5 %collective-permute-done.2.rest_4_.refs_7_ = bf16[256,1024]{1,0:T(8,128)(2,1)} collective-permute-done((bf16[256,1024]{1,0:T(8,128)(2,1)}, bf16[256,1024]{1,0:T(8,128)(2,1)}, u32[]{:S(2)}, u32[]{:S(2)}) %collective-permute-start.2) | collective-permute-done | bytes 524320 | tf_op jit(solution)/shard_map/shards/ppermute | solution.py:317
  23.3 1.2 collective-permute-start.8
  24.6 1.4 collective-permute-done.1.rest_3_.refs_5_
  26.0 0.3 collective-permute-start.5
  26.3 1.5 collective-permute-start.3
  27.8 1.7 %collective-permute-start.4 = (bf16[256,1024]{1,0:T(8,128)(2,1)}, bf16[256,1024]{1,0:T(8,128)(2,1)S(1)}, u32[]{:S(2)}, u32[]{:S(2)}) collective-permute-start(bf16[256,1024]{1,0:T(8,128)(2,1)} %collective-permute-done.2.rest_4_.refs_7_), channel_id=1, source_target_pairs={{0,3},{1,0},{2,1},{3,2},{4,7},{5,4},{6,5},{7,6},{8,11},{9,8},{10,9... | collective-permute-start | bytes 1572872 | tf_op jit(solution)/shard_map/shards_on/ppermute | solution.py:317
  29.6 2.6 %collective-permute-done.8.refs_2_ = bf16[4,256,128]{2,1,0:T(8,128)(2,1)S(1)} collective-permute-done((bf16[4,256,128]{2,1,0:T(8,128)(2,1)S(1)}, bf16[4,256,128]{2,1,0:T(8,128)(2,1)S(1)}, u32[]{:S(2)}, u32[]{:S(2)}) %collective-permute-start.8) | collective-permute-done | bytes 262176 | tf_op jit(solution)/shard_map/ppermute | solution.py:405
  32.2 0.8 slice.7
  33.0 2.8 %collective-permute-start.10 = (bf16[256,1024]{1,0:T(8,128)(2,1)}, bf16[256,1024]{1,0:T(8,128)(2,1)S(1)}, u32[]{:S(2)}, u32[]{:S(2)}) collective-permute-start(bf16[256,1024]{1,0:T(8,128)(2,1)} %slice.7), channel_id=1, source_target_pairs={{0,3},{1,0},{2,1},{3,2},{4,7},{5,4},{6,5},{7,6},{8,11},{9,8},{10,9... | collective-permute-start | bytes 1572872 | tf_op jit(solution)/shard_map/late_shards/ppermute | solution.py:317
  35.8 1.5 place_sums.1
  37.5 1.2 collective-permute-done.5.rest_7_
  38.7 1.4 collective-permute-done.3.rest_2_
  40.1 2.8 %collective-permute-done.4.rest_5_ = bf16[256,1024]{1,0:T(8,128)(2,1)S(1)} collective-permute-done((bf16[256,1024]{1,0:T(8,128)(2,1)}, bf16[256,1024]{1,0:T(8,128)(2,1)S(1)}, u32[]{:S(2)}, u32[]{:S(2)}) %collective-permute-start.4) | collective-permute-done | bytes 524320 | tf_op jit(solution)/shard_map/shards_on/ppermute | solution.py:317
  42.9 1.5 collective-permute-start.6
  44.4 1.4 collective-permute-start.11
  45.8 5.4 %collective-permute-done.10.rest_8_.rest_1_ = bf16[256,1024]{1,0:T(8,128)(2,1)S(1)} collective-permute-done((bf16[256,1024]{1,0:T(8,128)(2,1)}, bf16[256,1024]{1,0:T(8,128)(2,1)S(1)}, u32[]{:S(2)}, u32[]{:S(2)}) %collective-permute-start.10) | collective-permute-done | bytes 524320 | tf_op jit(solution)/shard_map/late_shards/ppermute | solution.py:317
  51.2 1.4 collective-permute-start.14
  52.6 0.9 add_convert_fusion.6
  53.6 1.0 copy.15.mask_ref
  54.6 3.3 %collective-permute-start.12 = (bf16[256,1024]{1,0:T(8,128)(2,1)S(1)}, bf16[256,1024]{1,0:T(8,128)(2,1)S(1)}, u32[]{:S(2)}, u32[]{:S(2)}) collective-permute-start(bf16[256,1024]{1,0:T(8,128)(2,1)S(1)} %collective-permute-done.10.rest_8_.rest_1_), channel_id=1, source_target_pairs={{0,3},{1,0},{2,1},{3,2},{4,7},{5,4},{6,5},{7,6},{8,11},{9,8},{10,9... | collective-permute-start | bytes 1572872 | tf_op jit(solution)/shard_map/late_shards_on/ppermute | solution.py:317
  58.0 6.9 %collective-permute-done.14.rest_5_ = bf16[256,1024]{1,0:T(8,128)(2,1)S(1)} collective-permute-done((bf16[256,1024]{1,0:T(8,128)(2,1)S(1)}, bf16[256,1024]{1,0:T(8,128)(2,1)S(1)}, u32[]{:S(2)}, u32[]{:S(2)}) %collective-permute-start.14) | collective-permute-done | bytes 524320 | tf_op jit(solution)/shard_map/late_shards_on/ppermute | solution.py:317
  65.0 1.7 %collective-permute-start.15 = (bf16[256,1024]{1,0:T(8,128)(2,1)S(1)}, bf16[256,1024]{1,0:T(8,128)(2,1)}, u32[]{:S(2)}, u32[]{:S(2)}) collective-permute-start(bf16[256,1024]{1,0:T(8,128)(2,1)S(1)} %collective-permute-done.14.rest_5_), channel_id=1, source_target_pairs={{0,3},{1,0},{2,1},{3,2},{4,7},{5,4},{6,5},{7,6},{8,11},{9,8},{10,9... | collective-permute-start | bytes 1572872 | tf_op jit(solution)/shard_map/late_shards_last/ppermute | solution.py:317
  66.8 11.5 %grads.2 = (bf16[272,1024]{1,0:T(8,128)(2,1)}, bf16[272,1024]{1,0:T(8,128)(2,1)}, bf16[272,1024]{1,0:T(8,128)(2,1)}, bf16[272,1024]{1,0:T(8,128)(2,1)}, bf16[272...) custom-call(bf16[768,2048]{1,0:T(8,128)(2,1)} %copy-done.3, ...), custom_call_target="tpu_custom_call" | custom-call | flops 6442450944 | bytes 13107200 | tf_op jit(solution)/shard_map/grads/pallas_call | solution.py:113
  78.3 1.9 %collective-permute-start.21 = (bf16[272,1024]{1,0:T(8,128)(2,1)}, bf16[272,1024]{1,0:T(8,128)(2,1)S(1)}, u32[]{:S(2)}, u32[]{:S(2)}) collective-permute-start(bf16[272,1024]{1,0:T(8,128)(2,1)} %get-tuple-element.60), channel_id=1, source_target_pairs={{0,3},{1,0},{2,1},{3,2},{4,7},{5,4},{6,5},{7,6},{8,11},{9,8},{10,9... | collective-permute-start | bytes 1671176 | tf_op jit(solution)/shard_map/sum_far_other/ppermute | solution.py:363
  80.4 0.9 collective-permute-done.16.rest_7_
  81.3 2.5 %reduce-scatter.2.cloned.1.call-done = bf16[1,4,128,128]{3,2,1,0:T(8,128)(2,1)} async-done(((bf16[4,4,128,128]{3,2,1,0:T(8,128)(2,1)}), bf16[1,4,128,128]{3,2,1,0:T(8,128)(2,1)}) %reduce-scatter.2.cloned.1.call-update) | async-done | bytes 131088 | tf_op jit(solution)/shard_map/reduce_scatter | solution.py:411
  83.8 0.9 copy-done.11
  84.7 2.3 %outer.1 = (f32[4,64,256]{2,1,0:T(8,128)}, f32[4,64,256]{2,1,0:T(8,128)}, bf16[4,128,128]{2,1,0:T(8,128)(2,1)S(1)}) custom-call(s32[4]{0:T(128)S(1)} %copy-done.13, bf16[4,128,128]{2,1,0:T(8,128)(2,1)S(1)} %bitcast.34, f32[4,64,256]{2,1,0:T(8,128)S(1)} %bitcast.32, f32[4,64,256]{2,1,0:T(8,128)S(1)} %bitcast.33), custom_call_target="tpu_custom_call" | custom-call | flops 524288 | bytes 2097152 | tf_op jit(solution)/shard_map/outer/pallas_call | solution.py:232
  86.9 3.2 %collective-permute-start.20 = (bf16[4,128,128]{2,1,0:T(8,128)(2,1)S(1)}, bf16[4,128,128]{2,1,0:T(8,128)(2,1)S(1)}, u32[]{:S(2)}, u32[]{:S(2)}) collective-permute-start(bf16[4,128,128]{2,1,0:T(8,128)(2,1)S(1)} %get-tuple-element.58), channel_id=1, source_target_pairs={{0,192},{8,200},{16,208},{24,216},{32,224},{40,232},{48,240},{56,2... | collective-permute-start | bytes 393224 | tf_op jit(solution)/shard_map/steps_along_z/ppermute | solution.py:422
  90.2 2.2 %collective-permute-start.19 = (bf16[4,128,128]{2,1,0:T(8,128)(2,1)S(1)}, bf16[4,128,128]{2,1,0:T(8,128)(2,1)S(1)}, u32[]{:S(2)}, u32[]{:S(2)}) collective-permute-start(bf16[4,128,128]{2,1,0:T(8,128)(2,1)S(1)} %get-tuple-element.58), channel_id=1, source_target_pairs={{0,128},{8,136},{16,144},{24,152},{32,160},{40,168},{48,176},{56,1... | collective-permute-start | bytes 393224 | tf_op jit(solution)/shard_map/steps_along_z/ppermute | solution.py:422
  92.4 1.6 collective-permute-start.18
  94.0 10.9 %grads.3 = (bf16[256,1024]{1,0:T(8,128)(2,1)}, bf16[256,1024]{1,0:T(8,128)(2,1)}, bf16[256,1024]{1,0:T(8,128)(2,1)}, bf16[256,1024]{1,0:T(8,128)(2,1)}, bf16[256...) custom-call(bf16[768,2048]{1,0:T(8,128)(2,1)} %copy-done.3, ...), custom_call_target="tpu_custom_call" | custom-call | flops 6442450944 | bytes 13107200 | tf_op jit(solution)/shard_map/grads/pallas_call | solution.py:113
  104.9 0.9 pad_maximum_fusion
  105.9 2.6 %collective-permute-start.23 = (bf16[256,1024]{1,0:T(8,128)(2,1)}, bf16[256,1024]{1,0:T(8,128)(2,1)S(1)}, u32[]{:S(2)}, u32[]{:S(2)}) collective-permute-start(bf16[256,1024]{1,0:T(8,128)(2,1)} %get-tuple-element.64), channel_id=1, source_target_pairs={{0,3},{1,0},{2,1},{3,2},{4,7},{5,4},{6,5},{7,6},{8,11},{9,8},{10,9... | collective-permute-start | bytes 1572872 | tf_op jit(solution)/shard_map/sum_near_other/ppermute | solution.py:363
  108.5 3.2 %collective-permute-start.32 = (bf16[272,1024]{1,0:T(8,128)(2,1)S(1)}, bf16[272,1024]{1,0:T(8,128)(2,1)S(1)}, u32[]{:S(2)}, u32[]{:S(2)}) collective-permute-start(bf16[272,1024]{1,0:T(8,128)(2,1)S(1)} %copy-done.21), channel_id=1, source_target_pairs={{0,3},{1,0},{2,1},{3,2},{4,7},{5,4},{6,5},{7,6},{8,11},{9,8},{10,9... | collective-permute-start | bytes 1671176 | tf_op jit(solution)/shard_map/sum_far/ppermute | solution.py:363
  111.7 0.2 add_convert_fusion.1
  111.9 1.1 collective-permute-start.33
  113.0 0.2 add_convert_fusion.2
  113.2 7.9 %collective-permute-done.23 = bf16[256,1024]{1,0:T(8,128)(2,1)S(1)} collective-permute-done((bf16[256,1024]{1,0:T(8,128)(2,1)}, bf16[256,1024]{1,0:T(8,128)(2,1)S(1)}, u32[]{:S(2)}, u32[]{:S(2)}) %collective-permute-start.23) | collective-permute-done | bytes 524320 | tf_op jit(solution)/shard_map/sum_near_other/ppermute | solution.py:363
  121.2 3.6 %collective-permute-done.26 = bf16[256,1024]{1,0:T(8,128)(2,1)S(1)} collective-permute-done((bf16[256,1024]{1,0:T(8,128)(2,1)}, bf16[256,1024]{1,0:T(8,128)(2,1)S(1)}, u32[]{:S(2)}, u32[]{:S(2)}) %collective-permute-start.26) | collective-permute-done | bytes 524320 | tf_op jit(solution)/shard_map/sum_far_other/ppermute | solution.py:363
  125.0 1.1 collective-permute-start.28
  126.0 1.0 add_convert_fusion.5
  127.0 3.2 %collective-permute-done.32 = bf16[272,1024]{1,0:T(8,128)(2,1)S(1)} collective-permute-done((bf16[272,1024]{1,0:T(8,128)(2,1)S(1)}, bf16[272,1024]{1,0:T(8,128)(2,1)S(1)}, u32[]{:S(2)}, u32[]{:S(2)}) %collective-permute-start.32) | collective-permute-done | bytes 557088 | tf_op jit(solution)/shard_map/sum_far/ppermute | solution.py:363
  130.3 1.8 %collective-permute-start.31 = (bf16[272,1024]{1,0:T(8,128)(2,1)S(1)}, bf16[272,1024]{1,0:T(8,128)(2,1)S(1)}, u32[]{:S(2)}, u32[]{:S(2)}) collective-permute-start(bf16[272,1024]{1,0:T(8,128)(2,1)S(1)} %add_convert_fusion.2), channel_id=1, source_target_pairs={{0,4},{1,5},{2,6},{3,7},{4,0},{5,1},{6,2},{7,3},{8,12},{9,13},{10,... | collective-permute-start | bytes 1671176 | tf_op jit(solution)/shard_map/sum_cross/ppermute | solution.py:363
  132.1 2.8 %collective-permute-start.24 = (bf16[256,1024]{1,0:T(8,128)(2,1)}, bf16[256,1024]{1,0:T(8,128)(2,1)}, u32[]{:S(2)}, u32[]{:S(2)}) collective-permute-start(bf16[256,1024]{1,0:T(8,128)(2,1)} %get-tuple-element.65), channel_id=1, source_target_pairs={{0,3},{1,0},{2,1},{3,2},{4,7},{5,4},{6,5},{7,6},{8,11},{9,8},{10,9... | collective-permute-start | bytes 1572872 | tf_op jit(solution)/shard_map/sum_near/ppermute | solution.py:363
  134.9 0.3 add_convert_fusion
  135.2 9.8 %collective-permute-done.27 = bf16[256,1024]{1,0:T(8,128)(2,1)S(1)} collective-permute-done((bf16[256,1024]{1,0:T(8,128)(2,1)S(1)}, bf16[256,1024]{1,0:T(8,128)(2,1)S(1)}, u32[]{:S(2)}, u32[]{:S(2)}) %collective-permute-start.27) | collective-permute-done | bytes 524320 | tf_op jit(solution)/shard_map/sum_far/ppermute | solution.py:363
  144.9 0.9 collective-permute-start.25
  145.8 0.7 collective-permute-start.34
  146.5 1.1 add_convert_fusion.3
  147.6 1.3 collective-permute-start.29
  148.9 0.6 collective-permute-done.31.refs_2_
  149.5 7.6 %collective-permute-done.34.refs_3_ = bf16[272,1024]{1,0:T(8,128)(2,1)S(1)} collective-permute-done((bf16[272,1024]{1,0:T(8,128)(2,1)S(1)}, bf16[272,1024]{1,0:T(8,128)(2,1)S(1)}, u32[]{:S(2)}, u32[]{:S(2)}) %collective-permute-start.34) | collective-permute-done | bytes 557088 | tf_op jit(solution)/shard_map/sum_side/ppermute | solution.py:363
  157.1 2.2 %copy-done.1 = bf16[32,4,128,128]{3,2,1,0:T(8,128)(2,1)S(1)} copy-done((bf16[32,4,128,128]{3,2,1,0:T(8,128)(2,1)S(1)}, bf16[32,4,128,128]{3,2,1,0:T(8,128)(2,1)}, u32[]{:S(2)}) %copy-start.1) | copy-done | bytes 4194328
  159.3 2.2 %final.2 = (bf16[256,2048]{1,0:T(8,128)(2,1)}, f32[8,128]{1,0:T(8,128)S(1)}) custom-call(s32[2]{0:T(128)S(1)} %pad_add_fusion.place_ref, s32[32]{0:T(128)S(1)} %copy-done.12, bf16[256,2048]{1,0:T(8,128)(2,1)S(1)} %bitcast.29, bf16[8,4,4,128,128]{4,3,2,1,0:T(8,128)(2,1)S(1)} %bitcast.23, bf16[272,1024]{1,0:T(8,128)(2,1)S(1)} %copy-done.7, ...), custom_call_target="tpu_custom_call" | custom-call | flops 2097152 | bytes 3670016 | tf_op jit(solution)/shard_map/final/pallas_call | solution.py:291
  161.7 3.1 %final.3 = bf16[256,2048]{1,0:T(8,128)(2,1)} custom-call(s32[2]{0:T(128)S(1)} %pad_add_fusion.place_ref, s32[32]{0:T(128)S(1)} %copy-done.12, bf16[256,2048]{1,0:T(8,128)(2,1)S(1)} %bitcast.30, bf16[8,4,4,128,128]{4,3,2,1,0:T(8,128)(2,1)S(1)} %bitcast.24, bf16[256,1024]{1,0:T(8,128)(2,1)S(1)} %copy-done.8, ...), custom_call_target="tpu_custom_call", output_to_operand_aliasing={{}: (9, {})} | custom-call | flops 2097152 | bytes 3670016 | tf_op jit(solution)/shard_map/final/pallas_call | solution.py:291
  (93 shorter events, 1.1 us)
Async XLA Ops:
  7.2 7.2 %copy-start = (bf16[1,256,2048]{2,1,0:T(8,128)(2,1)S(1)}, bf16[1,256,2048]{2,1,0:T(8,128)(2,1)}, u32[]{:S(2)}) copy-start(bf16[1,256,2048]{2,1,0:T(8,128)(2,1)} %param.13) | copy-start | bytes 3145732
  7.2 76.6 %reduce-scatter.2.cloned.1.call-start = ((), (), s32[]{:S(2)}) async-start(), calls=%async_computation.1 | async-start | bytes 655360 | tf_op jit(solution)/shard_map/reduce_scatter | solution.py:411
  9.2 14.2 %collective-permute-start.2 = (bf16[256,1024]{1,0:T(8,128)(2,1)}, bf16[256,1024]{1,0:T(8,128)(2,1)}, u32[]{:S(2)}, u32[]{:S(2)}) collective-permute-start(bf16[256,1024]{1,0:T(8,128)(2,1)} %slice.8), channel_id=1, source_target_pairs={{0,4},{1,5},{2,6},{3,7},{4,0},{5,1},{6,2},{7,3},{8,12},{9,13},{10,... | collective-permute-start | bytes 1572872 | tf_op jit(solution)/shard_map/shards/ppermute | solution.py:317
  11.1 14.9 %collective-permute-start.1 = (bf16[256,1024]{1,0:T(8,128)(2,1)}, bf16[256,1024]{1,0:T(8,128)(2,1)}, u32[]{:S(2)}, u32[]{:S(2)}) collective-permute-start(bf16[256,1024]{1,0:T(8,128)(2,1)} %slice.8), channel_id=1, source_target_pairs={{0,1},{1,2},{2,3},{3,0},{4,5},{5,6},{6,7},{7,4},{8,9},{9,10},{10,1... | collective-permute-start | bytes 1572872 | tf_op jit(solution)/shard_map/shards/ppermute | solution.py:317
  12.6 13.4 %collective-permute-start = (bf16[256,1024]{1,0:T(8,128)(2,1)}, bf16[256,1024]{1,0:T(8,128)(2,1)}, u32[]{:S(2)}, u32[]{:S(2)}) collective-permute-start(bf16[256,1024]{1,0:T(8,128)(2,1)} %slice.8), channel_id=1, source_target_pairs={{0,3},{1,0},{2,1},{3,2},{4,7},{5,4},{6,5},{7,6},{8,11},{9,8},{10,9... | collective-permute-start | bytes 1572872 | tf_op jit(solution)/shard_map/shards/ppermute | solution.py:317
  14.4 3.5 %copy-start.6 = (bf16[1,768,2048]{2,1,0:T(8,128)(2,1)S(1)}, bf16[1,768,2048]{2,1,0:T(8,128)(2,1)}, u32[]{:S(2)}) copy-start(bf16[1,768,2048]{2,1,0:T(8,128)(2,1)} %param.9) | copy-start | bytes 9437188
  15.8 12.0 %collective-permute-start.7 = (bf16[4,256,128]{2,1,0:T(8,128)(2,1)S(1)}, bf16[4,256,128]{2,1,0:T(8,128)(2,1)S(1)}, u32[]{:S(2)}, u32[]{:S(2)}) collective-permute-start(bf16[4,256,128]{2,1,0:T(8,128)(2,1)S(1)} %get-tuple-element.46), channel_id=1, source_target_pairs={{0,16},{8,24},{16,32},{24,40},{32,48},{40,56},{48,0},{56,8},{64,80... | collective-permute-start | bytes 786440 | tf_op jit(solution)/shard_map/ppermute | solution.py:405
  16.1 13.5 %collective-permute-start.9 = (bf16[4,256,128]{2,1,0:T(8,128)(2,1)S(1)}, bf16[4,256,128]{2,1,0:T(8,128)(2,1)S(1)}, u32[]{:S(2)}, u32[]{:S(2)}) collective-permute-start(bf16[4,256,128]{2,1,0:T(8,128)(2,1)S(1)} %get-tuple-element.49), channel_id=1, source_target_pairs={{0,48},{8,56},{16,0},{24,8},{32,16},{40,24},{48,32},{56,40},{64,11... | collective-permute-start | bytes 786440 | tf_op jit(solution)/shard_map/ppermute | solution.py:405
  17.9 14.3 %copy-start.4 = (bf16[1,256,2048]{2,1,0:T(8,128)(2,1)S(1)}, bf16[1,256,2048]{2,1,0:T(8,128)(2,1)}, u32[]{:S(2)}) copy-start(bf16[1,256,2048]{2,1,0:T(8,128)(2,1)} %param.12) | copy-start | bytes 3145732
  17.9 17.9 %copy-start.12 = (s32[32]{0:T(128)S(1)}, s32[32]{0:T(128)}, u32[]{:S(2)}) copy-start(s32[32]{0:T(128)} %module_ref.5) | copy-start | bytes 388
  19.8 17.5 %copy-start.3 = (bf16[768,2048]{1,0:T(8,128)(2,1)}, bf16[768,2048]{1,0:T(8,128)(2,1)S(1)}, u32[]{:S(2)}) copy-start(bf16[768,2048]{1,0:T(8,128)(2,1)S(1)} %norm.1.n_ref.refs_4_) | copy-start | bytes 9437188
  23.3 8.9 %collective-permute-start.8 = (bf16[4,256,128]{2,1,0:T(8,128)(2,1)S(1)}, bf16[4,256,128]{2,1,0:T(8,128)(2,1)S(1)}, u32[]{:S(2)}, u32[]{:S(2)}) collective-permute-start(bf16[4,256,128]{2,1,0:T(8,128)(2,1)S(1)} %get-tuple-element.48), channel_id=1, source_target_pairs={{0,32},{8,40},{16,48},{24,56},{32,0},{40,8},{48,16},{56,24},{64,96... | collective-permute-start | bytes 786440 | tf_op jit(solution)/shard_map/ppermute | solution.py:405
  26.0 12.7 %collective-permute-start.5 = (bf16[256,1024]{1,0:T(8,128)(2,1)}, bf16[256,1024]{1,0:T(8,128)(2,1)S(1)}, u32[]{:S(2)}, u32[]{:S(2)}) collective-permute-start(bf16[256,1024]{1,0:T(8,128)(2,1)} %collective-permute-done.1.rest_3_.refs_5_), channel_id=1, source_target_pairs={{0,4},{1,5},{2,6},{3,7},{4,0},{5,1},{6,2},{7,3},{8,12},{9,13},{10,... | collective-permute-start | bytes 1572872 | tf_op jit(solution)/shard_map/shards_on/ppermute | solution.py:317
  26.3 13.8 %collective-permute-start.3 = (bf16[256,1024]{1,0:T(8,128)(2,1)}, bf16[256,1024]{1,0:T(8,128)(2,1)S(1)}, u32[]{:S(2)}, u32[]{:S(2)}) collective-permute-start(bf16[256,1024]{1,0:T(8,128)(2,1)} %collective-permute-done.1.rest_3_.refs_5_), channel_id=1, source_target_pairs={{0,1},{1,2},{2,3},{3,0},{4,5},{5,6},{6,7},{7,4},{8,9},{9,10},{10,1... | collective-permute-start | bytes 1572872 | tf_op jit(solution)/shard_map/shards_on/ppermute | solution.py:317
  27.8 15.1 %collective-permute-start.4 = (bf16[256,1024]{1,0:T(8,128)(2,1)}, bf16[256,1024]{1,0:T(8,128)(2,1)S(1)}, u32[]{:S(2)}, u32[]{:S(2)}) collective-permute-start(bf16[256,1024]{1,0:T(8,128)(2,1)} %collective-permute-done.2.rest_4_.refs_7_), channel_id=1, source_target_pairs={{0,3},{1,0},{2,1},{3,2},{4,7},{5,4},{6,5},{7,6},{8,11},{9,8},{10,9... | collective-permute-start | bytes 1572872 | tf_op jit(solution)/shard_map/shards_on/ppermute | solution.py:317
  33.0 18.2 %collective-permute-start.10 = (bf16[256,1024]{1,0:T(8,128)(2,1)}, bf16[256,1024]{1,0:T(8,128)(2,1)S(1)}, u32[]{:S(2)}, u32[]{:S(2)}) collective-permute-start(bf16[256,1024]{1,0:T(8,128)(2,1)} %slice.7), channel_id=1, source_target_pairs={{0,3},{1,0},{2,1},{3,2},{4,7},{5,4},{6,5},{7,6},{8,11},{9,8},{10,9... | collective-permute-start | bytes 1572872 | tf_op jit(solution)/shard_map/late_shards/ppermute | solution.py:317
  37.4 16.2 %copy-start.20 = (s32[1,768]{1,0:T(1,128)S(1)}, s32[1,768]{1,0:T(1,128)}, u32[]{:S(2)}) copy-start(s32[1,768]{1,0:T(1,128)} %param.11) | copy-start | bytes 9220
  37.4 15.2 %collective-permute-start.17 = (bf16[4,4,128,128]{3,2,1,0:T(8,128)(2,1)S(1)}, bf16[4,4,128,128]{3,2,1,0:T(8,128)(2,1)S(1)}, u32[]{:S(2)}, u32[]{:S(2)}) collective-permute-start(bf16[4,4,128,128]{3,2,1,0:T(8,128)(2,1)S(1)} %get-tuple-element.57), channel_id=1, source_target_pairs={{0,8},{8,0},{16,24},{24,16},{32,40},{40,32},{48,56},{56,48},{64,72... | collective-permute-start | bytes 1572872 | tf_op jit(solution)/shard_map/ppermute | solution.py:408
  38.7 15.9 %copy-start.24 = (bf16[256,1024]{1,0:T(8,128)(2,1)}, bf16[256,1024]{1,0:T(8,128)(2,1)S(1)}, u32[]{:S(2)}) copy-start(bf16[256,1024]{1,0:T(8,128)(2,1)S(1)} %collective-permute-done.5.rest_7_) | copy-start | bytes 1572868
  40.1 14.5 %copy-start.25 = (bf16[256,1024]{1,0:T(8,128)(2,1)}, bf16[256,1024]{1,0:T(8,128)(2,1)S(1)}, u32[]{:S(2)}) copy-start(bf16[256,1024]{1,0:T(8,128)(2,1)S(1)} %collective-permute-done.3.rest_2_) | copy-start | bytes 1572868
  42.9 11.7 %copy-start.28 = (bf16[256,1024]{1,0:T(8,128)(2,1)}, bf16[256,1024]{1,0:T(8,128)(2,1)S(1)}, u32[]{:S(2)}) copy-start(bf16[256,1024]{1,0:T(8,128)(2,1)S(1)} %collective-permute-done.4.rest_5_) | copy-start | bytes 1572868
  42.9 15.1 %collective-permute-start.6 = (bf16[256,1024]{1,0:T(8,128)(2,1)S(1)}, bf16[256,1024]{1,0:T(8,128)(2,1)}, u32[]{:S(2)}, u32[]{:S(2)}) collective-permute-start(bf16[256,1024]{1,0:T(8,128)(2,1)S(1)} %collective-permute-done.5.rest_7_), channel_id=1, source_target_pairs={{0,1},{1,2},{2,3},{3,0},{4,5},{5,6},{6,7},{7,4},{8,9},{9,10},{10,1... | collective-permute-start | bytes 1572872 | tf_op jit(solution)/shard_map/shards_last/ppermute | solution.py:317
  44.4 13.6 %collective-permute-start.11 = (bf16[256,1024]{1,0:T(8,128)(2,1)}, bf16[256,1024]{1,0:T(8,128)(2,1)S(1)}, u32[]{:S(2)}, u32[]{:S(2)}) collective-permute-start(bf16[256,1024]{1,0:T(8,128)(2,1)} %slice.7), channel_id=1, source_target_pairs={{0,4},{1,5},{2,6},{3,7},{4,0},{5,1},{6,2},{7,3},{8,12},{9,13},{10,... | collective-permute-start | bytes 1572872 | tf_op jit(solution)/shard_map/late_shards/ppermute | solution.py:317
  51.2 3.4 %copy-start.22 = (bf16[256,1024]{1,0:T(8,128)(2,1)}, bf16[256,1024]{1,0:T(8,128)(2,1)S(1)}, u32[]{:S(2)}) copy-start(bf16[256,1024]{1,0:T(8,128)(2,1)S(1)} %collective-permute-done.10.rest_8_.rest_1_) | copy-start | bytes 1572868
  51.2 13.8 %collective-permute-start.14 = (bf16[256,1024]{1,0:T(8,128)(2,1)S(1)}, bf16[256,1024]{1,0:T(8,128)(2,1)S(1)}, u32[]{:S(2)}, u32[]{:S(2)}) collective-permute-start(bf16[256,1024]{1,0:T(8,128)(2,1)S(1)} %collective-permute-done.10.rest_8_.rest_1_), channel_id=1, source_target_pairs={{0,4},{1,5},{2,6},{3,7},{4,0},{5,1},{6,2},{7,3},{8,12},{9,13},{10,... | collective-permute-start | bytes 1572872 | tf_op jit(solution)/shard_map/late_shards_on/ppermute | solution.py:317
  53.6 103.5 %all-gather.3.cloned.1.call-start = ((), (), s32[]{:S(2)}) async-start(), calls=%async_computation.2 | async-start | bytes 4718592 | tf_op jit(solution)/shard_map/all_gather | solution.py:427
  54.6 25.6 %collective-permute-start.12 = (bf16[256,1024]{1,0:T(8,128)(2,1)S(1)}, bf16[256,1024]{1,0:T(8,128)(2,1)S(1)}, u32[]{:S(2)}, u32[]{:S(2)}) collective-permute-start(bf16[256,1024]{1,0:T(8,128)(2,1)S(1)} %collective-permute-done.10.rest_8_.rest_1_), channel_id=1, source_target_pairs={{0,3},{1,0},{2,1},{3,2},{4,7},{5,4},{6,5},{7,6},{8,11},{9,8},{10,9... | collective-permute-start | bytes 1572872 | tf_op jit(solution)/shard_map/late_shards_on/ppermute | solution.py:317
  57.9 23.3 %collective-permute-start.13 = (bf16[256,1024]{1,0:T(8,128)(2,1)}, bf16[256,1024]{1,0:T(8,128)(2,1)}, u32[]{:S(2)}, u32[]{:S(2)}) collective-permute-start(bf16[256,1024]{1,0:T(8,128)(2,1)} %slice.7), channel_id=1, source_target_pairs={{0,1},{1,2},{2,3},{3,0},{4,5},{5,6},{6,7},{7,4},{8,9},{9,10},{10,1... | collective-permute-start | bytes 1572872 | tf_op jit(solution)/shard_map/late_shards/ppermute | solution.py:317
  57.9 8.8 %copy-start.23 = (bf16[256,1024]{1,0:T(8,128)(2,1)}, bf16[256,1024]{1,0:T(8,128)(2,1)S(1)}, u32[]{:S(2)}) copy-start(bf16[256,1024]{1,0:T(8,128)(2,1)S(1)} %collective-permute-done.11.rest_9_.rest_4_) | copy-start | bytes 1572868
  58.0 23.3 %collective-permute-start.16 = (bf16[256,1024]{1,0:T(8,128)(2,1)S(1)}, bf16[256,1024]{1,0:T(8,128)(2,1)}, u32[]{:S(2)}, u32[]{:S(2)}) collective-permute-start(bf16[256,1024]{1,0:T(8,128)(2,1)S(1)} %collective-permute-done.11.rest_9_.rest_4_), channel_id=1, source_target_pairs={{0,1},{1,2},{2,3},{3,0},{4,5},{5,6},{6,7},{7,4},{8,9},{9,10},{10,1... | collective-permute-start | bytes 1572872 | tf_op jit(solution)/shard_map/late_shards_on/ppermute | solution.py:317
  65.0 13.3 %copy-start.26 = (bf16[256,1024]{1,0:T(8,128)(2,1)}, bf16[256,1024]{1,0:T(8,128)(2,1)S(1)}, u32[]{:S(2)}) copy-start(bf16[256,1024]{1,0:T(8,128)(2,1)S(1)} %collective-permute-done.14.rest_5_) | copy-start | bytes 1572868
  65.0 16.3 %collective-permute-start.15 = (bf16[256,1024]{1,0:T(8,128)(2,1)S(1)}, bf16[256,1024]{1,0:T(8,128)(2,1)}, u32[]{:S(2)}, u32[]{:S(2)}) collective-permute-start(bf16[256,1024]{1,0:T(8,128)(2,1)S(1)} %collective-permute-done.14.rest_5_), channel_id=1, source_target_pairs={{0,3},{1,0},{2,1},{3,2},{4,7},{5,4},{6,5},{7,6},{8,11},{9,8},{10,9... | collective-permute-start | bytes 1572872 | tf_op jit(solution)/shard_map/late_shards_last/ppermute | solution.py:317
  66.7 17.0 %copy-start.9 = (f32[4,256,64]{1,2,0:T(8,128)S(1)}, f32[4,256,64]{1,2,0:T(8,128)}, u32[]{:S(2)}) copy-start(f32[4,256,64]{1,2,0:T(8,128)} %param.14) | copy-start | bytes 786436
  66.7 17.0 %copy-start.10 = (f32[4,256,64]{1,2,0:T(8,128)S(1)}, f32[4,256,64]{1,2,0:T(8,128)}, u32[]{:S(2)}) copy-start(f32[4,256,64]{1,2,0:T(8,128)} %param.15) | copy-start | bytes 786436
  66.8 17.0 %copy-start.13 = (s32[4]{0:T(128)S(1)}, s32[4]{0:T(128)}, u32[]{:S(2)}) copy-start(s32[4]{0:T(128)} %count_ref) | copy-start | bytes 52
  78.3 27.5 %collective-permute-start.21 = (bf16[272,1024]{1,0:T(8,128)(2,1)}, bf16[272,1024]{1,0:T(8,128)(2,1)S(1)}, u32[]{:S(2)}, u32[]{:S(2)}) collective-permute-start(bf16[272,1024]{1,0:T(8,128)(2,1)} %get-tuple-element.60), channel_id=1, source_target_pairs={{0,3},{1,0},{2,1},{3,2},{4,7},{5,4},{6,5},{7,6},{8,11},{9,8},{10,9... | collective-permute-start | bytes 1671176 | tf_op jit(solution)/shard_map/sum_far_other/ppermute | solution.py:363
  80.2 25.6 %collective-permute-start.22 = (bf16[272,1024]{1,0:T(8,128)(2,1)}, bf16[272,1024]{1,0:T(8,128)(2,1)S(1)}, u32[]{:S(2)}, u32[]{:S(2)}) collective-permute-start(bf16[272,1024]{1,0:T(8,128)(2,1)} %get-tuple-element.61), channel_id=1, source_target_pairs={{0,1},{1,2},{2,3},{3,0},{4,5},{5,6},{6,7},{7,4},{8,9},{9,10},{10,1... | collective-permute-start | bytes 1671176 | tf_op jit(solution)/shard_map/sum_near_other/ppermute | solution.py:363
  86.9 17.9 %collective-permute-start.20 = (bf16[4,128,128]{2,1,0:T(8,128)(2,1)S(1)}, bf16[4,128,128]{2,1,0:T(8,128)(2,1)S(1)}, u32[]{:S(2)}, u32[]{:S(2)}) collective-permute-start(bf16[4,128,128]{2,1,0:T(8,128)(2,1)S(1)} %get-tuple-element.58), channel_id=1, source_target_pairs={{0,192},{8,200},{16,208},{24,216},{32,224},{40,232},{48,240},{56,2... | collective-permute-start | bytes 393224 | tf_op jit(solution)/shard_map/steps_along_z/ppermute | solution.py:422
  90.2 14.7 %collective-permute-start.19 = (bf16[4,128,128]{2,1,0:T(8,128)(2,1)S(1)}, bf16[4,128,128]{2,1,0:T(8,128)(2,1)S(1)}, u32[]{:S(2)}, u32[]{:S(2)}) collective-permute-start(bf16[4,128,128]{2,1,0:T(8,128)(2,1)S(1)} %get-tuple-element.58), channel_id=1, source_target_pairs={{0,128},{8,136},{16,144},{24,152},{32,160},{40,168},{48,176},{56,1... | collective-permute-start | bytes 393224 | tf_op jit(solution)/shard_map/steps_along_z/ppermute | solution.py:422
  92.4 12.5 %collective-permute-start.18 = (bf16[4,128,128]{2,1,0:T(8,128)(2,1)S(1)}, bf16[4,128,128]{2,1,0:T(8,128)(2,1)S(1)}, u32[]{:S(2)}, u32[]{:S(2)}) collective-permute-start(bf16[4,128,128]{2,1,0:T(8,128)(2,1)S(1)} %get-tuple-element.58), channel_id=1, source_target_pairs={{0,64},{8,72},{16,80},{24,88},{32,96},{40,104},{48,112},{56,120},{... | collective-permute-start | bytes 393224 | tf_op jit(solution)/shard_map/steps_along_z/ppermute | solution.py:422
  104.8 3.6 %copy-start.21 = (bf16[272,1024]{1,0:T(8,128)(2,1)S(1)}, bf16[272,1024]{1,0:T(8,128)(2,1)}, u32[]{:S(2)}) copy-start(bf16[272,1024]{1,0:T(8,128)(2,1)} %get-tuple-element.77) | copy-start | bytes 1671172
  104.9 6.8 %copy-start.16 = (bf16[272,1024]{1,0:T(8,128)(2,1)S(1)}, bf16[272,1024]{1,0:T(8,128)(2,1)}, u32[]{:S(2)}) copy-start(bf16[272,1024]{1,0:T(8,128)(2,1)} %get-tuple-element.78) | copy-start | bytes 1671172
  105.8 7.2 %copy-start.15 = (bf16[272,1024]{1,0:T(8,128)(2,1)S(1)}, bf16[272,1024]{1,0:T(8,128)(2,1)}, u32[]{:S(2)}) copy-start(bf16[272,1024]{1,0:T(8,128)(2,1)} %get-tuple-element.74) | copy-start | bytes 1671172
  105.9 15.3 %collective-permute-start.23 = (bf16[256,1024]{1,0:T(8,128)(2,1)}, bf16[256,1024]{1,0:T(8,128)(2,1)S(1)}, u32[]{:S(2)}, u32[]{:S(2)}) collective-permute-start(bf16[256,1024]{1,0:T(8,128)(2,1)} %get-tuple-element.64), channel_id=1, source_target_pairs={{0,3},{1,0},{2,1},{3,2},{4,7},{5,4},{6,5},{7,6},{8,11},{9,8},{10,9... | collective-permute-start | bytes 1572872 | tf_op jit(solution)/shard_map/sum_near_other/ppermute | solution.py:363
  108.5 16.3 %collective-permute-start.26 = (bf16[256,1024]{1,0:T(8,128)(2,1)}, bf16[256,1024]{1,0:T(8,128)(2,1)S(1)}, u32[]{:S(2)}, u32[]{:S(2)}) collective-permute-start(bf16[256,1024]{1,0:T(8,128)(2,1)} %get-tuple-element.69), channel_id=1, source_target_pairs={{0,1},{1,2},{2,3},{3,0},{4,5},{5,6},{6,7},{7,4},{8,9},{9,10},{10,1... | collective-permute-start | bytes 1572872 | tf_op jit(solution)/shard_map/sum_far_other/ppermute | solution.py:363
  108.5 21.8 %collective-permute-start.32 = (bf16[272,1024]{1,0:T(8,128)(2,1)S(1)}, bf16[272,1024]{1,0:T(8,128)(2,1)S(1)}, u32[]{:S(2)}, u32[]{:S(2)}) collective-permute-start(bf16[272,1024]{1,0:T(8,128)(2,1)S(1)} %copy-done.21), channel_id=1, source_target_pairs={{0,3},{1,0},{2,1},{3,2},{4,7},{5,4},{6,5},{7,6},{8,11},{9,8},{10,9... | collective-permute-start | bytes 1671176 | tf_op jit(solution)/shard_map/sum_far/ppermute | solution.py:363
  111.9 12.8 %copy-start.27 = (bf16[256,1024]{1,0:T(8,128)(2,1)S(1)}, bf16[256,1024]{1,0:T(8,128)(2,1)}, u32[]{:S(2)}) copy-start(bf16[256,1024]{1,0:T(8,128)(2,1)} %get-tuple-element.70) | copy-start | bytes 1572868
  111.9 12.8 %copy-start.18 = (bf16[256,1024]{1,0:T(8,128)(2,1)S(1)}, bf16[256,1024]{1,0:T(8,128)(2,1)}, u32[]{:S(2)}) copy-start(bf16[256,1024]{1,0:T(8,128)(2,1)} %get-tuple-element.71) | copy-start | bytes 1572868
  111.9 20.1 %collective-permute-start.33 = (bf16[272,1024]{1,0:T(8,128)(2,1)S(1)}, bf16[272,1024]{1,0:T(8,128)(2,1)S(1)}, u32[]{:S(2)}, u32[]{:S(2)}) collective-permute-start(bf16[272,1024]{1,0:T(8,128)(2,1)S(1)} %add_convert_fusion.1), channel_id=1, source_target_pairs={{0,4},{1,5},{2,6},{3,7},{4,0},{5,1},{6,2},{7,3},{8,12},{9,13},{10,... | collective-permute-start | bytes 1671176 | tf_op jit(solution)/shard_map/sum_cross_side/ppermute | solution.py:363
  113.0 34.6 %collective-permute-start.30 = (bf16[272,1024]{1,0:T(8,128)(2,1)}, bf16[272,1024]{1,0:T(8,128)(2,1)S(1)}, u32[]{:S(2)}, u32[]{:S(2)}) collective-permute-start(bf16[272,1024]{1,0:T(8,128)(2,1)} %get-tuple-element.73), channel_id=1, source_target_pairs={{0,1},{1,2},{2,3},{3,0},{4,5},{5,6},{6,7},{7,4},{8,9},{9,10},{10,1... | collective-permute-start | bytes 1671176 | tf_op jit(solution)/shard_map/sum_near/ppermute | solution.py:363
  113.2 12.8 %copy-start.17 = (bf16[256,1024]{1,0:T(8,128)(2,1)S(1)}, bf16[256,1024]{1,0:T(8,128)(2,1)}, u32[]{:S(2)}) copy-start(bf16[256,1024]{1,0:T(8,128)(2,1)} %get-tuple-element.66) | copy-start | bytes 1572868
  124.7 20.2 %collective-permute-start.27 = (bf16[256,1024]{1,0:T(8,128)(2,1)S(1)}, bf16[256,1024]{1,0:T(8,128)(2,1)S(1)}, u32[]{:S(2)}, u32[]{:S(2)}) collective-permute-start(bf16[256,1024]{1,0:T(8,128)(2,1)S(1)} %copy-done.27), channel_id=1, source_target_pairs={{0,1},{1,2},{2,3},{3,0},{4,5},{5,6},{6,7},{7,4},{8,9},{9,10},{10,1... | collective-permute-start | bytes 1572872 | tf_op jit(solution)/shard_map/sum_far/ppermute | solution.py:363
  125.0 9.9 %copy-start.14 = (bf16[272,1024]{1,0:T(8,128)(2,1)S(1)}, bf16[272,1024]{1,0:T(8,128)(2,1)}, u32[]{:S(2)}) copy-start(bf16[272,1024]{1,0:T(8,128)(2,1)} %get-tuple-element.75) | copy-start | bytes 1671172
  125.0 20.8 %collective-permute-start.28 = (bf16[256,1024]{1,0:T(8,128)(2,1)S(1)}, bf16[256,1024]{1,0:T(8,128)(2,1)S(1)}, u32[]{:S(2)}, u32[]{:S(2)}) collective-permute-start(bf16[256,1024]{1,0:T(8,128)(2,1)S(1)} %add_convert_fusion.4), channel_id=1, source_target_pairs={{0,4},{1,5},{2,6},{3,7},{4,0},{5,1},{6,2},{7,3},{8,12},{9,13},{10,... | collective-permute-start | bytes 1572872 | tf_op jit(solution)/shard_map/sum_cross_side/ppermute | solution.py:363
  130.3 19.2 %collective-permute-start.31 = (bf16[272,1024]{1,0:T(8,128)(2,1)S(1)}, bf16[272,1024]{1,0:T(8,128)(2,1)S(1)}, u32[]{:S(2)}, u32[]{:S(2)}) collective-permute-start(bf16[272,1024]{1,0:T(8,128)(2,1)S(1)} %add_convert_fusion.2), channel_id=1, source_target_pairs={{0,4},{1,5},{2,6},{3,7},{4,0},{5,1},{6,2},{7,3},{8,12},{9,13},{10,... | collective-permute-start | bytes 1671176 | tf_op jit(solution)/shard_map/sum_cross/ppermute | solution.py:363
  132.1 29.4 %collective-permute-start.24 = (bf16[256,1024]{1,0:T(8,128)(2,1)}, bf16[256,1024]{1,0:T(8,128)(2,1)}, u32[]{:S(2)}, u32[]{:S(2)}) collective-permute-start(bf16[256,1024]{1,0:T(8,128)(2,1)} %get-tuple-element.65), channel_id=1, source_target_pairs={{0,3},{1,0},{2,1},{3,2},{4,7},{5,4},{6,5},{7,6},{8,11},{9,8},{10,9... | collective-permute-start | bytes 1572872 | tf_op jit(solution)/shard_map/sum_near/ppermute | solution.py:363
  134.9 11.6 %copy-start.19 = (bf16[256,1024]{1,0:T(8,128)(2,1)S(1)}, bf16[256,1024]{1,0:T(8,128)(2,1)}, u32[]{:S(2)}) copy-start(bf16[256,1024]{1,0:T(8,128)(2,1)} %get-tuple-element.67) | copy-start | bytes 1572868
  135.2 21.9 %copy-start.5 = (bf16[1,256,2048]{2,1,0:T(8,128)(2,1)S(1)}, bf16[1,256,2048]{2,1,0:T(8,128)(2,1)}, u32[]{:S(2)}) copy-start(bf16[1,256,2048]{2,1,0:T(8,128)(2,1)} %param.12) | copy-start | bytes 3145732
  135.2 21.9 %copy-start.7 = (bf16[272,1024]{1,0:T(8,128)(2,1)S(1)}, bf16[272,1024]{1,0:T(8,128)(2,1)}, u32[]{:S(2)}) copy-start(bf16[272,1024]{1,0:T(8,128)(2,1)} %get-tuple-element.52.refs_0_) | copy-start | bytes 1671172
  144.9 16.6 %collective-permute-start.25 = (bf16[256,1024]{1,0:T(8,128)(2,1)}, bf16[256,1024]{1,0:T(8,128)(2,1)}, u32[]{:S(2)}, u32[]{:S(2)}) collective-permute-start(bf16[256,1024]{1,0:T(8,128)(2,1)} %add_convert_fusion.5), channel_id=1, source_target_pairs={{0,4},{1,5},{2,6},{3,7},{4,0},{5,1},{6,2},{7,3},{8,12},{9,13},{10,... | collective-permute-start | bytes 1572872 | tf_op jit(solution)/shard_map/sum_cross/ppermute | solution.py:363
  145.8 11.3 %collective-permute-start.34 = (bf16[272,1024]{1,0:T(8,128)(2,1)S(1)}, bf16[272,1024]{1,0:T(8,128)(2,1)S(1)}, u32[]{:S(2)}, u32[]{:S(2)}) collective-permute-start(bf16[272,1024]{1,0:T(8,128)(2,1)S(1)} %add_convert_fusion), channel_id=1, source_target_pairs={{0,3},{1,0},{2,1},{3,2},{4,7},{5,4},{6,5},{7,6},{8,11},{9,8},{10,9... | collective-permute-start | bytes 1671176 | tf_op jit(solution)/shard_map/sum_side/ppermute | solution.py:363
  147.6 13.9 %collective-permute-start.29 = (bf16[256,1024]{1,0:T(8,128)(2,1)}, bf16[256,1024]{1,0:T(8,128)(2,1)}, u32[]{:S(2)}, u32[]{:S(2)}) collective-permute-start(bf16[256,1024]{1,0:T(8,128)(2,1)} %add_convert_fusion.3), channel_id=1, source_target_pairs={{0,1},{1,2},{2,3},{3,0},{4,5},{5,6},{6,7},{7,4},{8,9},{9,10},{10,1... | collective-permute-start | bytes 1572872 | tf_op jit(solution)/shard_map/sum_side/ppermute | solution.py:363
  159.3 2.3 %copy-start.2 = (bf16[32,4,128,128]{3,2,1,0:T(8,128)(2,1)S(1)}, bf16[32,4,128,128]{3,2,1,0:T(8,128)(2,1)}, u32[]{:S(2)}) copy-start(bf16[32,4,128,128]{3,2,1,0:T(8,128)(2,1)} %all-gather.3.cloned.1.call-done) | copy-start | bytes 12582916
  159.3 2.4 %copy-start.8 = (bf16[256,1024]{1,0:T(8,128)(2,1)S(1)}, bf16[256,1024]{1,0:T(8,128)(2,1)}, u32[]{:S(2)}) copy-start(bf16[256,1024]{1,0:T(8,128)(2,1)} %get-tuple-element.59.refs_0_) | copy-start | bytes 1572868
  (3 other events, 4.2 us)
Sparse Core Ops, SparseCore 0:
  53.7 30.0 reduce-scatter.1
  106.0 31.3 all-gather.2
